TPU v7x, 512 devices: a whole 4x8x8 slice. The times are simulated.
512 devices in a mesh: gz: 8 (over x, core), xy: 64 (over y, z).
Axes of the slice: x: 4, y: 8, z: 8, core: 2. Of those that a mesh axis runs over, the one named last changes fastest.
Arguments:
- tile_planes: float32 [8, 6144, 2048], P('gz', 'xy'), may hold values from 0.5 to 2
- plane_owner: int32 [8, 6144, 1], P('gz', 'xy'), may hold values from 0 to 63, as said below
- plane_slot: int32 [8, 6144], P('gz', 'xy'), may hold values from 0 to 95, as said below
- view_shift: int32 [6], replicated, may hold values from -16 to 16
- psf_z: float32 [6, 33], replicated, may hold values from 0.05 to 1
- psf_x: float32 [6, 33], replicated, may hold values from 0.05 to 1
- psf_y: float32 [6, 33], replicated, may hold values from 0.05 to 1
- background: float32 [6], replicated, may hold values from 0.1 to 0.5
- initial_estimate: float32 [128, 1024, 128], P('gz', 'xy'), may hold values from 0.5 to 2
Outputs:
- deconvolved: float32 [128, 1024, 128], P('gz', 'xy')
Inputs may be any that keep to these rules, and one draw needn't show every extreme that they name: `plane_owner`: among the 96 rows of one device no brick owner is named more than 3 times, and some owner exactly 3 times. Within one z-slab every brick owner is named by exactly 96 rows. `plane_slot`: within one z-slab, the rows that name one brick owner carry each slot of 0 to 95 exactly once.
All inputs are finite; a program needn't handle non-finite values.
Results may differ from a plain program's by a relative error of at most 0.0001.
Values sent between devices are 32-bit elements; how exact they have to be, the bound alone decides.
No kernel may reach another device: no remote copies, remote signals or barrier semaphores. Data moves between devices by JAX's collectives and lax.ppermute only.
A program may use at most 64 MiB of HBM per device.

v0:
```python
import jax
import jax.numpy as jnp
from jax import lax
from jax.experimental import pallas as pl
from jax.experimental.pallas import tpu as pltpu
from jax.sharding import PartitionSpec as P

ITERS = 2
VIEWS = 6
TAPS = 33
R = 16
BZ = 16
BX = 16
NY = 128
SEND = 3
SRC = 96
PEERS = 64
EX = BX + 2 * R
EZ = BZ + 2 * R
SLOTS = VIEWS * BZ
CHUNK = SEND * BX + 1
VU = VIEWS * BX
F32 = jnp.float32
BF16 = jnp.bfloat16

VMEM = pl.BlockSpec(memory_space=pltpu.VMEM)
SMEM = pl.BlockSpec(memory_space=pltpu.SMEM)


def params(mib):
    return pltpu.CompilerParams(vmem_limit_bytes=mib * 1024 * 1024)


def shape(dims, dtype=F32):
    return jax.ShapeDtypeStruct(dims, dtype)


def split(value):
    high = value.astype(BF16)
    return high, (value - high.astype(F32)).astype(BF16)


def pack_kernel(owner, slot, planes, send, rows, count, named):
    for group in range(SRC // 8):
        for column in range(BX):
            rows[pl.ds(group * 8 * BX + column, 8, stride=BX), :] = planes[
                group * 8 : group * 8 + 8, column * NY : (column + 1) * NY
            ]

    def clear(peer, carry):
        count[peer] = 0
        for rank in range(SEND):
            named[peer * SEND + rank] = SLOTS
        return carry

    lax.fori_loop(0, PEERS, clear, 0)

    def place(plane, carry):
        peer = owner[plane]
        rank = count[peer]
        count[peer] = rank + 1
        named[peer * SEND + rank] = slot[plane]
        start = peer * CHUNK + rank * BX
        send[pl.ds(start, BX), :] = rows[pl.ds(pl.multiple_of(plane * BX, BX), BX), :]
        return carry

    lax.fori_loop(0, SRC, place, 0)
    lane = lax.broadcasted_iota(jnp.int32, (1, NY), 1)

    def tell(peer, carry):
        row = jnp.full((1, NY), named[peer * SEND], jnp.int32)
        for rank in range(1, SEND):
            row = jnp.where(lane == rank, named[peer * SEND + rank], row)
        send[pl.ds(peer * CHUNK + SEND * BX, 1), :] = row.astype(F32)
        return carry

    lax.fori_loop(0, PEERS, tell, 0)


def pack(owner, slot, planes):
    return pl.pallas_call(
        pack_kernel,
        out_shape=shape((PEERS * CHUNK, NY)),
        in_specs=[SMEM, SMEM, VMEM],
        out_specs=VMEM,
        scratch_shapes=[
            pltpu.VMEM((SRC * BX, NY), F32),
            pltpu.SMEM((PEERS,), jnp.int32),
            pltpu.SMEM((PEERS * SEND,), jnp.int32),
        ],
        compiler_params=params(16),
        name="pack_planes",
    )(owner, slot, planes)


def weight_kernel(taps, shift, x_fwd, x_back, y_fwd, y_back):
    row = lax.broadcasted_iota(jnp.int32, (BX, NY), 0)
    lane = lax.broadcasted_iota(jnp.int32, (BX, NY), 1)
    bands = []
    for view in range(VIEWS):
        band = jnp.zeros((BX, NY), F32)
        for tap in range(TAPS):
            band = jnp.where(lane - row == tap, taps[VIEWS + view, tap], band)
        bands.append(band)
    band = jnp.concatenate(bands + [jnp.zeros((NY - VU, NY), F32)], axis=0)
    high, low = split(band[:VU, :EX])
    x_fwd[...] = jnp.concatenate([high, low, high], axis=1)
    high, low = split(jnp.transpose(band)[:EX, :VU])
    x_back[...] = jnp.concatenate([high, low, high], axis=1)
    row = lax.broadcasted_iota(jnp.int32, (NY, NY), 0)
    lane = lax.broadcasted_iota(jnp.int32, (NY, NY), 1)

    def along_y(view, carry):
        offset = lane - row + R + shift[view]
        back = jnp.zeros((NY, NY), F32)
        for tap in range(TAPS):
            back = jnp.where(offset == tap, taps[2 * VIEWS + view, tap], back)
        high, low = split(back)
        y_back[view] = jnp.concatenate([high, low, high], axis=0)
        high, low = split(jnp.transpose(back))
        y_fwd[view] = jnp.concatenate([high, low, high], axis=0)
        return carry

    lax.fori_loop(0, VIEWS, along_y, 0)


def weights(taps, shift):
    return pl.pallas_call(
        weight_kernel,
        out_shape=[
            shape((VU, 3 * EX), BF16),
            shape((EX, 3 * VU), BF16),
            shape((VIEWS, 3 * NY, NY), BF16),
            shape((VIEWS, 3 * NY, NY), BF16),
        ],
        in_specs=[SMEM, SMEM],
        out_specs=[VMEM] * 4,
        compiler_params=params(16),
        name="operator_matrices",
    )(taps, shift)


def dot(left, right):
    return jnp.dot(left, right, preferred_element_type=F32)


def along_x_fwd(x_fwd, pieces, starts, wide):
    matrix = x_fwd[...]
    for piece, start in zip(pieces, starts):

        def one(plane, carry):
            high, low = split(piece[plane])
            wide[start + plane] = dot(matrix, jnp.concatenate([high, high, low], axis=0))
            return carry

        lax.fori_loop(0, BZ, one, 0, unroll=4)


def along_z_fwd(taps, wide, narrow):
    def one(index, carry):
        view = index // 2
        rows = pl.ds(pl.multiple_of(index * 8, 8), 8)
        window = [wide[plane, rows, :] for plane in range(BZ)]
        sums = [None] * BZ
        for tap in range(TAPS):
            if tap:
                window = window[1:] + [wide[tap + BZ - 1, rows, :]]
            weight = jnp.full((8, NY), taps[view, tap], F32)
            for plane in range(BZ):
                term = weight * window[plane]
                sums[plane] = term if tap == 0 else sums[plane] + term
        base = view * BZ * BX + (index % 2) * 8
        for plane in range(BZ):
            narrow[pl.ds(pl.multiple_of(base + plane * BX, 8), 8), :] = sums[plane]
        return carry

    lax.fori_loop(0, 2 * VIEWS, one, 0)


def rows_of(view):
    return pl.ds(pl.multiple_of(view * BZ * BX, BZ * BX), BZ * BX)


def along_y(matrix, value):
    high, low = split(value)
    return dot(jnp.concatenate([high, high, low], axis=1), matrix)


def placed(core):
    inside = jnp.where(core == 0, 2 * R, 0)
    outside = jnp.where(core == 0, 0, 2 * R)
    return [R, inside, outside]


def forward_kernel(core, taps, background, x_fwd, y_fwd, own, inside, outside, blur, wide, narrow):
    along_x_fwd(x_fwd, [own, inside, outside], placed(core[0]), wide)
    along_z_fwd(taps, wide, narrow)

    def one(view, carry):
        blur[rows_of(view), :] = along_y(y_fwd[view], narrow[rows_of(view), :]) + background[view]
        return carry

    lax.fori_loop(0, VIEWS, one, 0)


def forward(core, taps, background, x_fwd, y_fwd, own, inside, outside):
    return pl.pallas_call(
        forward_kernel,
        out_shape=shape((SLOTS * BX, NY)),
        in_specs=[SMEM] * 3 + [VMEM] * 5,
        out_specs=VMEM,
        scratch_shapes=[
            pltpu.VMEM((EZ, VU, NY), F32),
            pltpu.VMEM((SLOTS * BX, NY), F32),
        ],
        compiler_params=params(24),
        name="forward",
    )(core, taps, background, x_fwd, y_fwd, own, inside, outside)


def along_z_back(taps, narrow, wide):
    def one(index, carry):
        view = index // 2
        rows = pl.ds(pl.multiple_of(index * 8, 8), 8)
        base = view * BZ * BX + (index % 2) * 8
        planes = [
            narrow[pl.ds(pl.multiple_of(base + plane * BX, 8), 8), :] for plane in range(BZ)
        ]
        sums = [None] * BZ
        for tap in range(TAPS):
            weight = jnp.full((8, NY), taps[view, tap], F32)
            for plane in range(BZ):
                term = weight * planes[plane]
                sums[plane] = term if sums[plane] is None else sums[plane] + term
            wide[tap, rows, :] = sums[0]
            sums = sums[1:] + [None]
        for plane in range(BZ - 1):
            wide[TAPS + plane, rows, :] = sums[plane]
        return carry

    lax.fori_loop(0, 2 * VIEWS, one, 0)


def along_x_back(x_back, wide, pieces, starts):
    matrix = x_back[...]
    for piece, start in zip(pieces, starts):

        def one(plane, carry):
            high, low = split(wide[start + plane])
            piece[plane] = dot(matrix, jnp.concatenate([high, high, low], axis=0))
            return carry

        lax.fori_loop(0, BZ, one, 0, unroll=4)


def back_steps(core, taps, x_back, y_back, data, blur, own, inside, outside, wide, narrow):
    def one(view, carry):
        ratio = data[rows_of(view), :] / blur[rows_of(view), :]
        narrow[rows_of(view), :] = along_y(y_back[view], ratio)
        return carry

    lax.fori_loop(0, VIEWS, one, 0)
    along_z_back(taps, narrow, wide)
    along_x_back(x_back, wide, [own, inside, outside], placed(core[0]))


def first_back_kernel(
    core, taps, x_back, y_back, got, blur, data, own, inside, outside, wide, narrow, names, slots, sem
):
    names[...] = got[pl.ds(SEND * BX, PEERS, stride=CHUNK), :].astype(jnp.int32)
    copy = pltpu.make_async_copy(names, slots, sem)
    copy.start()
    copy.wait()

    def unpack(peer, carry):
        for rank in range(SEND):
            slot = slots[peer, rank]
            data[pl.ds(pl.multiple_of(slot * BX, BX), BX), :] = got[
                pl.ds(peer * CHUNK + rank * BX, BX), :
            ]
        return carry

    lax.fori_loop(0, PEERS, unpack, 0)
    back_steps(core, taps, x_back, y_back, data, blur, own, inside, outside, wide, narrow)


def first_back(core, taps, x_back, y_back, got, blur):
    return pl.pallas_call(
        first_back_kernel,
        out_shape=[shape(((SLOTS + 1) * BX, NY))] + [shape((BZ, EX, NY))] * 3,
        in_specs=[SMEM] * 2 + [VMEM] * 4,
        out_specs=[VMEM] * 4,
        scratch_shapes=[
            pltpu.VMEM((EZ, VU, NY), F32),
            pltpu.VMEM((SLOTS * BX, NY), F32),
            pltpu.VMEM((PEERS, NY), jnp.int32),
            pltpu.SMEM((PEERS, NY), jnp.int32),
            pltpu.SemaphoreType.DMA,
        ],
        compiler_params=params(24),
        name="first_back",
    )(core, taps, x_back, y_back, got, blur)


def later_kernel(
    core, taps, background, x_fwd, y_fwd, x_back, y_back, e_own, e_inside, e_outside, data,
    own, inside, outside, wide, narrow, blur,
):
    forward_kernel(
        core, taps, background, x_fwd, y_fwd, e_own, e_inside, e_outside, blur, wide, narrow
    )
    back_steps(core, taps, x_back, y_back, data, blur, own, inside, outside, wide, narrow)


def later(core, taps, background, x_fwd, y_fwd, x_back, y_back, e_own, e_inside, e_outside, data):
    return pl.pallas_call(
        later_kernel,
        out_shape=[shape((BZ, EX, NY))] * 3,
        in_specs=[SMEM] * 3 + [VMEM] * 8,
        out_specs=[VMEM] * 3,
        scratch_shapes=[
            pltpu.VMEM((EZ, VU, NY), F32),
            pltpu.VMEM((SLOTS * BX, NY), F32),
            pltpu.VMEM((SLOTS * BX, NY), F32),
        ],
        compiler_params=params(24),
        name="forward_and_back",
    )(core, taps, background, x_fwd, y_fwd, x_back, y_back, e_own, e_inside, e_outside, data)


def swaps(first, count):
    pairs = [(i, i + 1) for i in range(first, count - 1, 2)]
    return pairs + [(j, i) for i, j in pairs]


def gathered(block, odd):
    even_pair = lax.ppermute(block, "xy", swaps(0, PEERS))
    odd_pair = lax.ppermute(block, "xy", swaps(1, PEERS))
    left = jnp.where(odd, even_pair, odd_pair)
    right = jnp.where(odd, odd_pair, even_pair)
    own = jnp.concatenate([left, block, right], axis=1)
    count = lax.axis_size("gz")
    return own, lax.ppermute(own, "gz", swaps(0, count)), lax.ppermute(own, "gz", swaps(1, count))


def scattered(own, inside, outside, odd):
    count = lax.axis_size("gz")
    total = (
        own
        + lax.ppermute(inside, "gz", swaps(0, count))
        + lax.ppermute(outside, "gz", swaps(1, count))
    )
    left, right = total[:, :R], total[:, R + BX :]
    even_pair = lax.ppermute(jnp.where(odd, left, right), "xy", swaps(0, PEERS))
    odd_pair = lax.ppermute(jnp.where(odd, right, left), "xy", swaps(1, PEERS))
    return total[:, R : R + BX] + even_pair + odd_pair


def local(
    tile_planes,
    plane_owner,
    plane_slot,
    view_shift,
    psf_z,
    psf_x,
    psf_y,
    background,
    initial_estimate,
):
    core = lax.rem(lax.axis_index("gz"), 2).astype(jnp.int32).reshape(1)
    odd = lax.rem(lax.axis_index("xy"), 2) == 1
    send = pack(plane_owner.reshape(SRC), plane_slot.reshape(SRC), tile_planes[0])
    got = lax.all_to_all(
        send.reshape(PEERS, 1, CHUNK * NY), "xy", split_axis=0, concat_axis=0, tiled=True
    ).reshape(PEERS * CHUNK, NY)
    psf = jnp.concatenate([psf_z, psf_x, psf_y], axis=0)
    taps = psf / jnp.sum(psf, axis=1, keepdims=True)
    x_fwd, x_back, y_fwd, y_back = weights(taps, view_shift)
    estimate = initial_estimate
    for step in range(ITERS):
        pieces = gathered(estimate, odd)
        if step == 0:
            blur = forward(core, taps, background, x_fwd, y_fwd, *pieces)
            data, *parts = first_back(core, taps, x_back, y_back, got, blur)
        else:
            parts = later(
                core, taps, background, x_fwd, y_fwd, x_back, y_back, *pieces, data
            )
        estimate = estimate * (scattered(*parts, odd) / VIEWS)
    return estimate


def solution(mesh):
    return jax.shard_map(
        local,
        mesh=mesh,
        in_specs=(
            P("gz", "xy", None),
            P("gz", "xy", None),
            P("gz", "xy"),
            P(),
            P(),
            P(),
            P(),
            P(),
            P("gz", "xy", None),
        ),
        out_specs=P("gz", "xy", None),
        check_vma=False,
    )
```

profile of v0, /device:TPU:36, one launch (start us, length us, event | category | flops | bytes accessed | tf_op | source)
XLA Modules:
  0.0 172.6 jit_solution(17008965359551917622)
XLA Ops:
  0.0 1.1 copy-done.2
  1.1 0.7 copy-done.8
  1.8 0.7 copy-done.9
  2.4 4.0 %pack_planes.1 = f32[3136,128]{1,0:T(8,128)} custom-call(s32[96]{0:T(128)S(1)} %bitcast.8, s32[96]{0:T(128)S(1)} %bitcast.9, f32[96,2048]{1,0:T(8,128)S(1)} %bitcast.7), custom_call_target="tpu_custom_call" | custom-call | tf_op jit(solution)/shard_map/pack_planes/pallas_call | solution.py:81
  6.4 0.0 copy-start.10
  6.4 0.0 copy-start.7
  6.4 16.5 %all-to-all-start = ((f32[64,1,6272]{2,1,0:T(1,128)}), f32[64,1,6272]{2,1,0:T(1,128)S(1)}, u32[]{:S(2)}, u32[]{:S(2)}) async-start(f32[64,1,6272]{2,1,0:T(1,128)} %bitcast.4), calls=%async_computation | async-start | bytes 3211264 | tf_op jit(solution)/shard_map/all_to_all | solution.py:373
  22.9 0.0 copy-done.11
  22.9 4.6 %collective-permute-start.1 = (f32[16,16,128]{2,1,0:T(8,128)S(1)}, f32[16,16,128]{2,1,0:T(8,128)S(1)}, u32[]{:S(2)}, u32[]{:S(2)}) collective-permute-start(f32[16,16,128]{2,1,0:T(8,128)S(1)} %copy-done.11), channel_id=1, source_target_pairs={{1,2},{3,4},{5,6},{7,8},{9,10},{11,12},{13,14},{15,16},{17,18},{19... | collective-permute-start | bytes 393224 | tf_op jit(solution)/shard_map/ppermute | solution.py:338
  27.5 2.2 %collective-permute-start = (f32[16,16,128]{2,1,0:T(8,128)S(1)}, f32[16,16,128]{2,1,0:T(8,128)S(1)}, u32[]{:S(2)}, u32[]{:S(2)}) collective-permute-start(f32[16,16,128]{2,1,0:T(8,128)S(1)} %copy-done.11), channel_id=1, source_target_pairs={{0,1},{2,3},{4,5},{6,7},{8,9},{10,11},{12,13},{14,15},{16,17},{18,... | collective-permute-start | bytes 393224 | tf_op jit(solution)/shard_map/ppermute | solution.py:337
  29.7 33.8 %collective-permute-done.1 = f32[16,16,128]{2,1,0:T(8,128)S(1)} collective-permute-done((f32[16,16,128]{2,1,0:T(8,128)S(1)}, f32[16,16,128]{2,1,0:T(8,128)S(1)}, u32[]{:S(2)}, u32[]{:S(2)}) %collective-permute-start.1) | collective-permute-done | bytes 131104 | tf_op jit(solution)/shard_map/ppermute | solution.py:338
  63.5 0.0 collective-permute-done
  63.6 1.9 %collective-permute-start.3 = (f32[16,48,128]{2,1,0:T(8,128)S(1)}, f32[16,48,128]{2,1,0:T(8,128)S(1)}, u32[]{:S(2)}, u32[]{:S(2)}) collective-permute-start(f32[16,48,128]{2,1,0:T(8,128)S(1)} %pad_maximum_fusion.own), channel_id=1, source_target_pairs={{64,128},{192,256},{320,384},{128,64},{256,192},{384,320},{65,129}... | collective-permute-start | bytes 1179656 | tf_op jit(solution)/shard_map/ppermute | solution.py:343
  65.5 3.2 %collective-permute-start.2 = (f32[16,48,128]{2,1,0:T(8,128)S(1)}, f32[16,48,128]{2,1,0:T(8,128)S(1)}, u32[]{:S(2)}, u32[]{:S(2)}) collective-permute-start(f32[16,48,128]{2,1,0:T(8,128)S(1)} %pad_maximum_fusion.own), channel_id=1, source_target_pairs={{0,64},{128,192},{256,320},{384,448},{64,0},{192,128},{320,256},{4... | collective-permute-start | bytes 1179656 | tf_op jit(solution)/shard_map/ppermute | solution.py:343
  68.8 0.0 copy-done.13
  68.8 0.0 copy-done.14
  68.8 0.0 copy-done.15
  68.8 0.1 fusion.7
  68.9 0.1 fusion.6.taps
  69.0 0.0 copy-done.10
  69.0 2.4 %operator_matrices.1 = (bf16[96,144]{1,0:T(8,128)(2,1)S(1)}, bf16[48,288]{1,0:T(8,128)(2,1)S(1)}, bf16[6,384,128]{2,1,0:T(8,128)(2,1)S(1)}, bf16[6,384,128]{2,1,0:T(8,128)(2,1)S(1)}) custom-call(f32[18,33]{1,0:T(8,128)S(1)} %fusion.6.taps, s32[6]{0:T(128)S(1)} %copy-done.10), custom_call_target="tpu_custom_call" | custom-call | tf_op jit(solution)/shard_map/operator_matrices/pallas_call | solution.py:128
  71.4 1.3 collective-permute-done.3.outside
  72.7 0.7 copy-done.3
  73.5 0.0 collective-permute-done.2.inside
  73.5 0.8 copy-done.5
  74.2 0.0 copy-done.7
  74.2 1.0 copy-done.4
  75.2 1.0 copy-done.6
  76.2 6.4 %forward.1.blur = f32[1536,128]{1,0:T(8,128)S(1)} custom-call(s32[1]{0:T(128)} %bitcast.core, f32[18,33]{1,0:T(8,128)S(1)} %fusion.6.taps, f32[6]{0:T(128)S(1)} %copy-done.7, bf16[96,144]{1,0:T(8,128)(2,1)S(1)} %get-tuple-element.18.x_fwd, bf16[6,384,128]{2,1,0:T(8,128)(2,1)S(1)} %get-tuple-element.19.y_fwd, f32[16,48,128]{2,1,0:T(8,128)S(1)} %pad_maximum_fusion.own, ...), custom_call_target="tpu_custom_call" | custom-call | tf_op jit(solution)/shard_map/forward/pallas_call | solution.py:207
  82.7 0.0 copy-start
  82.7 0.8 copy-done
  83.5 0.0 all-to-all-done
  83.5 7.7 %first_back.1 = (f32[1552,128]{1,0:T(8,128)S(1)}, f32[16,48,128]{2,1,0:T(8,128)S(1)}, f32[16,48,128]{2,1,0:T(8,128)S(1)}, f32[16,48,128]{2,1,0:T(8,128)S(1)}) custom-call(s32[1]{0:T(128)} %bitcast.core, f32[18,33]{1,0:T(8,128)S(1)} %fusion.6.taps, bf16[48,288]{1,0:T(8,128)(2,1)S(1)} %get-tuple-element.16.x_back, ...), custom_call_target="tpu_custom_call" | custom-call | tf_op jit(solution)/shard_map/first_back/pallas_call | solution.py:288
  91.2 0.0 copy-start.12
  91.2 2.1 %collective-permute-start.4 = (f32[16,48,128]{2,1,0:T(8,128)S(1)}, f32[16,48,128]{2,1,0:T(8,128)S(1)}, u32[]{:S(2)}, u32[]{:S(2)}) collective-permute-start(f32[16,48,128]{2,1,0:T(8,128)S(1)} %get-tuple-element.21), channel_id=1, source_target_pairs={{0,64},{128,192},{256,320},{384,448},{64,0},{192,128},{320,256},{4... | collective-permute-start | bytes 1179656 | tf_op jit(solution)/shard_map/ppermute | solution.py:350
  93.3 2.5 %collective-permute-start.5 = (f32[16,48,128]{2,1,0:T(8,128)S(1)}, f32[16,48,128]{2,1,0:T(8,128)S(1)}, u32[]{:S(2)}, u32[]{:S(2)}) collective-permute-start(f32[16,48,128]{2,1,0:T(8,128)S(1)} %get-tuple-element.22), channel_id=1, source_target_pairs={{64,128},{192,256},{320,384},{128,64},{256,192},{384,320},{65,129}... | collective-permute-start | bytes 1179656 | tf_op jit(solution)/shard_map/ppermute | solution.py:351
  95.8 0.0 collective-permute-done.4
  95.8 6.5 %collective-permute-done.5 = f32[16,48,128]{2,1,0:T(8,128)S(1)} collective-permute-done((f32[16,48,128]{2,1,0:T(8,128)S(1)}, f32[16,48,128]{2,1,0:T(8,128)S(1)}, u32[]{:S(2)}, u32[]{:S(2)}) %collective-permute-start.5) | collective-permute-done | bytes 393248 | tf_op jit(solution)/shard_map/ppermute | solution.py:351
  102.4 0.1 add_add_fusion.1
  102.5 0.0 copy-start.1
  102.5 3.2 %collective-permute-start.6 = (f32[16,16,128]{2,1,0:T(8,128)S(1)}, f32[16,16,128]{2,1,0:T(8,128)S(1)}, u32[]{:S(2)}, u32[]{:S(2)}) collective-permute-start(f32[16,16,128]{2,1,0:T(8,128)S(1)} %get-tuple-element.29), channel_id=1, source_target_pairs={{0,1},{2,3},{4,5},{6,7},{8,9},{10,11},{12,13},{14,15},{16,17},{18,... | collective-permute-start | bytes 393224 | tf_op jit(solution)/shard_map/ppermute | solution.py:354
  105.7 3.0 %collective-permute-start.7 = (f32[16,16,128]{2,1,0:T(8,128)S(1)}, f32[16,16,128]{2,1,0:T(8,128)S(1)}, u32[]{:S(2)}, u32[]{:S(2)}) collective-permute-start(f32[16,16,128]{2,1,0:T(8,128)S(1)} %get-tuple-element.30), channel_id=1, source_target_pairs={{1,2},{3,4},{5,6},{7,8},{9,10},{11,12},{13,14},{15,16},{17,18},{19... | collective-permute-start | bytes 393224 | tf_op jit(solution)/shard_map/ppermute | solution.py:355
  108.6 1.8 %collective-permute-done.6 = f32[16,16,128]{2,1,0:T(8,128)S(1)} collective-permute-done((f32[16,16,128]{2,1,0:T(8,128)S(1)}, f32[16,16,128]{2,1,0:T(8,128)S(1)}, u32[]{:S(2)}, u32[]{:S(2)}) %collective-permute-start.6) | collective-permute-done | bytes 131104 | tf_op jit(solution)/shard_map/ppermute | solution.py:354
  110.4 6.1 %collective-permute-done.7 = f32[16,16,128]{2,1,0:T(8,128)S(1)} collective-permute-done((f32[16,16,128]{2,1,0:T(8,128)S(1)}, f32[16,16,128]{2,1,0:T(8,128)S(1)}, u32[]{:S(2)}, u32[]{:S(2)}) %collective-permute-start.7) | collective-permute-done | bytes 131104 | tf_op jit(solution)/shard_map/ppermute | solution.py:355
  116.5 0.0 copy-done.12
  116.5 3.2 %collective-permute-start.9 = (f32[16,16,128]{2,1,0:T(8,128)S(1)}, f32[16,16,128]{2,1,0:T(8,128)S(1)}, u32[]{:S(2)}, u32[]{:S(2)}) collective-permute-start(f32[16,16,128]{2,1,0:T(8,128)S(1)} %fusion.5), channel_id=1, source_target_pairs={{1,2},{3,4},{5,6},{7,8},{9,10},{11,12},{13,14},{15,16},{17,18},{19... | collective-permute-start | bytes 393224 | tf_op jit(solution)/shard_map/ppermute | solution.py:338
  119.8 1.9 %collective-permute-start.8 = (f32[16,16,128]{2,1,0:T(8,128)S(1)}, f32[16,16,128]{2,1,0:T(8,128)S(1)}, u32[]{:S(2)}, u32[]{:S(2)}) collective-permute-start(f32[16,16,128]{2,1,0:T(8,128)S(1)} %fusion.5), channel_id=1, source_target_pairs={{0,1},{2,3},{4,5},{6,7},{8,9},{10,11},{12,13},{14,15},{16,17},{18,... | collective-permute-start | bytes 393224 | tf_op jit(solution)/shard_map/ppermute | solution.py:337
  121.7 5.0 %collective-permute-done.9 = f32[16,16,128]{2,1,0:T(8,128)S(1)} collective-permute-done((f32[16,16,128]{2,1,0:T(8,128)S(1)}, f32[16,16,128]{2,1,0:T(8,128)S(1)}, u32[]{:S(2)}, u32[]{:S(2)}) %collective-permute-start.9) | collective-permute-done | bytes 131104 | tf_op jit(solution)/shard_map/ppermute | solution.py:338
  126.7 0.0 collective-permute-done.8
  126.8 1.9 %collective-permute-start.11 = (f32[16,48,128]{2,1,0:T(8,128)S(1)}, f32[16,48,128]{2,1,0:T(8,128)S(1)}, u32[]{:S(2)}, u32[]{:S(2)}) collective-permute-start(f32[16,48,128]{2,1,0:T(8,128)S(1)} %pad_maximum_fusion.1.e_own), channel_id=1, source_target_pairs={{64,128},{192,256},{320,384},{128,64},{256,192},{384,320},{65,129}... | collective-permute-start | bytes 1179656 | tf_op jit(solution)/shard_map/ppermute | solution.py:343
  128.7 3.5 %collective-permute-start.10 = (f32[16,48,128]{2,1,0:T(8,128)S(1)}, f32[16,48,128]{2,1,0:T(8,128)S(1)}, u32[]{:S(2)}, u32[]{:S(2)}) collective-permute-start(f32[16,48,128]{2,1,0:T(8,128)S(1)} %pad_maximum_fusion.1.e_own), channel_id=1, source_target_pairs={{0,64},{128,192},{256,320},{384,448},{64,0},{192,128},{320,256},{4... | collective-permute-start | bytes 1179656 | tf_op jit(solution)/shard_map/ppermute | solution.py:343
  132.2 3.7 %collective-permute-done.11.e_outside = f32[16,48,128]{2,1,0:T(8,128)S(1)} collective-permute-done((f32[16,48,128]{2,1,0:T(8,128)S(1)}, f32[16,48,128]{2,1,0:T(8,128)S(1)}, u32[]{:S(2)}, u32[]{:S(2)}) %collective-permute-start.11) | collective-permute-done | bytes 393248 | tf_op jit(solution)/shard_map/ppermute | solution.py:343
  135.9 0.0 collective-permute-done.10.e_inside
  135.9 11.8 %forward_and_back.1 = (f32[16,48,128]{2,1,0:T(8,128)S(1)}, f32[16,48,128]{2,1,0:T(8,128)S(1)}, f32[16,48,128]{2,1,0:T(8,128)S(1)}) custom-call(s32[1]{0:T(128)} %bitcast.core, f32[18,33]{1,0:T(8,128)S(1)} %fusion.6.taps, f32[6]{0:T(128)S(1)} %copy-done.7, bf16[96,144]{1,0:T(8,128)(2,1)S(1)} %get-tuple-element.18.x_fwd, bf16[6,384,128]{2,1,0:T(8,128)(2,1)S(1)} %copy-done.1, ...), custom_call_target="tpu_custom_call" | custom-call | tf_op jit(solution)/shard_map/forward_and_back/pallas_call | solution.py:316
  147.7 2.0 %collective-permute-start.12 = (f32[16,48,128]{2,1,0:T(8,128)S(1)}, f32[16,48,128]{2,1,0:T(8,128)S(1)}, u32[]{:S(2)}, u32[]{:S(2)}) collective-permute-start(f32[16,48,128]{2,1,0:T(8,128)S(1)} %get-tuple-element.25), channel_id=1, source_target_pairs={{0,64},{128,192},{256,320},{384,448},{64,0},{192,128},{320,256},{4... | collective-permute-start | bytes 1179656 | tf_op jit(solution)/shard_map/ppermute | solution.py:350
  149.8 2.4 %collective-permute-start.13 = (f32[16,48,128]{2,1,0:T(8,128)S(1)}, f32[16,48,128]{2,1,0:T(8,128)S(1)}, u32[]{:S(2)}, u32[]{:S(2)}) collective-permute-start(f32[16,48,128]{2,1,0:T(8,128)S(1)} %get-tuple-element.26), channel_id=1, source_target_pairs={{64,128},{192,256},{320,384},{128,64},{256,192},{384,320},{65,129}... | collective-permute-start | bytes 1179656 | tf_op jit(solution)/shard_map/ppermute | solution.py:351
  152.2 0.0 collective-permute-done.12
  152.2 6.6 %collective-permute-done.13 = f32[16,48,128]{2,1,0:T(8,128)S(1)} collective-permute-done((f32[16,48,128]{2,1,0:T(8,128)S(1)}, f32[16,48,128]{2,1,0:T(8,128)S(1)}, u32[]{:S(2)}, u32[]{:S(2)}) %collective-permute-start.13) | collective-permute-done | bytes 393248 | tf_op jit(solution)/shard_map/ppermute | solution.py:351
  158.9 0.1 add_add_fusion
  159.0 1.9 %collective-permute-start.14 = (f32[16,16,128]{2,1,0:T(8,128)S(1)}, f32[16,16,128]{2,1,0:T(8,128)S(1)}, u32[]{:S(2)}, u32[]{:S(2)}) collective-permute-start(f32[16,16,128]{2,1,0:T(8,128)S(1)} %get-tuple-element.27), channel_id=1, source_target_pairs={{0,1},{2,3},{4,5},{6,7},{8,9},{10,11},{12,13},{14,15},{16,17},{18,... | collective-permute-start | bytes 393224 | tf_op jit(solution)/shard_map/ppermute | solution.py:354
  160.9 5.8 %collective-permute-start.15 = (f32[16,16,128]{2,1,0:T(8,128)S(1)}, f32[16,16,128]{2,1,0:T(8,128)S(1)}, u32[]{:S(2)}, u32[]{:S(2)}) collective-permute-start(f32[16,16,128]{2,1,0:T(8,128)S(1)} %get-tuple-element.28), channel_id=1, source_target_pairs={{1,2},{3,4},{5,6},{7,8},{9,10},{11,12},{13,14},{15,16},{17,18},{19... | collective-permute-start | bytes 393224 | tf_op jit(solution)/shard_map/ppermute | solution.py:355
  166.7 0.0 collective-permute-done.14
  166.7 5.2 %collective-permute-done.15 = f32[16,16,128]{2,1,0:T(8,128)S(1)} collective-permute-done((f32[16,16,128]{2,1,0:T(8,128)S(1)}, f32[16,16,128]{2,1,0:T(8,128)S(1)}, u32[]{:S(2)}, u32[]{:S(2)}) %collective-permute-start.15) | collective-permute-done | bytes 131104 | tf_op jit(solution)/shard_map/ppermute | solution.py:355
  171.9 0.7 fusion.2
  (19 shorter events, 0.2 us)
Async XLA Ops:
  0.0 1.1 copy-start.2
  1.1 0.7 copy-start.8
  1.8 0.7 copy-start.9
  6.4 16.5 %copy-start.11 = (f32[16,16,128]{2,1,0:T(8,128)S(1)}, f32[16,16,128]{2,1,0:T(8,128)}, u32[]{:S(2)}) copy-start(f32[16,16,128]{2,1,0:T(8,128)} %param.17) | copy-start | bytes 393220
  6.4 62.4 %copy-start.13 = (f32[6,33]{1,0:T(8,128)S(1)}, f32[6,33]{1,0:T(8,128)}, u32[]{:S(2)}) copy-start(f32[6,33]{1,0:T(8,128)} %param.15) | copy-start | bytes 2380
  6.4 62.4 %copy-start.14 = (f32[6,33]{1,0:T(8,128)S(1)}, f32[6,33]{1,0:T(8,128)}, u32[]{:S(2)}) copy-start(f32[6,33]{1,0:T(8,128)} %param.14) | copy-start | bytes 2380
  6.4 62.4 %copy-start.15 = (f32[6,33]{1,0:T(8,128)S(1)}, f32[6,33]{1,0:T(8,128)}, u32[]{:S(2)}) copy-start(f32[6,33]{1,0:T(8,128)} %param.13) | copy-start | bytes 2380
  6.4 62.6 %copy-start.10 = (s32[6]{0:T(128)S(1)}, s32[6]{0:T(128)}, u32[]{:S(2)}) copy-start(s32[6]{0:T(128)} %shift.1) | copy-start | bytes 76
  6.4 67.8 %copy-start.7 = (f32[6]{0:T(128)S(1)}, f32[6]{0:T(128)}, u32[]{:S(2)}) copy-start(f32[6]{0:T(128)} %background.3) | copy-start | bytes 76
  6.4 77.0 %all-to-all-start = ((f32[64,1,6272]{2,1,0:T(1,128)}), f32[64,1,6272]{2,1,0:T(1,128)S(1)}, u32[]{:S(2)}, u32[]{:S(2)}) async-start(f32[64,1,6272]{2,1,0:T(1,128)} %bitcast.4), calls=%async_computation | async-start | bytes 3211264 | tf_op jit(solution)/shard_map/all_to_all | solution.py:373
  22.9 40.6 %collective-permute-start.1 = (f32[16,16,128]{2,1,0:T(8,128)S(1)}, f32[16,16,128]{2,1,0:T(8,128)S(1)}, u32[]{:S(2)}, u32[]{:S(2)}) collective-permute-start(f32[16,16,128]{2,1,0:T(8,128)S(1)} %copy-done.11), channel_id=1, source_target_pairs={{1,2},{3,4},{5,6},{7,8},{9,10},{11,12},{13,14},{15,16},{17,18},{19... | collective-permute-start | bytes 393224 | tf_op jit(solution)/shard_map/ppermute | solution.py:338
  27.5 36.0 %collective-permute-start = (f32[16,16,128]{2,1,0:T(8,128)S(1)}, f32[16,16,128]{2,1,0:T(8,128)S(1)}, u32[]{:S(2)}, u32[]{:S(2)}) collective-permute-start(f32[16,16,128]{2,1,0:T(8,128)S(1)} %copy-done.11), channel_id=1, source_target_pairs={{0,1},{2,3},{4,5},{6,7},{8,9},{10,11},{12,13},{14,15},{16,17},{18,... | collective-permute-start | bytes 393224 | tf_op jit(solution)/shard_map/ppermute | solution.py:337
  63.6 9.1 %collective-permute-start.3 = (f32[16,48,128]{2,1,0:T(8,128)S(1)}, f32[16,48,128]{2,1,0:T(8,128)S(1)}, u32[]{:S(2)}, u32[]{:S(2)}) collective-permute-start(f32[16,48,128]{2,1,0:T(8,128)S(1)} %pad_maximum_fusion.own), channel_id=1, source_target_pairs={{64,128},{192,256},{320,384},{128,64},{256,192},{384,320},{65,129}... | collective-permute-start | bytes 1179656 | tf_op jit(solution)/shard_map/ppermute | solution.py:343
  65.5 7.9 %collective-permute-start.2 = (f32[16,48,128]{2,1,0:T(8,128)S(1)}, f32[16,48,128]{2,1,0:T(8,128)S(1)}, u32[]{:S(2)}, u32[]{:S(2)}) collective-permute-start(f32[16,48,128]{2,1,0:T(8,128)S(1)} %pad_maximum_fusion.own), channel_id=1, source_target_pairs={{0,64},{128,192},{256,320},{384,448},{64,0},{192,128},{320,256},{4... | collective-permute-start | bytes 1179656 | tf_op jit(solution)/shard_map/ppermute | solution.py:343
  72.7 0.7 copy-start.3
  73.5 0.8 copy-start.5
  74.2 1.0 copy-start.4
  75.2 1.0 copy-start.6
  82.7 0.8 copy-start
  91.2 25.3 %copy-start.12 = (f32[16,16,128]{2,1,0:T(8,128)S(1)}, f32[16,16,128]{2,1,0:T(8,128)}, u32[]{:S(2)}) copy-start(f32[16,16,128]{2,1,0:T(8,128)} %param.17) | copy-start | bytes 393220
  91.2 4.6 %collective-permute-start.4 = (f32[16,48,128]{2,1,0:T(8,128)S(1)}, f32[16,48,128]{2,1,0:T(8,128)S(1)}, u32[]{:S(2)}, u32[]{:S(2)}) collective-permute-start(f32[16,48,128]{2,1,0:T(8,128)S(1)} %get-tuple-element.21), channel_id=1, source_target_pairs={{0,64},{128,192},{256,320},{384,448},{64,0},{192,128},{320,256},{4... | collective-permute-start | bytes 1179656 | tf_op jit(solution)/shard_map/ppermute | solution.py:350
  93.3 9.1 %collective-permute-start.5 = (f32[16,48,128]{2,1,0:T(8,128)S(1)}, f32[16,48,128]{2,1,0:T(8,128)S(1)}, u32[]{:S(2)}, u32[]{:S(2)}) collective-permute-start(f32[16,48,128]{2,1,0:T(8,128)S(1)} %get-tuple-element.22), channel_id=1, source_target_pairs={{64,128},{192,256},{320,384},{128,64},{256,192},{384,320},{65,129}... | collective-permute-start | bytes 1179656 | tf_op jit(solution)/shard_map/ppermute | solution.py:351
  102.5 33.4 %copy-start.1 = (bf16[6,384,128]{2,1,0:T(8,128)(2,1)S(1)}, bf16[6,384,128]{2,1,0:T(8,128)(2,1)}, u32[]{:S(2)}) copy-start(bf16[6,384,128]{2,1,0:T(8,128)(2,1)} %copy-done) | copy-start | bytes 1769476
  102.5 7.9 %collective-permute-start.6 = (f32[16,16,128]{2,1,0:T(8,128)S(1)}, f32[16,16,128]{2,1,0:T(8,128)S(1)}, u32[]{:S(2)}, u32[]{:S(2)}) collective-permute-start(f32[16,16,128]{2,1,0:T(8,128)S(1)} %get-tuple-element.29), channel_id=1, source_target_pairs={{0,1},{2,3},{4,5},{6,7},{8,9},{10,11},{12,13},{14,15},{16,17},{18,... | collective-permute-start | bytes 393224 | tf_op jit(solution)/shard_map/ppermute | solution.py:354
  105.7 10.8 %collective-permute-start.7 = (f32[16,16,128]{2,1,0:T(8,128)S(1)}, f32[16,16,128]{2,1,0:T(8,128)S(1)}, u32[]{:S(2)}, u32[]{:S(2)}) collective-permute-start(f32[16,16,128]{2,1,0:T(8,128)S(1)} %get-tuple-element.30), channel_id=1, source_target_pairs={{1,2},{3,4},{5,6},{7,8},{9,10},{11,12},{13,14},{15,16},{17,18},{19... | collective-permute-start | bytes 393224 | tf_op jit(solution)/shard_map/ppermute | solution.py:355
  116.5 10.2 %collective-permute-start.9 = (f32[16,16,128]{2,1,0:T(8,128)S(1)}, f32[16,16,128]{2,1,0:T(8,128)S(1)}, u32[]{:S(2)}, u32[]{:S(2)}) collective-permute-start(f32[16,16,128]{2,1,0:T(8,128)S(1)} %fusion.5), channel_id=1, source_target_pairs={{1,2},{3,4},{5,6},{7,8},{9,10},{11,12},{13,14},{15,16},{17,18},{19... | collective-permute-start | bytes 393224 | tf_op jit(solution)/shard_map/ppermute | solution.py:338
  119.8 6.9 %collective-permute-start.8 = (f32[16,16,128]{2,1,0:T(8,128)S(1)}, f32[16,16,128]{2,1,0:T(8,128)S(1)}, u32[]{:S(2)}, u32[]{:S(2)}) collective-permute-start(f32[16,16,128]{2,1,0:T(8,128)S(1)} %fusion.5), channel_id=1, source_target_pairs={{0,1},{2,3},{4,5},{6,7},{8,9},{10,11},{12,13},{14,15},{16,17},{18,... | collective-permute-start | bytes 393224 | tf_op jit(solution)/shard_map/ppermute | solution.py:337
  126.8 9.1 %collective-permute-start.11 = (f32[16,48,128]{2,1,0:T(8,128)S(1)}, f32[16,48,128]{2,1,0:T(8,128)S(1)}, u32[]{:S(2)}, u32[]{:S(2)}) collective-permute-start(f32[16,48,128]{2,1,0:T(8,128)S(1)} %pad_maximum_fusion.1.e_own), channel_id=1, source_target_pairs={{64,128},{192,256},{320,384},{128,64},{256,192},{384,320},{65,129}... | collective-permute-start | bytes 1179656 | tf_op jit(solution)/shard_map/ppermute | solution.py:343
  128.7 7.2 %collective-permute-start.10 = (f32[16,48,128]{2,1,0:T(8,128)S(1)}, f32[16,48,128]{2,1,0:T(8,128)S(1)}, u32[]{:S(2)}, u32[]{:S(2)}) collective-permute-start(f32[16,48,128]{2,1,0:T(8,128)S(1)} %pad_maximum_fusion.1.e_own), channel_id=1, source_target_pairs={{0,64},{128,192},{256,320},{384,448},{64,0},{192,128},{320,256},{4... | collective-permute-start | bytes 1179656 | tf_op jit(solution)/shard_map/ppermute | solution.py:343
  147.7 4.5 %collective-permute-start.12 = (f32[16,48,128]{2,1,0:T(8,128)S(1)}, f32[16,48,128]{2,1,0:T(8,128)S(1)}, u32[]{:S(2)}, u32[]{:S(2)}) collective-permute-start(f32[16,48,128]{2,1,0:T(8,128)S(1)} %get-tuple-element.25), channel_id=1, source_target_pairs={{0,64},{128,192},{256,320},{384,448},{64,0},{192,128},{320,256},{4... | collective-permute-start | bytes 1179656 | tf_op jit(solution)/shard_map/ppermute | solution.py:350
  149.8 9.1 %collective-permute-start.13 = (f32[16,48,128]{2,1,0:T(8,128)S(1)}, f32[16,48,128]{2,1,0:T(8,128)S(1)}, u32[]{:S(2)}, u32[]{:S(2)}) collective-permute-start(f32[16,48,128]{2,1,0:T(8,128)S(1)} %get-tuple-element.26), channel_id=1, source_target_pairs={{64,128},{192,256},{320,384},{128,64},{256,192},{384,320},{65,129}... | collective-permute-start | bytes 1179656 | tf_op jit(solution)/shard_map/ppermute | solution.py:351
  159.0 7.8 %collective-permute-start.14 = (f32[16,16,128]{2,1,0:T(8,128)S(1)}, f32[16,16,128]{2,1,0:T(8,128)S(1)}, u32[]{:S(2)}, u32[]{:S(2)}) collective-permute-start(f32[16,16,128]{2,1,0:T(8,128)S(1)} %get-tuple-element.27), channel_id=1, source_target_pairs={{0,1},{2,3},{4,5},{6,7},{8,9},{10,11},{12,13},{14,15},{16,17},{18,... | collective-permute-start | bytes 393224 | tf_op jit(solution)/shard_map/ppermute | solution.py:354
  160.9 11.0 %collective-permute-start.15 = (f32[16,16,128]{2,1,0:T(8,128)S(1)}, f32[16,16,128]{2,1,0:T(8,128)S(1)}, u32[]{:S(2)}, u32[]{:S(2)}) collective-permute-start(f32[16,16,128]{2,1,0:T(8,128)S(1)} %get-tuple-element.28), channel_id=1, source_target_pairs={{1,2},{3,4},{5,6},{7,8},{9,10},{11,12},{13,14},{15,16},{17,18},{19... | collective-permute-start | bytes 393224 | tf_op jit(solution)/shard_map/ppermute | solution.py:355
where the time goes:
time: 173 us
  waiting for transfers between devices  70 us (40%)
  starting transfers between devices  61.9 us (36%)
  Pallas kernels  32.4 us (19%)
  local copies, waits for them, and re-layouts  6.8 us (4%)
    ppermute x2, waiting for transfers between devices, gathered(): odd_pair = lax.ppermute(block, 'xy', swaps(1, PEERS))  38.8 us
    all_to_all x1, starting transfers between devices, local(): lax.all_to_all(send.reshape(PEERS, 1, CHUNK * NY), 'xy', split_axis=0, co...  16.5 us
    ppermute x2, waiting for transfers between devices, scattered(): lax.ppermute(outside, 'gz', swaps(1, count))  13.2 us
    pallas_call x1, Pallas kernels, later(): pl.pallas_call(later_kernel, out_shape=[shape((BZ, EX, NY))] * 3, in_spec...  11.8 us
    ppermute x2, waiting for transfers between devices, scattered(): odd_pair = lax.ppermute(jnp.where(odd, right, left), 'xy', swaps(1, PEERS))  11.3 us
    ppermute x2, starting transfers between devices, scattered(): odd_pair = lax.ppermute(jnp.where(odd, right, left), 'xy', swaps(1, PEERS))  8.81 us
    ppermute x2, starting transfers between devices, gathered(): odd_pair = lax.ppermute(block, 'xy', swaps(1, PEERS))  7.82 us
    pallas_call x1, Pallas kernels, first_back(): pl.pallas_call(first_back_kernel, out_shape=[shape(((SLOTS + 1) * BX, NY)...  7.72 us
  transfers between devices with their start and end apart: 17, of which 9 were waited for; matrix products, arithmetic and copies ran while one was open for 0% of the time, Pallas kernels for 5%

commit v1 on v0

v1 whole, which is shorter than its diff:
```python
import jax
import jax.numpy as jnp
from jax import lax
from jax.experimental import pallas as pl
from jax.experimental.pallas import tpu as pltpu
from jax.sharding import PartitionSpec as P

ITERS = 2
VIEWS = 6
TAPS = 33
R = 16
BZ = 16
BX = 16
NY = 128
SEND = 3
SRC = 96
PEERS = 64
EX = BX + 2 * R
EZ = BZ + 2 * R
SLOTS = VIEWS * BZ
CHUNK = SEND * BX + 1
VU = VIEWS * BX
PITCH = VU + 8
LINE = BZ + 8
AT_ONCE = 4
F32 = jnp.float32
BF16 = jnp.bfloat16

VMEM = pl.BlockSpec(memory_space=pltpu.VMEM)
SMEM = pl.BlockSpec(memory_space=pltpu.SMEM)


def params(mib):
    return pltpu.CompilerParams(vmem_limit_bytes=mib * 1024 * 1024)


def shape(dims, dtype=F32):
    return jax.ShapeDtypeStruct(dims, dtype)


def split(value):
    high = value.astype(BF16)
    return high, (value - high.astype(F32)).astype(BF16)


def pack_kernel(owner, slot, planes, send, rows, count):
    for peer in range(PEERS):
        count[peer] = 0
    send[pl.ds(SEND * BX, PEERS, stride=CHUNK), :] = jnp.full((PEERS, NY), SLOTS, F32)
    for group in range(SRC // 8):
        for column in range(BX):
            rows[pl.ds(group * 8 * BX + column, 8, stride=BX), :] = planes[
                group * 8 : group * 8 + 8, column * NY : (column + 1) * NY
            ]
    lane = lax.broadcasted_iota(jnp.int32, (1, NY), 1)

    def place(plane, carry):
        peer = owner[plane]
        rank = count[peer]
        count[peer] = rank + 1
        start = peer * CHUNK
        send[pl.ds(start + rank * BX, BX), :] = rows[pl.ds(pl.multiple_of(plane * BX, BX), BX), :]
        pltpu.store(
            send.at[pl.ds(start + SEND * BX, 1), :],
            jnp.full((1, NY), slot[plane], jnp.int32).astype(F32),
            mask=lane == rank,
        )
        return carry

    lax.fori_loop(0, SRC, place, 0, unroll=8)


def pack(owner, slot, planes):
    return pl.pallas_call(
        pack_kernel,
        out_shape=shape((PEERS * CHUNK, NY)),
        in_specs=[SMEM, SMEM, VMEM],
        out_specs=VMEM,
        scratch_shapes=[
            pltpu.VMEM((SRC * BX, NY), F32),
            pltpu.SMEM((PEERS,), jnp.int32),
        ],
        compiler_params=params(16),
        name="pack_planes",
    )(owner, slot, planes)


def bands(taps, first):
    row = lax.broadcasted_iota(jnp.int32, (BX, NY), 0)
    lane = lax.broadcasted_iota(jnp.int32, (BX, NY), 1)
    each = []
    for view in range(VIEWS):
        band = jnp.zeros((BX, NY), F32)
        for tap in range(TAPS):
            band = jnp.where(lane - row == tap, taps[first + view, tap], band)
        each.append(band)
    return jnp.concatenate(each + [jnp.zeros((NY - VU, NY), F32)], axis=0)


def by_terms(value):
    high, low = split(value)
    return jnp.concatenate([high, low, high], axis=1)


def weight_kernel(taps, shift, z_fwd, z_back, x_fwd, x_back, y_fwd, y_back):
    band = bands(taps, 0)
    turned = jnp.transpose(band)[:EZ]
    for view in range(VIEWS):
        z_fwd[view] = by_terms(band[view * BZ : (view + 1) * BZ, :EZ])
        z_back[view] = by_terms(turned[:, view * BZ : (view + 1) * BZ])
    band = bands(taps, VIEWS)
    x_fwd[...] = by_terms(band[:VU, :EX])
    x_back[...] = by_terms(jnp.transpose(band)[:EX, :VU])
    row = lax.broadcasted_iota(jnp.int32, (NY, NY), 0)
    lane = lax.broadcasted_iota(jnp.int32, (NY, NY), 1)

    def along_y(view, carry):
        offset = lane - row + R + shift[view]
        back = jnp.zeros((NY, NY), F32)
        for tap in range(TAPS):
            back = jnp.where(offset == tap, taps[2 * VIEWS + view, tap], back)
        high, low = split(back)
        y_back[view] = jnp.concatenate([high, low, high], axis=0)
        high, low = split(jnp.transpose(back))
        y_fwd[view] = jnp.concatenate([high, low, high], axis=0)
        return carry

    lax.fori_loop(0, VIEWS, along_y, 0)


def weights(taps, shift):
    return pl.pallas_call(
        weight_kernel,
        out_shape=[
            shape((VIEWS, BZ, 3 * EZ), BF16),
            shape((VIEWS, EZ, 3 * BZ), BF16),
            shape((VU, 3 * EX), BF16),
            shape((EX, 3 * VU), BF16),
            shape((VIEWS, 3 * NY, NY), BF16),
            shape((VIEWS, 3 * NY, NY), BF16),
        ],
        in_specs=[SMEM, SMEM],
        out_specs=[VMEM] * 6,
        compiler_params=params(16),
        name="operator_matrices",
    )(taps, shift)


def dot(left, right):
    return jnp.dot(left, right, preferred_element_type=F32)


def terms(value):
    high, low = split(value)
    return jnp.concatenate([high, high, low], axis=0)


def along_x_fwd(matrix, pieces, starts, wide):
    matrix = matrix[...]
    for piece, start in zip(pieces, starts):
        for first in range(0, BZ, AT_ONCE):
            planes = range(first, first + AT_ONCE)
            product = dot(matrix, jnp.concatenate([terms(piece[p]) for p in planes], axis=1))
            for i, plane in enumerate(planes):
                rows = pl.ds(pl.multiple_of((start + plane) * PITCH, 8), VU)
                wide[rows, :] = product[:, i * NY : (i + 1) * NY]


def along_z_fwd(matrix, wide, narrow):
    def one(view, carry):
        for first in range(0, BX, AT_ONCE):
            columns = range(first, first + AT_ONCE)
            loaded = [wide[pl.ds(view * BX + c, EZ, stride=PITCH), :] for c in columns]
            product = dot(matrix[view], jnp.concatenate([terms(v) for v in loaded], axis=1))
            for i, column in enumerate(columns):
                rows = pl.ds(pl.multiple_of((view * BX + column) * BZ, BZ), BZ)
                narrow[rows, :] = product[:, i * NY : (i + 1) * NY]
        return carry

    lax.fori_loop(0, VIEWS, one, 0)


def rows_of(view):
    return pl.ds(view * BZ * BX, BZ * BX)


def along_y(matrix, value):
    high, low = split(value)
    return dot(jnp.concatenate([high, high, low], axis=1), matrix)


def placed(core):
    inside = jnp.where(core == 0, 2 * R, 0)
    outside = jnp.where(core == 0, 0, 2 * R)
    return [R, inside, outside]


def forward_kernel(
    core, background, z_fwd, x_fwd, y_fwd, own, inside, outside, blur, wide, narrow
):
    along_x_fwd(x_fwd, [own, inside, outside], placed(core[0]), wide)
    along_z_fwd(z_fwd, wide, narrow)
    for view in range(VIEWS):
        blur[rows_of(view), :] = along_y(y_fwd[view], narrow[rows_of(view), :]) + background[view]


def forward(core, background, z_fwd, x_fwd, y_fwd, own, inside, outside):
    return pl.pallas_call(
        forward_kernel,
        out_shape=shape((SLOTS * BX, NY)),
        in_specs=[SMEM] * 2 + [VMEM] * 6,
        out_specs=VMEM,
        scratch_shapes=[pltpu.VMEM((EZ * PITCH, NY), F32), pltpu.VMEM((SLOTS * BX, NY), F32)],
        compiler_params=params(24),
        name="forward",
    )(core, background, z_fwd, x_fwd, y_fwd, own, inside, outside)


def along_z_back(matrix, narrow, wide):
    def one(view, carry):
        for first in range(0, BX, AT_ONCE):
            columns = range(first, first + AT_ONCE)
            loaded = [
                narrow[pl.ds(pl.multiple_of((view * BX + c) * BZ, BZ), BZ), :] for c in columns
            ]
            product = dot(matrix[view], jnp.concatenate([terms(v) for v in loaded], axis=1))
            for i, column in enumerate(columns):
                wide[pl.ds(view * BX + column, EZ, stride=PITCH), :] = product[
                    :, i * NY : (i + 1) * NY
                ]
        return carry

    lax.fori_loop(0, VIEWS, one, 0)


def along_x_back(matrix, wide, pieces, starts):
    matrix = matrix[...]
    for piece, start in zip(pieces, starts):
        for first in range(0, BZ, AT_ONCE):
            planes = range(first, first + AT_ONCE)
            loaded = [
                wide[pl.ds(pl.multiple_of((start + p) * PITCH, 8), VU), :] for p in planes
            ]
            product = dot(matrix, jnp.concatenate([terms(v) for v in loaded], axis=1))
            for i, plane in enumerate(planes):
                piece[plane] = product[:, i * NY : (i + 1) * NY]


def back_steps(core, z_back, x_back, y_back, data, blur, own, inside, outside, wide, narrow):
    for view in range(VIEWS):
        lines = [
            data[pl.ds((view * BX + column) * LINE, BZ), :] for column in range(BX)
        ]
        ratio = jnp.concatenate(lines, axis=0) / blur[rows_of(view), :]
        narrow[rows_of(view), :] = along_y(y_back[view], ratio)
    along_z_back(z_back, narrow, wide)
    along_x_back(x_back, wide, [own, inside, outside], placed(core[0]))


def first_back_kernel(
    core, z_back, x_back, y_back, got, blur, data, own, inside, outside,
    wide, narrow, names, slots, sem,
):
    names[...] = got[pl.ds(SEND * BX, PEERS, stride=CHUNK), :].astype(jnp.int32)
    copy = pltpu.make_async_copy(names, slots, sem)
    copy.start()
    copy.wait()

    def unpack(peer, carry):
        for rank in range(SEND):
            slot = slots[peer, rank]
            start = (slot // BZ) * (BX * LINE) + slot % BZ
            data[pl.ds(start, BX, stride=LINE), :] = got[pl.ds(peer * CHUNK + rank * BX, BX), :]
        return carry

    lax.fori_loop(0, PEERS, unpack, 0, unroll=4)
    back_steps(core, z_back, x_back, y_back, data, blur, own, inside, outside, wide, narrow)


def first_back(core, z_back, x_back, y_back, got, blur):
    return pl.pallas_call(
        first_back_kernel,
        out_shape=[shape(((VIEWS + 1) * BX * LINE, NY))] + [shape((BZ, EX, NY))] * 3,
        in_specs=[SMEM] + [VMEM] * 5,
        out_specs=[VMEM] * 4,
        scratch_shapes=[
            pltpu.VMEM((EZ * PITCH, NY), F32),
            pltpu.VMEM((SLOTS * BX, NY), F32),
            pltpu.VMEM((PEERS, NY), jnp.int32),
            pltpu.SMEM((PEERS, NY), jnp.int32),
            pltpu.SemaphoreType.DMA,
        ],
        compiler_params=params(24),
        name="first_back",
    )(core, z_back, x_back, y_back, got, blur)


def later_kernel(
    core, background, z_fwd, x_fwd, y_fwd, z_back, x_back, y_back, e_own, e_inside, e_outside,
    data, own, inside, outside, wide, narrow, blur,
):
    forward_kernel(
        core, background, z_fwd, x_fwd, y_fwd, e_own, e_inside, e_outside, blur, wide, narrow
    )
    back_steps(core, z_back, x_back, y_back, data, blur, own, inside, outside, wide, narrow)


def later(core, background, forth, back, pieces, data):
    return pl.pallas_call(
        later_kernel,
        out_shape=[shape((BZ, EX, NY))] * 3,
        in_specs=[SMEM] * 2 + [VMEM] * 10,
        out_specs=[VMEM] * 3,
        scratch_shapes=[
            pltpu.VMEM((EZ * PITCH, NY), F32),
            pltpu.VMEM((SLOTS * BX, NY), F32),
            pltpu.VMEM((SLOTS * BX, NY), F32),
        ],
        compiler_params=params(24),
        name="forward_and_back",
    )(core, background, *forth, *back, *pieces, data)


def swaps(first, count):
    pairs = [(i, i + 1) for i in range(first, count - 1, 2)]
    return pairs + [(j, i) for i, j in pairs]


def beside(block):
    return lax.ppermute(block, "xy", swaps(0, PEERS)), lax.ppermute(block, "xy", swaps(1, PEERS))


def gathered(block, even_pair, odd_pair, odd):
    left = jnp.where(odd, even_pair, odd_pair)
    right = jnp.where(odd, odd_pair, even_pair)
    own = jnp.concatenate([left, block, right], axis=1)
    count = lax.axis_size("gz")
    return own, lax.ppermute(own, "gz", swaps(0, count)), lax.ppermute(own, "gz", swaps(1, count))


def scattered(own, inside, outside, odd):
    count = lax.axis_size("gz")
    total = (
        own
        + lax.ppermute(outside, "gz", swaps(1, count))
        + lax.ppermute(inside, "gz", swaps(0, count))
    )
    left, right = total[:, :R], total[:, R + BX :]
    even_pair = lax.ppermute(jnp.where(odd, left, right), "xy", swaps(0, PEERS))
    odd_pair = lax.ppermute(jnp.where(odd, right, left), "xy", swaps(1, PEERS))
    return total[:, R : R + BX] + even_pair + odd_pair


def local(
    tile_planes,
    plane_owner,
    plane_slot,
    view_shift,
    psf_z,
    psf_x,
    psf_y,
    background,
    initial_estimate,
):
    core = lax.rem(lax.axis_index("gz"), 2).astype(jnp.int32).reshape(1)
    odd = lax.rem(lax.axis_index("xy"), 2) == 1
    send = pack(plane_owner.reshape(SRC), plane_slot.reshape(SRC), tile_planes[0])
    send, *sides = lax.optimization_barrier((send, *beside(initial_estimate)))
    got = lax.all_to_all(
        send.reshape(PEERS, 1, CHUNK * NY), "xy", split_axis=0, concat_axis=0, tiled=True
    ).reshape(PEERS * CHUNK, NY)
    psf = jnp.concatenate([psf_z, psf_x, psf_y], axis=0)
    taps = psf / jnp.sum(psf, axis=1, keepdims=True)
    matrices = weights(taps, view_shift)
    forth, back = matrices[::2], matrices[1::2]
    estimate = initial_estimate
    for step in range(ITERS):
        if step:
            sides = beside(estimate)
        pieces = gathered(estimate, *sides, odd)
        if step == 0:
            blur = forward(core, background, *forth, *pieces)
            data, *parts = first_back(core, *back, got, blur)
        else:
            parts = later(core, background, forth, back, pieces, data)
        estimate = estimate * (scattered(*parts, odd) / VIEWS)
    return estimate


def solution(mesh):
    return jax.shard_map(
        local,
        mesh=mesh,
        in_specs=(
            P("gz", "xy", None),
            P("gz", "xy", None),
            P("gz", "xy"),
            P(),
            P(),
            P(),
            P(),
            P(),
            P("gz", "xy", None),
        ),
        out_specs=P("gz", "xy", None),
        check_vma=False,
    )
```

time: 173 us -> 146 us (0.84)
  the two profiles are of different devices: /device:TPU:36 before, /device:TPU:34 now
where the time goes in v1:
time: 146 us; the launch traced here: 145 us
  starting transfers between devices  66.8 us (46%)
  waiting for transfers between devices  51.2 us (35%)
  Pallas kernels  17.6 us (12%)
  local copies, waits for them, and re-layouts  8.16 us (6%)
    all_to_all x1, waiting for transfers between devices, local(): lax.all_to_all(send.reshape(PEERS, 1, CHUNK * NY), 'xy', split_axis=0, co...  22.8 us
    ppermute x2, starting transfers between devices, beside(): lax.ppermute(block, 'xy', swaps(1, PEERS))  17.5 us
    all_to_all x1, starting transfers between devices, local(): lax.all_to_all(send.reshape(PEERS, 1, CHUNK * NY), 'xy', split_axis=0, co...  10.2 us
    ppermute x2, starting transfers between devices, scattered(): odd_pair = lax.ppermute(jnp.where(odd, right, left), 'xy', swaps(1, PEERS))  9.95 us
    ppermute x2, waiting for transfers between devices, scattered(): odd_pair = lax.ppermute(jnp.where(odd, right, left), 'xy', swaps(1, PEERS))  9.33 us
    unnamed x36, local copies, waits for them, and re-layouts  8.16 us
    ppermute x2, waiting for transfers between devices, scattered(): lax.ppermute(outside, 'gz', swaps(1, count))  7.56 us
    ppermute x2, starting transfers between devices, gathered(): lax.ppermute(own, 'gz', swaps(0, count))  6.76 us
  transfers between devices with their start and end apart: 17, of which 11 were waited for; matrix products, arithmetic and copies ran while one was open for 0% of the time, Pallas kernels for 5%

profile of v1, /device:TPU:34, one launch (start us, length us, event | category | flops | bytes accessed | tf_op | source)
XLA Modules:
  0.0 145.3 jit_solution(2527083360076305498)
XLA Ops:
  0.0 10.8 %collective-permute-start.1 = (f32[16,16,128]{2,1,0:T(8,128)}, f32[16,16,128]{2,1,0:T(8,128)S(1)}, u32[]{:S(2)}, u32[]{:S(2)}) collective-permute-start(f32[16,16,128]{2,1,0:T(8,128)} %param.17), channel_id=1, source_target_pairs={{1,2},{3,4},{5,6},{7,8},{9,10},{11,12},{13,14},{15,16},{17,18},{19... | collective-permute-start | bytes 393224 | tf_op jit(solution)/shard_map/ppermute | solution.py:330
  10.8 1.9 %collective-permute-start = (f32[16,16,128]{2,1,0:T(8,128)}, f32[16,16,128]{2,1,0:T(8,128)S(1)}, u32[]{:S(2)}, u32[]{:S(2)}) collective-permute-start(f32[16,16,128]{2,1,0:T(8,128)} %param.17), channel_id=1, source_target_pairs={{0,1},{2,3},{4,5},{6,7},{8,9},{10,11},{12,13},{14,15},{16,17},{18,... | collective-permute-start | bytes 393224 | tf_op jit(solution)/shard_map/ppermute | solution.py:330
  12.8 0.0 copy-start.2
  12.8 1.1 copy-done.2
  13.9 0.7 copy-done.10
  14.6 0.7 copy-done.11
  15.2 2.4 %pack_planes.1 = f32[3136,128]{1,0:T(8,128)} custom-call(s32[96]{0:T(128)S(1)} %bitcast.8, s32[96]{0:T(128)S(1)} %bitcast.9, f32[96,2048]{1,0:T(8,128)S(1)} %bitcast.7), custom_call_target="tpu_custom_call" | custom-call | tf_op jit(solution)/shard_map/pack_planes/pallas_call | solution.py:74
  17.6 0.0 collective-permute-done.1
  17.6 0.3 collective-permute-done
  17.9 0.0 copy-start.12
  17.9 0.0 copy-start.9
  17.9 10.2 %all-to-all-start = ((f32[64,1,6272]{2,1,0:T(1,128)}), f32[64,1,6272]{2,1,0:T(1,128)S(1)}, u32[]{:S(2)}, u32[]{:S(2)}) async-start(f32[64,1,6272]{2,1,0:T(1,128)} %bitcast.4), calls=%async_computation | async-start | bytes 3211264 | tf_op jit(solution)/shard_map/all_to_all | solution.py:369
  28.2 0.0 copy-done.13
  28.3 1.9 %collective-permute-start.3 = (f32[16,48,128]{2,1,0:T(8,128)S(1)}, f32[16,48,128]{2,1,0:T(8,128)S(1)}, u32[]{:S(2)}, u32[]{:S(2)}) collective-permute-start(f32[16,48,128]{2,1,0:T(8,128)S(1)} %pad_maximum_fusion.own), channel_id=1, source_target_pairs={{64,128},{192,256},{320,384},{128,64},{256,192},{384,320},{65,129}... | collective-permute-start | bytes 1179656 | tf_op jit(solution)/shard_map/ppermute | solution.py:338
  30.2 3.5 %collective-permute-start.2 = (f32[16,48,128]{2,1,0:T(8,128)S(1)}, f32[16,48,128]{2,1,0:T(8,128)S(1)}, u32[]{:S(2)}, u32[]{:S(2)}) collective-permute-start(f32[16,48,128]{2,1,0:T(8,128)S(1)} %pad_maximum_fusion.own), channel_id=1, source_target_pairs={{0,64},{128,192},{256,320},{384,448},{64,0},{192,128},{320,256},{4... | collective-permute-start | bytes 1179656 | tf_op jit(solution)/shard_map/ppermute | solution.py:338
  33.7 0.0 copy-done.15
  33.7 0.0 copy-done.16
  33.7 0.1 fusion.7
  33.9 0.1 fusion.6.taps
  33.9 0.0 copy-done.12
  33.9 2.6 %operator_matrices.1 = (bf16[6,16,144]{2,1,0:T(8,128)(2,1)S(1)}, bf16[6,48,48]{2,1,0:T(8,128)(2,1)S(1)}, bf16[96,144]{1,0:T(8,128)(2,1)S(1)}, bf16[48,288]{1,0:T...) custom-call(f32[18,33]{1,0:T(8,128)S(1)} %fusion.6.taps, s32[6]{0:T(128)S(1)} %copy-done.12), custom_call_target="tpu_custom_call" | custom-call | tf_op jit(solution)/shard_map/operator_matrices/pallas_call | solution.py:132
  36.5 0.0 copy-start.7
  36.5 0.6 copy-done.7
  37.1 0.2 collective-permute-done.3.outside
  37.4 0.7 copy-done.3
  38.1 0.0 collective-permute-done.2.inside
  38.1 0.7 copy-done.5
  38.9 1.0 copy-done.4
  39.9 1.0 copy-done.6
  40.9 2.7 %forward.1.blur = f32[1536,128]{1,0:T(8,128)S(1)} custom-call(s32[1]{0:T(128)} %bitcast.core, f32[6]{0:T(128)S(1)} %copy-done.9, bf16[6,16,144]{2,1,0:T(8,128)(2,1)S(1)} %get-tuple-element.25.z_fwd, bf16[96,144]{1,0:T(8,128)(2,1)S(1)} %get-tuple-element.26.x_fwd, bf16[6,384,128]{2,1,0:T(8,128)(2,1)S(1)} %get-tuple-element.27.y_fwd, ...), custom_call_target="tpu_custom_call" | custom-call | tf_op jit(solution)/shard_map/forward/pallas_call | solution.py:208
  43.5 0.0 copy-start
  43.5 0.8 copy-done
  44.4 22.8 %all-to-all-done = f32[64,1,6272]{2,1,0:T(1,128)S(1)} async-done(((f32[64,1,6272]{2,1,0:T(1,128)}), f32[64,1,6272]{2,1,0:T(1,128)S(1)}, u32[]{:S(2)}, u32[]{:S(2)}) %all-to-all-start) | async-done | bytes 1605664 | tf_op jit(solution)/shard_map/all_to_all | solution.py:369
  67.2 0.8 copy-done.8
  68.0 4.9 %first_back.1 = (f32[2688,128]{1,0:T(8,128)S(1)}, f32[16,48,128]{2,1,0:T(8,128)S(1)}, f32[16,48,128]{2,1,0:T(8,128)S(1)}, f32[16,48,128]{2,1,0:T(8,128)S(1)}) custom-call(s32[1]{0:T(128)} %bitcast.core, bf16[6,48,48]{2,1,0:T(8,128)(2,1)S(1)} %get-tuple-element.21.z_back, bf16[48,288]{1,0:T(8,128)(2,1)S(1)} %copy-done.8, ...), custom_call_target="tpu_custom_call" | custom-call | tf_op jit(solution)/shard_map/first_back/pallas_call | solution.py:281
  72.9 0.0 copy-start.14
  72.9 2.1 %collective-permute-start.4 = (f32[16,48,128]{2,1,0:T(8,128)S(1)}, f32[16,48,128]{2,1,0:T(8,128)S(1)}, u32[]{:S(2)}, u32[]{:S(2)}) collective-permute-start(f32[16,48,128]{2,1,0:T(8,128)S(1)} %get-tuple-element.31), channel_id=1, source_target_pairs={{64,128},{192,256},{320,384},{128,64},{256,192},{384,320},{65,129}... | collective-permute-start | bytes 1179656 | tf_op jit(solution)/shard_map/ppermute | solution.py:345
  75.0 3.5 %collective-permute-start.5 = (f32[16,48,128]{2,1,0:T(8,128)S(1)}, f32[16,48,128]{2,1,0:T(8,128)S(1)}, u32[]{:S(2)}, u32[]{:S(2)}) collective-permute-start(f32[16,48,128]{2,1,0:T(8,128)S(1)} %get-tuple-element.32), channel_id=1, source_target_pairs={{0,64},{128,192},{256,320},{384,448},{64,0},{192,128},{320,256},{4... | collective-permute-start | bytes 1179656 | tf_op jit(solution)/shard_map/ppermute | solution.py:346
  78.5 3.7 %collective-permute-done.4 = f32[16,48,128]{2,1,0:T(8,128)S(1)} collective-permute-done((f32[16,48,128]{2,1,0:T(8,128)S(1)}, f32[16,48,128]{2,1,0:T(8,128)S(1)}, u32[]{:S(2)}, u32[]{:S(2)}) %collective-permute-start.4) | collective-permute-done | bytes 393248 | tf_op jit(solution)/shard_map/ppermute | solution.py:345
  82.2 0.0 collective-permute-done.5
  82.2 0.1 add_add_fusion.1
  82.3 2.1 %collective-permute-start.6 = (f32[16,16,128]{2,1,0:T(8,128)S(1)}, f32[16,16,128]{2,1,0:T(8,128)S(1)}, u32[]{:S(2)}, u32[]{:S(2)}) collective-permute-start(f32[16,16,128]{2,1,0:T(8,128)S(1)} %get-tuple-element.39), channel_id=1, source_target_pairs={{0,1},{2,3},{4,5},{6,7},{8,9},{10,11},{12,13},{14,15},{16,17},{18,... | collective-permute-start | bytes 393224 | tf_op jit(solution)/shard_map/ppermute | solution.py:349
  84.3 6.6 %collective-permute-start.7 = (f32[16,16,128]{2,1,0:T(8,128)S(1)}, f32[16,16,128]{2,1,0:T(8,128)S(1)}, u32[]{:S(2)}, u32[]{:S(2)}) collective-permute-start(f32[16,16,128]{2,1,0:T(8,128)S(1)} %get-tuple-element.40), channel_id=1, source_target_pairs={{1,2},{3,4},{5,6},{7,8},{9,10},{11,12},{13,14},{15,16},{17,18},{19... | collective-permute-start | bytes 393224 | tf_op jit(solution)/shard_map/ppermute | solution.py:350
  91.0 0.0 collective-permute-done.6
  91.0 4.1 %collective-permute-done.7 = f32[16,16,128]{2,1,0:T(8,128)S(1)} collective-permute-done((f32[16,16,128]{2,1,0:T(8,128)S(1)}, f32[16,16,128]{2,1,0:T(8,128)S(1)}, u32[]{:S(2)}, u32[]{:S(2)}) %collective-permute-start.7) | collective-permute-done | bytes 131104 | tf_op jit(solution)/shard_map/ppermute | solution.py:350
  95.1 6.6 %collective-permute-start.9 = (f32[16,16,128]{2,1,0:T(8,128)S(1)}, f32[16,16,128]{2,1,0:T(8,128)S(1)}, u32[]{:S(2)}, u32[]{:S(2)}) collective-permute-start(f32[16,16,128]{2,1,0:T(8,128)S(1)} %fusion.5), channel_id=1, source_target_pairs={{1,2},{3,4},{5,6},{7,8},{9,10},{11,12},{13,14},{15,16},{17,18},{19... | collective-permute-start | bytes 393224 | tf_op jit(solution)/shard_map/ppermute | solution.py:330
  101.8 1.9 %collective-permute-start.8 = (f32[16,16,128]{2,1,0:T(8,128)S(1)}, f32[16,16,128]{2,1,0:T(8,128)S(1)}, u32[]{:S(2)}, u32[]{:S(2)}) collective-permute-start(f32[16,16,128]{2,1,0:T(8,128)S(1)} %fusion.5), channel_id=1, source_target_pairs={{0,1},{2,3},{4,5},{6,7},{8,9},{10,11},{12,13},{14,15},{16,17},{18,... | collective-permute-start | bytes 393224 | tf_op jit(solution)/shard_map/ppermute | solution.py:330
  103.7 1.6 %collective-permute-done.9 = f32[16,16,128]{2,1,0:T(8,128)S(1)} collective-permute-done((f32[16,16,128]{2,1,0:T(8,128)S(1)}, f32[16,16,128]{2,1,0:T(8,128)S(1)}, u32[]{:S(2)}, u32[]{:S(2)}) %collective-permute-start.9) | collective-permute-done | bytes 131104 | tf_op jit(solution)/shard_map/ppermute | solution.py:330
  105.3 3.3 %collective-permute-done.8 = f32[16,16,128]{2,1,0:T(8,128)S(1)} collective-permute-done((f32[16,16,128]{2,1,0:T(8,128)S(1)}, f32[16,16,128]{2,1,0:T(8,128)S(1)}, u32[]{:S(2)}, u32[]{:S(2)}) %collective-permute-start.8) | collective-permute-done | bytes 131104 | tf_op jit(solution)/shard_map/ppermute | solution.py:330
  108.7 1.9 %collective-permute-start.11 = (f32[16,48,128]{2,1,0:T(8,128)S(1)}, f32[16,48,128]{2,1,0:T(8,128)S(1)}, u32[]{:S(2)}, u32[]{:S(2)}) collective-permute-start(f32[16,48,128]{2,1,0:T(8,128)S(1)} %pad_maximum_fusion.1.e_own), channel_id=1, source_target_pairs={{64,128},{192,256},{320,384},{128,64},{256,192},{384,320},{65,129}... | collective-permute-start | bytes 1179656 | tf_op jit(solution)/shard_map/ppermute | solution.py:338
  110.6 3.3 %collective-permute-start.10 = (f32[16,48,128]{2,1,0:T(8,128)S(1)}, f32[16,48,128]{2,1,0:T(8,128)S(1)}, u32[]{:S(2)}, u32[]{:S(2)}) collective-permute-start(f32[16,48,128]{2,1,0:T(8,128)S(1)} %pad_maximum_fusion.1.e_own), channel_id=1, source_target_pairs={{0,64},{128,192},{256,320},{384,448},{64,0},{192,128},{320,256},{4... | collective-permute-start | bytes 1179656 | tf_op jit(solution)/shard_map/ppermute | solution.py:338
  113.9 3.9 %collective-permute-done.11.e_outside = f32[16,48,128]{2,1,0:T(8,128)S(1)} collective-permute-done((f32[16,48,128]{2,1,0:T(8,128)S(1)}, f32[16,48,128]{2,1,0:T(8,128)S(1)}, u32[]{:S(2)}, u32[]{:S(2)}) %collective-permute-start.11) | collective-permute-done | bytes 393248 | tf_op jit(solution)/shard_map/ppermute | solution.py:338
  117.8 0.0 collective-permute-done.10.e_inside
  117.8 5.0 %forward_and_back.1 = (f32[16,48,128]{2,1,0:T(8,128)S(1)}, f32[16,48,128]{2,1,0:T(8,128)S(1)}, f32[16,48,128]{2,1,0:T(8,128)S(1)}) custom-call(s32[1]{0:T(128)} %bitcast.core, f32[6]{0:T(128)S(1)} %copy-done.9, bf16[6,16,144]{2,1,0:T(8,128)(2,1)S(1)} %get-tuple-element.25.z_fwd, bf16[96,144]{1,0:T(8,128)(2,1)S(1)} %get-tuple-element.26.x_fwd, ...), custom_call_target="tpu_custom_call" | custom-call | tf_op jit(solution)/shard_map/forward_and_back/pallas_call | solution.py:309
  122.8 1.9 %collective-permute-start.12 = (f32[16,48,128]{2,1,0:T(8,128)S(1)}, f32[16,48,128]{2,1,0:T(8,128)S(1)}, u32[]{:S(2)}, u32[]{:S(2)}) collective-permute-start(f32[16,48,128]{2,1,0:T(8,128)S(1)} %get-tuple-element.35), channel_id=1, source_target_pairs={{64,128},{192,256},{320,384},{128,64},{256,192},{384,320},{65,129}... | collective-permute-start | bytes 1179656 | tf_op jit(solution)/shard_map/ppermute | solution.py:345
  124.7 3.3 %collective-permute-start.13 = (f32[16,48,128]{2,1,0:T(8,128)S(1)}, f32[16,48,128]{2,1,0:T(8,128)S(1)}, u32[]{:S(2)}, u32[]{:S(2)}) collective-permute-start(f32[16,48,128]{2,1,0:T(8,128)S(1)} %get-tuple-element.36), channel_id=1, source_target_pairs={{0,64},{128,192},{256,320},{384,448},{64,0},{192,128},{320,256},{4... | collective-permute-start | bytes 1179656 | tf_op jit(solution)/shard_map/ppermute | solution.py:346
  128.0 3.9 %collective-permute-done.12 = f32[16,48,128]{2,1,0:T(8,128)S(1)} collective-permute-done((f32[16,48,128]{2,1,0:T(8,128)S(1)}, f32[16,48,128]{2,1,0:T(8,128)S(1)}, u32[]{:S(2)}, u32[]{:S(2)}) %collective-permute-start.12) | collective-permute-done | bytes 393248 | tf_op jit(solution)/shard_map/ppermute | solution.py:345
  131.9 0.0 collective-permute-done.13
  131.9 0.1 add_add_fusion
  132.0 1.9 %collective-permute-start.14 = (f32[16,16,128]{2,1,0:T(8,128)S(1)}, f32[16,16,128]{2,1,0:T(8,128)S(1)}, u32[]{:S(2)}, u32[]{:S(2)}) collective-permute-start(f32[16,16,128]{2,1,0:T(8,128)S(1)} %get-tuple-element.37), channel_id=1, source_target_pairs={{0,1},{2,3},{4,5},{6,7},{8,9},{10,11},{12,13},{14,15},{16,17},{18,... | collective-permute-start | bytes 393224 | tf_op jit(solution)/shard_map/ppermute | solution.py:349
  133.9 3.3 %collective-permute-start.15 = (f32[16,16,128]{2,1,0:T(8,128)S(1)}, f32[16,16,128]{2,1,0:T(8,128)S(1)}, u32[]{:S(2)}, u32[]{:S(2)}) collective-permute-start(f32[16,16,128]{2,1,0:T(8,128)S(1)} %get-tuple-element.38), channel_id=1, source_target_pairs={{1,2},{3,4},{5,6},{7,8},{9,10},{11,12},{13,14},{15,16},{17,18},{19... | collective-permute-start | bytes 393224 | tf_op jit(solution)/shard_map/ppermute | solution.py:350
  137.2 2.2 %collective-permute-done.14 = f32[16,16,128]{2,1,0:T(8,128)S(1)} collective-permute-done((f32[16,16,128]{2,1,0:T(8,128)S(1)}, f32[16,16,128]{2,1,0:T(8,128)S(1)}, u32[]{:S(2)}, u32[]{:S(2)}) %collective-permute-start.14) | collective-permute-done | bytes 131104 | tf_op jit(solution)/shard_map/ppermute | solution.py:349
  139.4 5.2 %collective-permute-done.15 = f32[16,16,128]{2,1,0:T(8,128)S(1)} collective-permute-done((f32[16,16,128]{2,1,0:T(8,128)S(1)}, f32[16,16,128]{2,1,0:T(8,128)S(1)}, u32[]{:S(2)}, u32[]{:S(2)}) %collective-permute-start.15) | collective-permute-done | bytes 131104 | tf_op jit(solution)/shard_map/ppermute | solution.py:350
  144.6 0.7 fusion.2
  (23 shorter events, 0.2 us)
Async XLA Ops:
  0.0 17.6 %collective-permute-start.1 = (f32[16,16,128]{2,1,0:T(8,128)}, f32[16,16,128]{2,1,0:T(8,128)S(1)}, u32[]{:S(2)}, u32[]{:S(2)}) collective-permute-start(f32[16,16,128]{2,1,0:T(8,128)} %param.17), channel_id=1, source_target_pairs={{1,2},{3,4},{5,6},{7,8},{9,10},{11,12},{13,14},{15,16},{17,18},{19... | collective-permute-start | bytes 393224 | tf_op jit(solution)/shard_map/ppermute | solution.py:330
  10.8 7.1 %collective-permute-start = (f32[16,16,128]{2,1,0:T(8,128)}, f32[16,16,128]{2,1,0:T(8,128)S(1)}, u32[]{:S(2)}, u32[]{:S(2)}) collective-permute-start(f32[16,16,128]{2,1,0:T(8,128)} %param.17), channel_id=1, source_target_pairs={{0,1},{2,3},{4,5},{6,7},{8,9},{10,11},{12,13},{14,15},{16,17},{18,... | collective-permute-start | bytes 393224 | tf_op jit(solution)/shard_map/ppermute | solution.py:330
  12.8 1.1 copy-start.2
  13.9 0.7 copy-start.10
  14.6 0.7 copy-start.11
  17.9 10.3 %copy-start.13 = (f32[16,16,128]{2,1,0:T(8,128)S(1)}, f32[16,16,128]{2,1,0:T(8,128)}, u32[]{:S(2)}) copy-start(f32[16,16,128]{2,1,0:T(8,128)} %param.17) | copy-start | bytes 393220
  17.9 15.8 %copy-start.15 = (f32[6,33]{1,0:T(8,128)S(1)}, f32[6,33]{1,0:T(8,128)}, u32[]{:S(2)}) copy-start(f32[6,33]{1,0:T(8,128)} %param.15) | copy-start | bytes 2380
  17.9 15.8 %copy-start.16 = (f32[6,33]{1,0:T(8,128)S(1)}, f32[6,33]{1,0:T(8,128)}, u32[]{:S(2)}) copy-start(f32[6,33]{1,0:T(8,128)} %param.14) | copy-start | bytes 2380
  17.9 15.8 %copy-start.17 = (f32[6,33]{1,0:T(8,128)S(1)}, f32[6,33]{1,0:T(8,128)}, u32[]{:S(2)}) copy-start(f32[6,33]{1,0:T(8,128)} %param.13) | copy-start | bytes 2380
  17.9 16.0 %copy-start.12 = (s32[6]{0:T(128)S(1)}, s32[6]{0:T(128)}, u32[]{:S(2)}) copy-start(s32[6]{0:T(128)} %shift.1) | copy-start | bytes 76
  17.9 20.9 %copy-start.9 = (f32[6]{0:T(128)S(1)}, f32[6]{0:T(128)}, u32[]{:S(2)}) copy-start(f32[6]{0:T(128)} %background.3) | copy-start | bytes 76
  17.9 49.3 %all-to-all-start = ((f32[64,1,6272]{2,1,0:T(1,128)}), f32[64,1,6272]{2,1,0:T(1,128)S(1)}, u32[]{:S(2)}, u32[]{:S(2)}) async-start(f32[64,1,6272]{2,1,0:T(1,128)} %bitcast.4), calls=%async_computation | async-start | bytes 3211264 | tf_op jit(solution)/shard_map/all_to_all | solution.py:369
  28.3 9.1 %collective-permute-start.3 = (f32[16,48,128]{2,1,0:T(8,128)S(1)}, f32[16,48,128]{2,1,0:T(8,128)S(1)}, u32[]{:S(2)}, u32[]{:S(2)}) collective-permute-start(f32[16,48,128]{2,1,0:T(8,128)S(1)} %pad_maximum_fusion.own), channel_id=1, source_target_pairs={{64,128},{192,256},{320,384},{128,64},{256,192},{384,320},{65,129}... | collective-permute-start | bytes 1179656 | tf_op jit(solution)/shard_map/ppermute | solution.py:338
  30.2 7.9 %collective-permute-start.2 = (f32[16,48,128]{2,1,0:T(8,128)S(1)}, f32[16,48,128]{2,1,0:T(8,128)S(1)}, u32[]{:S(2)}, u32[]{:S(2)}) collective-permute-start(f32[16,48,128]{2,1,0:T(8,128)S(1)} %pad_maximum_fusion.own), channel_id=1, source_target_pairs={{0,64},{128,192},{256,320},{384,448},{64,0},{192,128},{320,256},{4... | collective-permute-start | bytes 1179656 | tf_op jit(solution)/shard_map/ppermute | solution.py:338
  36.5 0.6 copy-start.7
  37.4 0.8 copy-start.3
  38.1 0.8 copy-start.5
  38.9 1.0 copy-start.4
  39.9 1.0 copy-start.6
  43.5 0.8 copy-start
  67.2 0.8 copy-start.8
  72.9 22.2 %copy-start.14 = (f32[16,16,128]{2,1,0:T(8,128)S(1)}, f32[16,16,128]{2,1,0:T(8,128)}, u32[]{:S(2)}) copy-start(f32[16,16,128]{2,1,0:T(8,128)} %param.17) | copy-start | bytes 393220
  72.9 9.2 %collective-permute-start.4 = (f32[16,48,128]{2,1,0:T(8,128)S(1)}, f32[16,48,128]{2,1,0:T(8,128)S(1)}, u32[]{:S(2)}, u32[]{:S(2)}) collective-permute-start(f32[16,48,128]{2,1,0:T(8,128)S(1)} %get-tuple-element.31), channel_id=1, source_target_pairs={{64,128},{192,256},{320,384},{128,64},{256,192},{384,320},{65,129}... | collective-permute-start | bytes 1179656 | tf_op jit(solution)/shard_map/ppermute | solution.py:345
  75.0 7.2 %collective-permute-start.5 = (f32[16,48,128]{2,1,0:T(8,128)S(1)}, f32[16,48,128]{2,1,0:T(8,128)S(1)}, u32[]{:S(2)}, u32[]{:S(2)}) collective-permute-start(f32[16,48,128]{2,1,0:T(8,128)S(1)} %get-tuple-element.32), channel_id=1, source_target_pairs={{0,64},{128,192},{256,320},{384,448},{64,0},{192,128},{320,256},{4... | collective-permute-start | bytes 1179656 | tf_op jit(solution)/shard_map/ppermute | solution.py:346
  82.2 35.5 %copy-start.1 = (bf16[6,384,128]{2,1,0:T(8,128)(2,1)S(1)}, bf16[6,384,128]{2,1,0:T(8,128)(2,1)}, u32[]{:S(2)}) copy-start(bf16[6,384,128]{2,1,0:T(8,128)(2,1)} %copy-done) | copy-start | bytes 1769476
  82.3 8.7 %collective-permute-start.6 = (f32[16,16,128]{2,1,0:T(8,128)S(1)}, f32[16,16,128]{2,1,0:T(8,128)S(1)}, u32[]{:S(2)}, u32[]{:S(2)}) collective-permute-start(f32[16,16,128]{2,1,0:T(8,128)S(1)} %get-tuple-element.39), channel_id=1, source_target_pairs={{0,1},{2,3},{4,5},{6,7},{8,9},{10,11},{12,13},{14,15},{16,17},{18,... | collective-permute-start | bytes 393224 | tf_op jit(solution)/shard_map/ppermute | solution.py:349
  84.3 10.7 %collective-permute-start.7 = (f32[16,16,128]{2,1,0:T(8,128)S(1)}, f32[16,16,128]{2,1,0:T(8,128)S(1)}, u32[]{:S(2)}, u32[]{:S(2)}) collective-permute-start(f32[16,16,128]{2,1,0:T(8,128)S(1)} %get-tuple-element.40), channel_id=1, source_target_pairs={{1,2},{3,4},{5,6},{7,8},{9,10},{11,12},{13,14},{15,16},{17,18},{19... | collective-permute-start | bytes 393224 | tf_op jit(solution)/shard_map/ppermute | solution.py:350
  95.1 10.2 %collective-permute-start.9 = (f32[16,16,128]{2,1,0:T(8,128)S(1)}, f32[16,16,128]{2,1,0:T(8,128)S(1)}, u32[]{:S(2)}, u32[]{:S(2)}) collective-permute-start(f32[16,16,128]{2,1,0:T(8,128)S(1)} %fusion.5), channel_id=1, source_target_pairs={{1,2},{3,4},{5,6},{7,8},{9,10},{11,12},{13,14},{15,16},{17,18},{19... | collective-permute-start | bytes 393224 | tf_op jit(solution)/shard_map/ppermute | solution.py:330
  101.8 6.9 %collective-permute-start.8 = (f32[16,16,128]{2,1,0:T(8,128)S(1)}, f32[16,16,128]{2,1,0:T(8,128)S(1)}, u32[]{:S(2)}, u32[]{:S(2)}) collective-permute-start(f32[16,16,128]{2,1,0:T(8,128)S(1)} %fusion.5), channel_id=1, source_target_pairs={{0,1},{2,3},{4,5},{6,7},{8,9},{10,11},{12,13},{14,15},{16,17},{18,... | collective-permute-start | bytes 393224 | tf_op jit(solution)/shard_map/ppermute | solution.py:330
  108.7 9.1 %collective-permute-start.11 = (f32[16,48,128]{2,1,0:T(8,128)S(1)}, f32[16,48,128]{2,1,0:T(8,128)S(1)}, u32[]{:S(2)}, u32[]{:S(2)}) collective-permute-start(f32[16,48,128]{2,1,0:T(8,128)S(1)} %pad_maximum_fusion.1.e_own), channel_id=1, source_target_pairs={{64,128},{192,256},{320,384},{128,64},{256,192},{384,320},{65,129}... | collective-permute-start | bytes 1179656 | tf_op jit(solution)/shard_map/ppermute | solution.py:338
  110.6 7.2 %collective-permute-start.10 = (f32[16,48,128]{2,1,0:T(8,128)S(1)}, f32[16,48,128]{2,1,0:T(8,128)S(1)}, u32[]{:S(2)}, u32[]{:S(2)}) collective-permute-start(f32[16,48,128]{2,1,0:T(8,128)S(1)} %pad_maximum_fusion.1.e_own), channel_id=1, source_target_pairs={{0,64},{128,192},{256,320},{384,448},{64,0},{192,128},{320,256},{4... | collective-permute-start | bytes 1179656 | tf_op jit(solution)/shard_map/ppermute | solution.py:338
  122.8 9.1 %collective-permute-start.12 = (f32[16,48,128]{2,1,0:T(8,128)S(1)}, f32[16,48,128]{2,1,0:T(8,128)S(1)}, u32[]{:S(2)}, u32[]{:S(2)}) collective-permute-start(f32[16,48,128]{2,1,0:T(8,128)S(1)} %get-tuple-element.35), channel_id=1, source_target_pairs={{64,128},{192,256},{320,384},{128,64},{256,192},{384,320},{65,129}... | collective-permute-start | bytes 1179656 | tf_op jit(solution)/shard_map/ppermute | solution.py:345
  124.7 7.2 %collective-permute-start.13 = (f32[16,48,128]{2,1,0:T(8,128)S(1)}, f32[16,48,128]{2,1,0:T(8,128)S(1)}, u32[]{:S(2)}, u32[]{:S(2)}) collective-permute-start(f32[16,48,128]{2,1,0:T(8,128)S(1)} %get-tuple-element.36), channel_id=1, source_target_pairs={{0,64},{128,192},{256,320},{384,448},{64,0},{192,128},{320,256},{4... | collective-permute-start | bytes 1179656 | tf_op jit(solution)/shard_map/ppermute | solution.py:346
  132.0 7.4 %collective-permute-start.14 = (f32[16,16,128]{2,1,0:T(8,128)S(1)}, f32[16,16,128]{2,1,0:T(8,128)S(1)}, u32[]{:S(2)}, u32[]{:S(2)}) collective-permute-start(f32[16,16,128]{2,1,0:T(8,128)S(1)} %get-tuple-element.37), channel_id=1, source_target_pairs={{0,1},{2,3},{4,5},{6,7},{8,9},{10,11},{12,13},{14,15},{16,17},{18,... | collective-permute-start | bytes 393224 | tf_op jit(solution)/shard_map/ppermute | solution.py:349
  133.9 10.7 %collective-permute-start.15 = (f32[16,16,128]{2,1,0:T(8,128)S(1)}, f32[16,16,128]{2,1,0:T(8,128)S(1)}, u32[]{:S(2)}, u32[]{:S(2)}) collective-permute-start(f32[16,16,128]{2,1,0:T(8,128)S(1)} %get-tuple-element.38), channel_id=1, source_target_pairs={{1,2},{3,4},{5,6},{7,8},{9,10},{11,12},{13,14},{15,16},{17,18},{19... | collective-permute-start | bytes 393224 | tf_op jit(solution)/shard_map/ppermute | solution.py:350

commit v2 on v1

v2 whole, which is shorter than its diff:
```python
import jax
import jax.numpy as jnp
from jax import lax
from jax.experimental import pallas as pl
from jax.experimental.pallas import tpu as pltpu
from jax.sharding import PartitionSpec as P

ITERS = 2
VIEWS = 6
TAPS = 33
R = 16
BZ = 16
BX = 16
NY = 128
SEND = 3
SRC = 96
PEERS = 64
EX = BX + 2 * R
EZ = BZ + 2 * R
SLOTS = VIEWS * BZ
CHUNK = SEND * BX + 1
VU = VIEWS * BX
PITCH = VU + 8
LINE = BX + 8
AT_ONCE = 4
F32 = jnp.float32
BF16 = jnp.bfloat16

VMEM = pl.BlockSpec(memory_space=pltpu.VMEM)
SMEM = pl.BlockSpec(memory_space=pltpu.SMEM)


def params(mib):
    return pltpu.CompilerParams(vmem_limit_bytes=mib * 1024 * 1024)


def shape(dims, dtype=F32):
    return jax.ShapeDtypeStruct(dims, dtype)


def split(value):
    high = value.astype(BF16)
    return high, (value - high.astype(F32)).astype(BF16)


def pack_kernel(named, planes, send, rows, count):
    for peer in range(PEERS):
        count[peer] = 0
    send[pl.ds(SEND * BX, PEERS, stride=CHUNK), :] = jnp.full((PEERS, NY), SLOTS, F32)
    for group in range(SRC // 8):
        for column in range(BX):
            rows[pl.ds(group * 8 * BX + column, 8, stride=BX), :] = planes[
                group * 8 : group * 8 + 8, column * NY : (column + 1) * NY
            ]
    lane = lax.broadcasted_iota(jnp.int32, (1, NY), 1)

    def place(plane, carry):
        peer = named[plane] >> 7
        rank = count[peer]
        count[peer] = rank + 1
        start = peer * CHUNK
        send[pl.ds(start + rank * BX, BX), :] = rows[pl.ds(pl.multiple_of(plane * BX, BX), BX), :]
        pltpu.store(
            send.at[pl.ds(start + SEND * BX, 1), :],
            jnp.full((1, NY), named[plane] & (NY - 1), jnp.int32).astype(F32),
            mask=lane == rank,
        )
        return carry

    lax.fori_loop(0, SRC, place, 0, unroll=8)


def pack(named, planes):
    return pl.pallas_call(
        pack_kernel,
        out_shape=shape((PEERS * CHUNK, NY)),
        in_specs=[SMEM, VMEM],
        out_specs=VMEM,
        scratch_shapes=[
            pltpu.VMEM((SRC * BX, NY), F32),
            pltpu.SMEM((PEERS,), jnp.int32),
        ],
        compiler_params=params(16),
        name="pack_planes",
    )(named, planes)


def bands(taps, first, place):
    row = lax.broadcasted_iota(jnp.int32, (BX, NY), 0)
    lane = place(lax.broadcasted_iota(jnp.int32, (BX, NY), 1))
    each = []
    for view in range(VIEWS):
        band = jnp.zeros((BX, NY), F32)
        for tap in range(TAPS):
            band = jnp.where(lane - row == tap, taps[first + view, tap], band)
        each.append(band)
    return jnp.concatenate(each + [jnp.zeros((NY - VU, NY), F32)], axis=0)


def by_terms(value):
    high, low = split(value)
    return jnp.concatenate([high, low, high], axis=1)


def views_of(ref):
    z_rows, x_rows = VIEWS * EZ, 3 * EX
    return (
        ref.at[pl.ds(0, z_rows), :],
        ref.at[pl.ds(z_rows, x_rows), :],
        ref.at[pl.ds(z_rows + x_rows, VIEWS * 3 * NY), :],
    )


def weight_kernel(index, taps, shift, z_fwd, x_fwd, y_fwd, back):
    z_back, x_back, y_back = views_of(back)
    band = bands(taps, 0, lambda lane: lane)
    turned = jnp.transpose(band)[:EZ]
    for view in range(VIEWS):
        z_fwd[view] = by_terms(band[view * BZ : (view + 1) * BZ, :EZ])
        z_back[pl.ds(view * EZ, EZ), : 3 * BZ] = by_terms(turned[:, view * BZ : (view + 1) * BZ])
    flip = jnp.where(index[0] % 2 == 0, 2 * BX, 0)
    band = bands(
        taps,
        VIEWS,
        lambda lane: jnp.where(
            lane < BX, lane + flip, jnp.where((lane >= 2 * BX) & (lane < EX), lane - flip, lane)
        ),
    )
    x_fwd[...] = by_terms(band[:VU, :EX])
    high, low = split(jnp.transpose(band)[:EX, :VU])
    for i, part in enumerate([high, low, high]):
        x_back[pl.ds(i * EX, EX), :VU] = part
    row = lax.broadcasted_iota(jnp.int32, (NY, NY), 0)
    lane = lax.broadcasted_iota(jnp.int32, (NY, NY), 1)

    def along_y(view, carry):
        offset = lane - row + R + shift[view]
        back = jnp.zeros((NY, NY), F32)
        for tap in range(TAPS):
            back = jnp.where(offset == tap, taps[2 * VIEWS + view, tap], back)
        high, low = split(back)
        y_back[pl.ds(pl.multiple_of(view * 3 * NY, NY), 3 * NY), :] = jnp.concatenate(
            [high, low, high], axis=0
        )
        high, low = split(jnp.transpose(back))
        y_fwd[view] = jnp.concatenate([high, low, high], axis=0)
        return carry

    lax.fori_loop(0, VIEWS, along_y, 0)


def weights(index, taps, shift):
    return pl.pallas_call(
        weight_kernel,
        out_shape=[
            shape((VIEWS, BZ, 3 * EZ), BF16),
            shape((VU, 3 * EX), BF16),
            shape((VIEWS, 3 * NY, NY), BF16),
            shape((VIEWS * EZ + 3 * EX + VIEWS * 3 * NY, NY), BF16),
        ],
        in_specs=[SMEM] * 3,
        out_specs=[VMEM] * 4,
        compiler_params=params(16),
        name="operator_matrices",
    )(index, taps, shift)


def dot(left, right):
    return jnp.dot(left, right, preferred_element_type=F32)


def terms(value):
    high, low = split(value)
    return jnp.concatenate([high, high, low], axis=0)


def along_x_fwd(matrix, pieces, starts, wide):
    matrix = matrix[...]
    for piece, start in zip(pieces, starts):
        for first in range(0, BZ, AT_ONCE):
            planes = range(first, first + AT_ONCE)
            product = dot(matrix, jnp.concatenate([terms(piece[p]) for p in planes], axis=1))
            for i, plane in enumerate(planes):
                rows = pl.ds(pl.multiple_of((start + plane) * PITCH, 8), VU)
                wide[rows, :] = product[:, i * NY : (i + 1) * NY]


def along_z_fwd(matrix, wide, narrow):
    def one(view, carry):
        for first in range(0, BX, AT_ONCE):
            columns = range(first, first + AT_ONCE)
            loaded = [wide[pl.ds(view * BX + c, EZ, stride=PITCH), :] for c in columns]
            product = dot(matrix[view], jnp.concatenate([terms(v) for v in loaded], axis=1))
            for i, column in enumerate(columns):
                rows = pl.ds(view * BZ * LINE + column, BZ, stride=LINE)
                narrow[rows, :] = product[:, i * NY : (i + 1) * NY]
        return carry

    lax.fori_loop(0, VIEWS, one, 0, unroll=True)


def rows_of(view):
    return pl.ds(view * BZ * BX, BZ * BX)


def planes_of(view):
    starts = [(view * BZ + plane) * LINE for plane in range(BZ)]
    return [pl.ds(start, BX) for start in starts]


def along_y(matrix, value):
    high, low = split(value)
    return dot(jnp.concatenate([high, high, low], axis=1), matrix)


def placed(core):
    inside = jnp.where(core == 0, 2 * R, 0)
    outside = jnp.where(core == 0, 0, 2 * R)
    return [R, inside, outside]


def forward_kernel(
    core, background, z_fwd, x_fwd, y_fwd, own, inside, outside, blur, wide, narrow
):
    along_x_fwd(x_fwd, [own, inside, outside], placed(core[0]), wide)
    along_z_fwd(z_fwd, wide, narrow)
    for view in range(VIEWS):
        value = jnp.concatenate([narrow[rows, :] for rows in planes_of(view)], axis=0)
        blur[rows_of(view), :] = along_y(y_fwd[view], value) + background[view]


def forward(core, background, z_fwd, x_fwd, y_fwd, own, inside, outside):
    return pl.pallas_call(
        forward_kernel,
        out_shape=shape((SLOTS * BX, NY)),
        in_specs=[SMEM] * 2 + [VMEM] * 6,
        out_specs=VMEM,
        scratch_shapes=[pltpu.VMEM((EZ * PITCH, NY), F32), pltpu.VMEM((SLOTS * LINE, NY), F32)],
        compiler_params=params(24),
        name="forward",
    )(core, background, z_fwd, x_fwd, y_fwd, own, inside, outside)


def along_z_back(matrix, narrow, wide):
    def one(view, carry):
        for first in range(0, BX, AT_ONCE):
            columns = range(first, first + AT_ONCE)
            loaded = [
                narrow[pl.ds(view * BZ * LINE + c, BZ, stride=LINE), :] for c in columns
            ]
            rows = pl.ds(pl.multiple_of(view * EZ, EZ), EZ)
            product = dot(
                matrix[rows, : 3 * BZ], jnp.concatenate([terms(v) for v in loaded], axis=1)
            )
            for i, column in enumerate(columns):
                wide[pl.ds(view * BX + column, EZ, stride=PITCH), :] = product[
                    :, i * NY : (i + 1) * NY
                ]
        return carry

    lax.fori_loop(0, VIEWS, one, 0, unroll=True)


def along_x_back(matrix, wide, pieces, starts):
    parts = [matrix[pl.ds(i * EX, EX), :VU] for i in range(3)]
    matrix = jnp.concatenate(parts, axis=1)
    for piece, start in zip(pieces, starts):
        for first in range(0, BZ, AT_ONCE):
            planes = range(first, first + AT_ONCE)
            loaded = [
                wide[pl.ds(pl.multiple_of((start + p) * PITCH, 8), VU), :] for p in planes
            ]
            product = dot(matrix, jnp.concatenate([terms(v) for v in loaded], axis=1))
            for i, plane in enumerate(planes):
                piece[plane] = product[:, i * NY : (i + 1) * NY]


def back_steps(core, where, back, got, blur, own, inside, outside, wide, narrow):
    z_back, x_back, y_back = views_of(back)
    for view in range(VIEWS):
        data = [got[pl.ds(where[view * BZ + plane], BX), :] for plane in range(BZ)]
        ratio = jnp.concatenate(data, axis=0) / blur[rows_of(view), :]
        value = along_y(y_back[pl.ds(view * 3 * NY, 3 * NY), :], ratio)
        for plane, rows in enumerate(planes_of(view)):
            narrow[rows, :] = value[plane * BX : (plane + 1) * BX]
    along_z_back(z_back, narrow, wide)
    along_x_back(x_back, wide, [own, inside, outside], placed(core[0]))


def first_back_kernel(
    core, back, got, blur, where, own, inside, outside,
    wide, narrow, names, slots, sem,
):
    named = got[pl.ds(SEND * BX, PEERS, stride=CHUNK), :].astype(jnp.int32)
    names[...] = jnp.transpose(jnp.concatenate([named, named], axis=0))[:8]
    copy = pltpu.make_async_copy(names, slots, sem)
    copy.start()
    copy.wait()
    for peer in range(PEERS):
        for rank in range(SEND):
            where[slots[rank, peer]] = peer * CHUNK + rank * BX
    back_steps(core, where, back, got, blur, own, inside, outside, wide, narrow)


def first_back(core, back, got, blur):
    return pl.pallas_call(
        first_back_kernel,
        out_shape=[shape((NY,), jnp.int32)] + [shape((BZ, EX, NY))] * 3,
        in_specs=[SMEM] + [VMEM] * 3,
        out_specs=[SMEM] + [VMEM] * 3,
        scratch_shapes=[
            pltpu.VMEM((EZ * PITCH, NY), F32),
            pltpu.VMEM((SLOTS * LINE, NY), F32),
            pltpu.VMEM((8, NY), jnp.int32),
            pltpu.SMEM((8, NY), jnp.int32),
            pltpu.SemaphoreType.DMA,
        ],
        compiler_params=params(24),
        name="first_back",
    )(core, back, got, blur)


def later_kernel(
    core, background, where, z_fwd, x_fwd, y_fwd, back,
    e_own, e_inside, e_outside, got, own, inside, outside, wide, narrow, blur,
):
    forward_kernel(
        core, background, z_fwd, x_fwd, y_fwd, e_own, e_inside, e_outside, blur, wide, narrow
    )
    back_steps(core, where, back, got, blur, own, inside, outside, wide, narrow)


def later(core, background, where, forth, back, pieces, got):
    return pl.pallas_call(
        later_kernel,
        out_shape=[shape((BZ, EX, NY))] * 3,
        in_specs=[SMEM] * 3 + [VMEM] * 8,
        out_specs=[VMEM] * 3,
        scratch_shapes=[
            pltpu.VMEM((EZ * PITCH, NY), F32),
            pltpu.VMEM((SLOTS * LINE, NY), F32),
            pltpu.VMEM((SLOTS * BX, NY), F32),
        ],
        compiler_params=params(24),
        name="forward_and_back",
    )(core, background, where, *forth, back, *pieces, got)


def swaps(first, count):
    pairs = [(i, i + 1) for i in range(first, count - 1, 2)]
    return pairs + [(j, i) for i, j in pairs]


def to_partners(to_even, to_odd):
    return lax.ppermute(to_even, "xy", swaps(0, PEERS)), lax.ppermute(to_odd, "xy", swaps(1, PEERS))


def past_partners(past_even, past_odd):
    right = [(i, i + 2) for i in range(PEERS - 2)]
    one = [p for p in right if p[0] % 2 == 0] + [(j, i) for i, j in right if i % 2 == 1]
    two = [(j, i) for i, j in one]
    return lax.ppermute(past_even, "xy", one), lax.ppermute(past_odd, "xy", two)


def above_and_below(block):
    count = lax.axis_size("gz")
    return lax.ppermute(block, "gz", swaps(0, count)), lax.ppermute(block, "gz", swaps(1, count))


def slab_sum(own, inside, outside):
    count = lax.axis_size("gz")
    return (
        own
        + lax.ppermute(outside, "gz", swaps(1, count))
        + lax.ppermute(inside, "gz", swaps(0, count))
    )


def three_sums(total):
    even, odd = to_partners(total[:, : 2 * BX], total[:, BX:])
    behind_odd, behind_even = past_partners(total[:, :BX], total[:, 2 * BX :])
    return jnp.concatenate(
        [
            total[:, :BX] + even[:, BX:] + behind_even,
            total[:, BX : 2 * BX] + even[:, :BX] + odd[:, BX:],
            total[:, 2 * BX :] + odd[:, :BX] + behind_odd,
        ],
        axis=1,
    )


def own_sum(total):
    even, odd = to_partners(total[:, :BX], total[:, 2 * BX :])
    return total[:, BX : 2 * BX] + even + odd


def local(
    tile_planes,
    plane_owner,
    plane_slot,
    view_shift,
    psf_z,
    psf_x,
    psf_y,
    background,
    initial_estimate,
):
    core = lax.rem(lax.axis_index("gz"), 2).astype(jnp.int32).reshape(1)
    index = lax.axis_index("xy").astype(jnp.int32).reshape(1)
    send = pack(plane_owner.reshape(SRC) * NY + plane_slot.reshape(SRC), tile_planes[0])
    even, odd = to_partners(initial_estimate, initial_estimate)
    send, even, odd = lax.optimization_barrier((send, even, odd))
    got = lax.all_to_all(
        send.reshape(PEERS, 1, CHUNK * NY), "xy", split_axis=0, concat_axis=0, tiled=True
    ).reshape(PEERS * CHUNK, NY)
    psf = jnp.concatenate([psf_z, psf_x, psf_y], axis=0)
    taps = psf / jnp.sum(psf, axis=1, keepdims=True)
    *forth, back = weights(index, taps, view_shift)
    bricks = jnp.concatenate([even, initial_estimate, odd], axis=1)
    for step in range(ITERS):
        pieces = (bricks, *above_and_below(bricks))
        if step == 0:
            blur = forward(core, background, *forth, *pieces)
            where, *parts = first_back(core, back, got, blur)
        else:
            parts = later(core, background, where, forth, back, pieces, got)
        total = slab_sum(*parts)
        if step + 1 < ITERS:
            bricks = bricks * (three_sums(total) / VIEWS)
    return bricks[:, BX : 2 * BX] * (own_sum(total) / VIEWS)


def solution(mesh):
    return jax.shard_map(
        local,
        mesh=mesh,
        in_specs=(
            P("gz", "xy", None),
            P("gz", "xy", None),
            P("gz", "xy"),
            P(),
            P(),
            P(),
            P(),
            P(),
            P("gz", "xy", None),
        ),
        out_specs=P("gz", "xy", None),
        check_vma=False,
    )
```

time: 146 us -> 138 us (0.945)
  Pallas kernels: 17.6 us -> 13.2 us
  waiting for transfers between devices: 51.2 us -> 47.3 us
  starting transfers between devices: 66.8 us -> 68.8 us
  local copies, waits for them, and re-layouts: 8.16 us -> 6.2 us
    ppermute x16, waiting for transfers between devices: 28.4 us -> 24.8 us  [the longest x2 7.31 us: slab_sum(): lax.ppermute(outside, 'gz', swaps(1, count))]
    pallas_call x1, Pallas kernels: 4.94 us -> 2.64 us  [first_back(): pl.pallas_call(first_back_kernel, out_shape=[shape((NY,), jnp.int32)] + [...]
    unnamed x36 -> x32, local copies, waits for them, and re-layouts: 8.16 us -> 6.11 us
    ppermute x16, starting transfers between devices: 56.6 us -> 58.3 us  [the longest x3 21.7 us: to_partners(): lax.ppermute(to_odd, 'xy', swaps(1, PEERS))]
  transfers between devices with their start and end apart: 17 -> 17, of which waited for: 11 -> 8; matrix products, arithmetic and copies ran while one was open for 0% -> 1% of each run, Pallas kernels for 5% -> 5%
where the time goes in v2:
time: 138 us
  starting transfers between devices  68.8 us (50%)
  waiting for transfers between devices  47.3 us (34%)
  Pallas kernels  13.2 us (10%)
  local copies, waits for them, and re-layouts  6.2 us (4%)
  other arithmetic  1.87 us (1%)
    all_to_all x1, waiting for transfers between devices, local(): lax.all_to_all(send.reshape(PEERS, 1, CHUNK * NY), 'xy', split_axis=0, co...  22.4 us
    ppermute x3, starting transfers between devices, to_partners(): lax.ppermute(to_odd, 'xy', swaps(1, PEERS))  21.7 us
    all_to_all x1, starting transfers between devices, local(): lax.all_to_all(send.reshape(PEERS, 1, CHUNK * NY), 'xy', split_axis=0, co...  10.5 us
    ppermute x3, starting transfers between devices, to_partners(): lax.ppermute(to_even, 'xy', swaps(0, PEERS))  8.11 us
    ppermute x2, waiting for transfers between devices, slab_sum(): lax.ppermute(outside, 'gz', swaps(1, count))  7.31 us
    ppermute x2, starting transfers between devices, above_and_below(): lax.ppermute(block, 'gz', swaps(0, count))  7.01 us
    ppermute x2, starting transfers between devices, slab_sum(): lax.ppermute(inside, 'gz', swaps(0, count))  7.01 us
    unnamed x32, local copies, waits for them, and re-layouts  6.11 us
  transfers between devices with their start and end apart: 17, of which 8 were waited for; matrix products, arithmetic and copies ran while one was open for 1% of the time, Pallas kernels for 5%

profile of v2, /device:TPU:34, one launch (start us, length us, event | category | flops | bytes accessed | tf_op | source)
XLA Modules:
  0.0 137.7 jit_solution(12215430448474235320)
XLA Ops:
  0.0 4.3 %collective-permute-start = (f32[16,16,128]{2,1,0:T(8,128)}, f32[16,16,128]{2,1,0:T(8,128)S(1)}, u32[]{:S(2)}, u32[]{:S(2)}) collective-permute-start(f32[16,16,128]{2,1,0:T(8,128)} %param.17), channel_id=1, source_target_pairs={{0,1},{2,3},{4,5},{6,7},{8,9},{10,11},{12,13},{14,15},{16,17},{18,... | collective-permute-start | bytes 393224 | tf_op jit(solution)/shard_map/ppermute | solution.py:355
  4.3 9.0 %collective-permute-start.1 = (f32[16,16,128]{2,1,0:T(8,128)}, f32[16,16,128]{2,1,0:T(8,128)S(1)}, u32[]{:S(2)}, u32[]{:S(2)}) collective-permute-start(f32[16,16,128]{2,1,0:T(8,128)} %param.17), channel_id=1, source_target_pairs={{1,2},{3,4},{5,6},{7,8},{9,10},{11,12},{13,14},{15,16},{17,18},{19... | collective-permute-start | bytes 393224 | tf_op jit(solution)/shard_map/ppermute | solution.py:355
  13.3 0.7 bitcast_add_fusion.named
  14.0 1.1 copy-done.2
  15.1 2.4 %pack_planes.1 = f32[3136,128]{1,0:T(8,128)} custom-call(s32[96]{0:T(128)S(1)} %bitcast_add_fusion.named, f32[96,2048]{1,0:T(8,128)S(1)} %bitcast.11), custom_call_target="tpu_custom_call" | custom-call | tf_op jit(solution)/shard_map/pack_planes/pallas_call | solution.py:74
  17.6 0.0 collective-permute-done
  17.6 0.0 collective-permute-done.1
  17.6 0.0 copy-start.12
  17.6 0.0 copy-start.13
  17.6 0.0 copy-start.14
  17.6 0.0 copy-start.10
  17.6 0.0 copy-start.9
  17.6 10.5 %all-to-all-start = ((f32[64,1,6272]{2,1,0:T(1,128)}), f32[64,1,6272]{2,1,0:T(1,128)S(1)}, u32[]{:S(2)}, u32[]{:S(2)}) async-start(f32[64,1,6272]{2,1,0:T(1,128)} %bitcast.5), calls=%async_computation | async-start | bytes 3211264 | tf_op jit(solution)/shard_map/all_to_all | solution.py:413
  28.2 0.0 copy-done.11
  28.2 1.9 %collective-permute-start.3 = (f32[16,48,128]{2,1,0:T(8,128)S(1)}, f32[16,48,128]{2,1,0:T(8,128)S(1)}, u32[]{:S(2)}, u32[]{:S(2)}) collective-permute-start(f32[16,48,128]{2,1,0:T(8,128)S(1)} %constant_dynamic-update-slice_fusion.own), channel_id=1, source_target_pairs={{64,128},{192,256},{320,384},{128,64},{256,192},{384,320},{65,129}... | collective-permute-start | bytes 1179656 | tf_op jit(solution)/shard_map/ppermute | solution.py:367
  30.2 3.5 %collective-permute-start.2 = (f32[16,48,128]{2,1,0:T(8,128)S(1)}, f32[16,48,128]{2,1,0:T(8,128)S(1)}, u32[]{:S(2)}, u32[]{:S(2)}) collective-permute-start(f32[16,48,128]{2,1,0:T(8,128)S(1)} %constant_dynamic-update-slice_fusion.own), channel_id=1, source_target_pairs={{0,64},{128,192},{256,320},{384,448},{64,0},{192,128},{320,256},{4... | collective-permute-start | bytes 1179656 | tf_op jit(solution)/shard_map/ppermute | solution.py:367
  33.7 0.1 fusion.7
  33.8 0.1 fusion.6.taps
  33.9 0.0 copy-done.10
  33.9 2.6 %operator_matrices.1 = (bf16[6,16,144]{2,1,0:T(8,128)(2,1)S(1)}, bf16[96,144]{1,0:T(8,128)(2,1)S(1)}, bf16[6,384,128]{2,1,0:T(8,128)(2,1)S(1)}, bf16[2736,128]{1,0:T(8,128)(2,1)S(1)}) custom-call(s32[1]{0:T(128)} %bitcast.4.index, f32[18,33]{1,0:T(8,128)S(1)} %fusion.6.taps, s32[6]{0:T(128)S(1)} %copy-done.10), custom_call_target="tpu_custom_call" | custom-call | tf_op jit(solution)/shard_map/operator_matrices/pallas_call | solution.py:153
  36.5 0.9 collective-permute-done.3.outside
  37.3 0.7 copy-done.3
  38.1 0.0 collective-permute-done.2.inside
  38.1 0.7 copy-done.5
  38.8 0.0 copy-done.9
  38.8 1.0 copy-done.4
  39.8 1.0 copy-done.6
  40.8 2.0 %forward.1.blur = f32[1536,128]{1,0:T(8,128)S(1)} custom-call(s32[1]{0:T(128)} %bitcast.3.core, f32[6]{0:T(128)S(1)} %copy-done.9, bf16[6,16,144]{2,1,0:T(8,128)(2,1)S(1)} %get-tuple-element.23.z_fwd, bf16[96,144]{1,0:T(8,128)(2,1)S(1)} %get-tuple-element.24.x_fwd, bf16[6,384,128]{2,1,0:T(8,128)(2,1)S(1)} %get-tuple-element.25.y_fwd, ...), custom_call_target="tpu_custom_call" | custom-call | tf_op jit(solution)/shard_map/forward/pallas_call | solution.py:233
  42.8 0.8 copy-done
  43.6 0.6 copy-done.7
  44.2 22.4 %all-to-all-done = f32[64,1,6272]{2,1,0:T(1,128)S(1)} async-done(((f32[64,1,6272]{2,1,0:T(1,128)}), f32[64,1,6272]{2,1,0:T(1,128)S(1)}, u32[]{:S(2)}, u32[]{:S(2)}) %all-to-all-start) | async-done | bytes 1605664 | tf_op jit(solution)/shard_map/all_to_all | solution.py:413
  66.7 2.6 %first_back.1 = (s32[128]{0:T(128)S(1)}, f32[16,48,128]{2,1,0:T(8,128)S(1)}, f32[16,48,128]{2,1,0:T(8,128)S(1)}, f32[16,48,128]{2,1,0:T(8,128)S(1)}) custom-call(s32[1]{0:T(128)} %bitcast.3.core, bf16[2736,128]{1,0:T(8,128)(2,1)S(1)} %get-tuple-element.21.back, f32[3136,128]{1,0:T(8,128)S(1)} %bitcast.9, f32[1536,128]{1,0:T(8,128)S(1)} %forward.1.blur), custom_call_target="tpu_custom_call" | custom-call | tf_op jit(solution)/shard_map/first_back/pallas_call | solution.py:306
  69.3 1.9 %collective-permute-start.4 = (f32[16,48,128]{2,1,0:T(8,128)S(1)}, f32[16,48,128]{2,1,0:T(8,128)S(1)}, u32[]{:S(2)}, u32[]{:S(2)}) collective-permute-start(f32[16,48,128]{2,1,0:T(8,128)S(1)} %get-tuple-element.27), channel_id=1, source_target_pairs={{64,128},{192,256},{320,384},{128,64},{256,192},{384,320},{65,129}... | collective-permute-start | bytes 1179656 | tf_op jit(solution)/shard_map/ppermute | solution.py:374
  71.2 3.5 %collective-permute-start.5 = (f32[16,48,128]{2,1,0:T(8,128)S(1)}, f32[16,48,128]{2,1,0:T(8,128)S(1)}, u32[]{:S(2)}, u32[]{:S(2)}) collective-permute-start(f32[16,48,128]{2,1,0:T(8,128)S(1)} %get-tuple-element.28), channel_id=1, source_target_pairs={{0,64},{128,192},{256,320},{384,448},{64,0},{192,128},{320,256},{4... | collective-permute-start | bytes 1179656 | tf_op jit(solution)/shard_map/ppermute | solution.py:375
  74.7 3.7 %collective-permute-done.4 = f32[16,48,128]{2,1,0:T(8,128)S(1)} collective-permute-done((f32[16,48,128]{2,1,0:T(8,128)S(1)}, f32[16,48,128]{2,1,0:T(8,128)S(1)}, u32[]{:S(2)}, u32[]{:S(2)}) %collective-permute-start.4) | collective-permute-done | bytes 393248 | tf_op jit(solution)/shard_map/ppermute | solution.py:374
  78.4 0.0 collective-permute-done.5
  78.4 0.1 add_add_fusion.1
  78.5 1.9 %collective-permute-start.6 = (f32[16,32,128]{2,1,0:T(8,128)S(1)}, f32[16,32,128]{2,1,0:T(8,128)S(1)}, u32[]{:S(2)}, u32[]{:S(2)}) collective-permute-start(f32[16,32,128]{2,1,0:T(8,128)S(1)} %get-tuple-element.40), channel_id=1, source_target_pairs={{0,1},{2,3},{4,5},{6,7},{8,9},{10,11},{12,13},{14,15},{16,17},{18,... | collective-permute-start | bytes 786440 | tf_op jit(solution)/shard_map/ppermute | solution.py:355
  80.5 0.0 copy-start.1
  80.5 0.0 copy-start.8
  80.5 7.2 %collective-permute-start.8 = (f32[16,32,128]{2,1,0:T(8,128)S(1)}, f32[16,32,128]{2,1,0:T(8,128)S(1)}, u32[]{:S(2)}, u32[]{:S(2)}) collective-permute-start(f32[16,32,128]{2,1,0:T(8,128)S(1)} %get-tuple-element.41), channel_id=1, source_target_pairs={{1,2},{3,4},{5,6},{7,8},{9,10},{11,12},{13,14},{15,16},{17,18},{19... | collective-permute-start | bytes 786440 | tf_op jit(solution)/shard_map/ppermute | solution.py:355
  87.8 3.4 %collective-permute-start.7 = (f32[16,16,128]{2,1,0:T(8,128)S(1)}, f32[16,16,128]{2,1,0:T(8,128)S(1)}, u32[]{:S(2)}, u32[]{:S(2)}) collective-permute-start(f32[16,16,128]{2,1,0:T(8,128)S(1)} %get-tuple-element.38), channel_id=1, source_target_pairs={{2,0},{4,2},{6,4},{8,6},{10,8},{12,10},{14,12},{16,14},{18,16},{20... | collective-permute-start | bytes 393224 | tf_op jit(solution)/shard_map/ppermute | solution.py:362
  91.2 3.4 %collective-permute-start.9 = (f32[16,16,128]{2,1,0:T(8,128)S(1)}, f32[16,16,128]{2,1,0:T(8,128)S(1)}, u32[]{:S(2)}, u32[]{:S(2)}) collective-permute-start(f32[16,16,128]{2,1,0:T(8,128)S(1)} %get-tuple-element.39), channel_id=1, source_target_pairs={{0,2},{2,4},{4,6},{6,8},{8,10},{10,12},{12,14},{14,16},{16,18},{18... | collective-permute-start | bytes 393224 | tf_op jit(solution)/shard_map/ppermute | solution.py:362
  94.5 4.5 %collective-permute-done.7 = f32[16,16,128]{2,1,0:T(8,128)S(1)} collective-permute-done((f32[16,16,128]{2,1,0:T(8,128)S(1)}, f32[16,16,128]{2,1,0:T(8,128)S(1)}, u32[]{:S(2)}, u32[]{:S(2)}) %collective-permute-start.7) | collective-permute-done | bytes 131104 | tf_op jit(solution)/shard_map/ppermute | solution.py:362
  99.0 3.2 %collective-permute-done.9 = f32[16,16,128]{2,1,0:T(8,128)S(1)} collective-permute-done((f32[16,16,128]{2,1,0:T(8,128)S(1)}, f32[16,16,128]{2,1,0:T(8,128)S(1)}, u32[]{:S(2)}, u32[]{:S(2)}) %collective-permute-start.9) | collective-permute-done | bytes 131104 | tf_op jit(solution)/shard_map/ppermute | solution.py:362
  102.2 0.0 collective-permute-done.6
  102.2 0.0 collective-permute-done.8
  102.2 0.1 fusion.5
  102.3 0.1 fusion.e_own
  102.4 1.9 %collective-permute-start.11 = (f32[16,48,128]{2,1,0:T(8,128)S(1)}, f32[16,48,128]{2,1,0:T(8,128)S(1)}, u32[]{:S(2)}, u32[]{:S(2)}) collective-permute-start(f32[16,48,128]{2,1,0:T(8,128)S(1)} %fusion.e_own), channel_id=1, source_target_pairs={{64,128},{192,256},{320,384},{128,64},{256,192},{384,320},{65,129}... | collective-permute-start | bytes 1179656 | tf_op jit(solution)/shard_map/ppermute | solution.py:367
  104.3 3.5 %collective-permute-start.10 = (f32[16,48,128]{2,1,0:T(8,128)S(1)}, f32[16,48,128]{2,1,0:T(8,128)S(1)}, u32[]{:S(2)}, u32[]{:S(2)}) collective-permute-start(f32[16,48,128]{2,1,0:T(8,128)S(1)} %fusion.e_own), channel_id=1, source_target_pairs={{0,64},{128,192},{256,320},{384,448},{64,0},{192,128},{320,256},{4... | collective-permute-start | bytes 1179656 | tf_op jit(solution)/shard_map/ppermute | solution.py:367
  107.8 3.6 %collective-permute-done.11.e_outside = f32[16,48,128]{2,1,0:T(8,128)S(1)} collective-permute-done((f32[16,48,128]{2,1,0:T(8,128)S(1)}, f32[16,48,128]{2,1,0:T(8,128)S(1)}, u32[]{:S(2)}, u32[]{:S(2)}) %collective-permute-start.11) | collective-permute-done | bytes 393248 | tf_op jit(solution)/shard_map/ppermute | solution.py:367
  111.5 0.0 collective-permute-done.10.e_inside
  111.5 3.6 %forward_and_back.1 = (f32[16,48,128]{2,1,0:T(8,128)S(1)}, f32[16,48,128]{2,1,0:T(8,128)S(1)}, f32[16,48,128]{2,1,0:T(8,128)S(1)}) custom-call(s32[1]{0:T(128)} %bitcast.3.core, f32[6]{0:T(128)S(1)} %copy-done.9, s32[128]{0:T(128)S(1)} %get-tuple-element.29.where, bf16[6,16,144]{2,1,0:T(8,128)(2,1)S(1)} %get-tuple-element.23.z_fwd, ...), custom_call_target="tpu_custom_call" | custom-call | tf_op jit(solution)/shard_map/forward_and_back/pallas_call | solution.py:334
  115.1 1.9 %collective-permute-start.12 = (f32[16,48,128]{2,1,0:T(8,128)S(1)}, f32[16,48,128]{2,1,0:T(8,128)S(1)}, u32[]{:S(2)}, u32[]{:S(2)}) collective-permute-start(f32[16,48,128]{2,1,0:T(8,128)S(1)} %get-tuple-element.31), channel_id=1, source_target_pairs={{64,128},{192,256},{320,384},{128,64},{256,192},{384,320},{65,129}... | collective-permute-start | bytes 1179656 | tf_op jit(solution)/shard_map/ppermute | solution.py:374
  117.0 3.5 %collective-permute-start.13 = (f32[16,48,128]{2,1,0:T(8,128)S(1)}, f32[16,48,128]{2,1,0:T(8,128)S(1)}, u32[]{:S(2)}, u32[]{:S(2)}) collective-permute-start(f32[16,48,128]{2,1,0:T(8,128)S(1)} %get-tuple-element.32), channel_id=1, source_target_pairs={{0,64},{128,192},{256,320},{384,448},{64,0},{192,128},{320,256},{4... | collective-permute-start | bytes 1179656 | tf_op jit(solution)/shard_map/ppermute | solution.py:375
  120.5 3.7 %collective-permute-done.12 = f32[16,48,128]{2,1,0:T(8,128)S(1)} collective-permute-done((f32[16,48,128]{2,1,0:T(8,128)S(1)}, f32[16,48,128]{2,1,0:T(8,128)S(1)}, u32[]{:S(2)}, u32[]{:S(2)}) %collective-permute-start.12) | collective-permute-done | bytes 393248 | tf_op jit(solution)/shard_map/ppermute | solution.py:374
  124.2 0.0 collective-permute-done.13
  124.2 0.1 add_add_fusion
  124.3 1.9 %collective-permute-start.14 = (f32[16,16,128]{2,1,0:T(8,128)S(1)}, f32[16,16,128]{2,1,0:T(8,128)S(1)}, u32[]{:S(2)}, u32[]{:S(2)}) collective-permute-start(f32[16,16,128]{2,1,0:T(8,128)S(1)} %get-tuple-element.36), channel_id=1, source_target_pairs={{0,1},{2,3},{4,5},{6,7},{8,9},{10,11},{12,13},{14,15},{16,17},{18,... | collective-permute-start | bytes 393224 | tf_op jit(solution)/shard_map/ppermute | solution.py:355
  126.2 5.5 %collective-permute-start.15 = (f32[16,16,128]{2,1,0:T(8,128)S(1)}, f32[16,16,128]{2,1,0:T(8,128)S(1)}, u32[]{:S(2)}, u32[]{:S(2)}) collective-permute-start(f32[16,16,128]{2,1,0:T(8,128)S(1)} %get-tuple-element.37), channel_id=1, source_target_pairs={{1,2},{3,4},{5,6},{7,8},{9,10},{11,12},{13,14},{15,16},{17,18},{19... | collective-permute-start | bytes 393224 | tf_op jit(solution)/shard_map/ppermute | solution.py:355
  131.7 0.0 collective-permute-done.14
  131.7 5.2 %collective-permute-done.15 = f32[16,16,128]{2,1,0:T(8,128)S(1)} collective-permute-done((f32[16,16,128]{2,1,0:T(8,128)S(1)}, f32[16,16,128]{2,1,0:T(8,128)S(1)}, u32[]{:S(2)}, u32[]{:S(2)}) %collective-permute-start.15) | collective-permute-done | bytes 131104 | tf_op jit(solution)/shard_map/ppermute | solution.py:355
  137.0 0.7 fusion.3
  (19 shorter events, 0.1 us)
Async XLA Ops:
  0.0 17.6 %collective-permute-start = (f32[16,16,128]{2,1,0:T(8,128)}, f32[16,16,128]{2,1,0:T(8,128)S(1)}, u32[]{:S(2)}, u32[]{:S(2)}) collective-permute-start(f32[16,16,128]{2,1,0:T(8,128)} %param.17), channel_id=1, source_target_pairs={{0,1},{2,3},{4,5},{6,7},{8,9},{10,11},{12,13},{14,15},{16,17},{18,... | collective-permute-start | bytes 393224 | tf_op jit(solution)/shard_map/ppermute | solution.py:355
  4.3 13.3 %collective-permute-start.1 = (f32[16,16,128]{2,1,0:T(8,128)}, f32[16,16,128]{2,1,0:T(8,128)S(1)}, u32[]{:S(2)}, u32[]{:S(2)}) collective-permute-start(f32[16,16,128]{2,1,0:T(8,128)} %param.17), channel_id=1, source_target_pairs={{1,2},{3,4},{5,6},{7,8},{9,10},{11,12},{13,14},{15,16},{17,18},{19... | collective-permute-start | bytes 393224 | tf_op jit(solution)/shard_map/ppermute | solution.py:355
  14.0 1.1 copy-start.2
  17.6 10.6 %copy-start.11 = (f32[16,16,128]{2,1,0:T(8,128)S(1)}, f32[16,16,128]{2,1,0:T(8,128)}, u32[]{:S(2)}) copy-start(f32[16,16,128]{2,1,0:T(8,128)} %param.17) | copy-start | bytes 393220
  17.6 16.1 %copy-start.12 = (f32[6,33]{1,0:T(8,128)S(1)}, f32[6,33]{1,0:T(8,128)}, u32[]{:S(2)}) copy-start(f32[6,33]{1,0:T(8,128)} %param.15) | copy-start | bytes 2380
  17.6 16.1 %copy-start.13 = (f32[6,33]{1,0:T(8,128)S(1)}, f32[6,33]{1,0:T(8,128)}, u32[]{:S(2)}) copy-start(f32[6,33]{1,0:T(8,128)} %param.14) | copy-start | bytes 2380
  17.6 16.1 %copy-start.14 = (f32[6,33]{1,0:T(8,128)S(1)}, f32[6,33]{1,0:T(8,128)}, u32[]{:S(2)}) copy-start(f32[6,33]{1,0:T(8,128)} %param.13) | copy-start | bytes 2380
  17.6 16.3 %copy-start.10 = (s32[6]{0:T(128)S(1)}, s32[6]{0:T(128)}, u32[]{:S(2)}) copy-start(s32[6]{0:T(128)} %shift.1) | copy-start | bytes 76
  17.6 21.2 %copy-start.9 = (f32[6]{0:T(128)S(1)}, f32[6]{0:T(128)}, u32[]{:S(2)}) copy-start(f32[6]{0:T(128)} %background.3) | copy-start | bytes 76
  17.6 49.0 %all-to-all-start = ((f32[64,1,6272]{2,1,0:T(1,128)}), f32[64,1,6272]{2,1,0:T(1,128)S(1)}, u32[]{:S(2)}, u32[]{:S(2)}) async-start(f32[64,1,6272]{2,1,0:T(1,128)} %bitcast.5), calls=%async_computation | async-start | bytes 3211264 | tf_op jit(solution)/shard_map/all_to_all | solution.py:413
  28.2 9.1 %collective-permute-start.3 = (f32[16,48,128]{2,1,0:T(8,128)S(1)}, f32[16,48,128]{2,1,0:T(8,128)S(1)}, u32[]{:S(2)}, u32[]{:S(2)}) collective-permute-start(f32[16,48,128]{2,1,0:T(8,128)S(1)} %constant_dynamic-update-slice_fusion.own), channel_id=1, source_target_pairs={{64,128},{192,256},{320,384},{128,64},{256,192},{384,320},{65,129}... | collective-permute-start | bytes 1179656 | tf_op jit(solution)/shard_map/ppermute | solution.py:367
  30.2 7.9 %collective-permute-start.2 = (f32[16,48,128]{2,1,0:T(8,128)S(1)}, f32[16,48,128]{2,1,0:T(8,128)S(1)}, u32[]{:S(2)}, u32[]{:S(2)}) collective-permute-start(f32[16,48,128]{2,1,0:T(8,128)S(1)} %constant_dynamic-update-slice_fusion.own), channel_id=1, source_target_pairs={{0,64},{128,192},{256,320},{384,448},{64,0},{192,128},{320,256},{4... | collective-permute-start | bytes 1179656 | tf_op jit(solution)/shard_map/ppermute | solution.py:367
  37.3 0.7 copy-start.3
  38.1 0.7 copy-start.5
  38.8 1.0 copy-start.4
  39.8 1.0 copy-start.6
  42.8 0.8 copy-start
  43.6 0.6 copy-start.7
  69.3 9.1 %collective-permute-start.4 = (f32[16,48,128]{2,1,0:T(8,128)S(1)}, f32[16,48,128]{2,1,0:T(8,128)S(1)}, u32[]{:S(2)}, u32[]{:S(2)}) collective-permute-start(f32[16,48,128]{2,1,0:T(8,128)S(1)} %get-tuple-element.27), channel_id=1, source_target_pairs={{64,128},{192,256},{320,384},{128,64},{256,192},{384,320},{65,129}... | collective-permute-start | bytes 1179656 | tf_op jit(solution)/shard_map/ppermute | solution.py:374
  71.2 7.2 %collective-permute-start.5 = (f32[16,48,128]{2,1,0:T(8,128)S(1)}, f32[16,48,128]{2,1,0:T(8,128)S(1)}, u32[]{:S(2)}, u32[]{:S(2)}) collective-permute-start(f32[16,48,128]{2,1,0:T(8,128)S(1)} %get-tuple-element.28), channel_id=1, source_target_pairs={{0,64},{128,192},{256,320},{384,448},{64,0},{192,128},{320,256},{4... | collective-permute-start | bytes 1179656 | tf_op jit(solution)/shard_map/ppermute | solution.py:375
  78.5 23.7 %collective-permute-start.6 = (f32[16,32,128]{2,1,0:T(8,128)S(1)}, f32[16,32,128]{2,1,0:T(8,128)S(1)}, u32[]{:S(2)}, u32[]{:S(2)}) collective-permute-start(f32[16,32,128]{2,1,0:T(8,128)S(1)} %get-tuple-element.40), channel_id=1, source_target_pairs={{0,1},{2,3},{4,5},{6,7},{8,9},{10,11},{12,13},{14,15},{16,17},{18,... | collective-permute-start | bytes 786440 | tf_op jit(solution)/shard_map/ppermute | solution.py:355
  80.5 31.0 %copy-start.1 = (bf16[6,384,128]{2,1,0:T(8,128)(2,1)S(1)}, bf16[6,384,128]{2,1,0:T(8,128)(2,1)}, u32[]{:S(2)}) copy-start(bf16[6,384,128]{2,1,0:T(8,128)(2,1)} %copy-done) | copy-start | bytes 1769476
  80.5 31.0 %copy-start.8 = (bf16[96,144]{1,0:T(8,128)(2,1)S(1)}, bf16[96,144]{1,0:T(8,128)(2,1)}, u32[]{:S(2)}) copy-start(bf16[96,144]{1,0:T(8,128)(2,1)} %copy-done.7) | copy-start | bytes 82948
  80.5 21.7 %collective-permute-start.8 = (f32[16,32,128]{2,1,0:T(8,128)S(1)}, f32[16,32,128]{2,1,0:T(8,128)S(1)}, u32[]{:S(2)}, u32[]{:S(2)}) collective-permute-start(f32[16,32,128]{2,1,0:T(8,128)S(1)} %get-tuple-element.41), channel_id=1, source_target_pairs={{1,2},{3,4},{5,6},{7,8},{9,10},{11,12},{13,14},{15,16},{17,18},{19... | collective-permute-start | bytes 786440 | tf_op jit(solution)/shard_map/ppermute | solution.py:355
  87.8 11.3 %collective-permute-start.7 = (f32[16,16,128]{2,1,0:T(8,128)S(1)}, f32[16,16,128]{2,1,0:T(8,128)S(1)}, u32[]{:S(2)}, u32[]{:S(2)}) collective-permute-start(f32[16,16,128]{2,1,0:T(8,128)S(1)} %get-tuple-element.38), channel_id=1, source_target_pairs={{2,0},{4,2},{6,4},{8,6},{10,8},{12,10},{14,12},{16,14},{18,16},{20... | collective-permute-start | bytes 393224 | tf_op jit(solution)/shard_map/ppermute | solution.py:362
  91.2 11.1 %collective-permute-start.9 = (f32[16,16,128]{2,1,0:T(8,128)S(1)}, f32[16,16,128]{2,1,0:T(8,128)S(1)}, u32[]{:S(2)}, u32[]{:S(2)}) collective-permute-start(f32[16,16,128]{2,1,0:T(8,128)S(1)} %get-tuple-element.39), channel_id=1, source_target_pairs={{0,2},{2,4},{4,6},{6,8},{8,10},{10,12},{12,14},{14,16},{16,18},{18... | collective-permute-start | bytes 393224 | tf_op jit(solution)/shard_map/ppermute | solution.py:362
  102.4 9.1 %collective-permute-start.11 = (f32[16,48,128]{2,1,0:T(8,128)S(1)}, f32[16,48,128]{2,1,0:T(8,128)S(1)}, u32[]{:S(2)}, u32[]{:S(2)}) collective-permute-start(f32[16,48,128]{2,1,0:T(8,128)S(1)} %fusion.e_own), channel_id=1, source_target_pairs={{64,128},{192,256},{320,384},{128,64},{256,192},{384,320},{65,129}... | collective-permute-start | bytes 1179656 | tf_op jit(solution)/shard_map/ppermute | solution.py:367
  104.3 7.2 %collective-permute-start.10 = (f32[16,48,128]{2,1,0:T(8,128)S(1)}, f32[16,48,128]{2,1,0:T(8,128)S(1)}, u32[]{:S(2)}, u32[]{:S(2)}) collective-permute-start(f32[16,48,128]{2,1,0:T(8,128)S(1)} %fusion.e_own), channel_id=1, source_target_pairs={{0,64},{128,192},{256,320},{384,448},{64,0},{192,128},{320,256},{4... | collective-permute-start | bytes 1179656 | tf_op jit(solution)/shard_map/ppermute | solution.py:367
  115.1 9.1 %collective-permute-start.12 = (f32[16,48,128]{2,1,0:T(8,128)S(1)}, f32[16,48,128]{2,1,0:T(8,128)S(1)}, u32[]{:S(2)}, u32[]{:S(2)}) collective-permute-start(f32[16,48,128]{2,1,0:T(8,128)S(1)} %get-tuple-element.31), channel_id=1, source_target_pairs={{64,128},{192,256},{320,384},{128,64},{256,192},{384,320},{65,129}... | collective-permute-start | bytes 1179656 | tf_op jit(solution)/shard_map/ppermute | solution.py:374
  117.0 7.2 %collective-permute-start.13 = (f32[16,48,128]{2,1,0:T(8,128)S(1)}, f32[16,48,128]{2,1,0:T(8,128)S(1)}, u32[]{:S(2)}, u32[]{:S(2)}) collective-permute-start(f32[16,48,128]{2,1,0:T(8,128)S(1)} %get-tuple-element.32), channel_id=1, source_target_pairs={{0,64},{128,192},{256,320},{384,448},{64,0},{192,128},{320,256},{4... | collective-permute-start | bytes 1179656 | tf_op jit(solution)/shard_map/ppermute | solution.py:375
  124.3 7.4 %collective-permute-start.14 = (f32[16,16,128]{2,1,0:T(8,128)S(1)}, f32[16,16,128]{2,1,0:T(8,128)S(1)}, u32[]{:S(2)}, u32[]{:S(2)}) collective-permute-start(f32[16,16,128]{2,1,0:T(8,128)S(1)} %get-tuple-element.36), channel_id=1, source_target_pairs={{0,1},{2,3},{4,5},{6,7},{8,9},{10,11},{12,13},{14,15},{16,17},{18,... | collective-permute-start | bytes 393224 | tf_op jit(solution)/shard_map/ppermute | solution.py:355
  126.2 10.7 %collective-permute-start.15 = (f32[16,16,128]{2,1,0:T(8,128)S(1)}, f32[16,16,128]{2,1,0:T(8,128)S(1)}, u32[]{:S(2)}, u32[]{:S(2)}) collective-permute-start(f32[16,16,128]{2,1,0:T(8,128)S(1)} %get-tuple-element.37), channel_id=1, source_target_pairs={{1,2},{3,4},{5,6},{7,8},{9,10},{11,12},{13,14},{15,16},{17,18},{19... | collective-permute-start | bytes 393224 | tf_op jit(solution)/shard_map/ppermute | solution.py:355

commit v3 on v2

--- a/solution.py
+++ b/solution.py
@@ -49,7 +49,7 @@
     send[pl.ds(SEND * BX, PEERS, stride=CHUNK), :] = jnp.full((PEERS, NY), SLOTS, F32)
     for group in range(SRC // 8):
         for column in range(BX):
-            rows[pl.ds(group * 8 * BX + column, 8, stride=BX), :] = planes[
+            rows[pl.ds(group * 8 * LINE + column, 8, stride=LINE), :] = planes[
                 group * 8 : group * 8 + 8, column * NY : (column + 1) * NY
             ]
     lane = lax.broadcasted_iota(jnp.int32, (1, NY), 1)
@@ -59,7 +59,7 @@
         rank = count[peer]
         count[peer] = rank + 1
         start = peer * CHUNK
-        send[pl.ds(start + rank * BX, BX), :] = rows[pl.ds(pl.multiple_of(plane * BX, BX), BX), :]
+        send[pl.ds(start + rank * BX, BX), :] = rows[pl.ds(pl.multiple_of(plane * LINE, 8), BX), :]
         pltpu.store(
             send.at[pl.ds(start + SEND * BX, 1), :],
             jnp.full((1, NY), named[plane] & (NY - 1), jnp.int32).astype(F32),
@@ -77,7 +77,7 @@
         in_specs=[SMEM, VMEM],
         out_specs=VMEM,
         scratch_shapes=[
-            pltpu.VMEM((SRC * BX, NY), F32),
+            pltpu.VMEM((SRC * LINE, NY), F32),
             pltpu.SMEM((PEERS,), jnp.int32),
         ],
         compiler_params=params(16),
@@ -103,7 +103,7 @@
 
 
 def views_of(ref):
-    z_rows, x_rows = VIEWS * EZ, 3 * EX
+    z_rows, x_rows = VIEWS * EZ, 2 * EX
     return (
         ref.at[pl.ds(0, z_rows), :],
         ref.at[pl.ds(z_rows, x_rows), :],
@@ -116,7 +116,7 @@
     band = bands(taps, 0, lambda lane: lane)
     turned = jnp.transpose(band)[:EZ]
     for view in range(VIEWS):
-        z_fwd[view] = by_terms(band[view * BZ : (view + 1) * BZ, :EZ])
+        z_fwd[view] = by_rows(band[view * BZ : (view + 1) * BZ, :EZ])
         z_back[pl.ds(view * EZ, EZ), : 3 * BZ] = by_terms(turned[:, view * BZ : (view + 1) * BZ])
     flip = jnp.where(index[0] % 2 == 0, 2 * BX, 0)
     band = bands(
@@ -128,7 +128,7 @@
     )
     x_fwd[...] = by_terms(band[:VU, :EX])
     high, low = split(jnp.transpose(band)[:EX, :VU])
-    for i, part in enumerate([high, low, high]):
+    for i, part in enumerate([high, low]):
         x_back[pl.ds(i * EX, EX), :VU] = part
     row = lax.broadcasted_iota(jnp.int32, (NY, NY), 0)
     lane = lax.broadcasted_iota(jnp.int32, (NY, NY), 1)
@@ -153,10 +153,10 @@
     return pl.pallas_call(
         weight_kernel,
         out_shape=[
-            shape((VIEWS, BZ, 3 * EZ), BF16),
+            shape((VIEWS, 2 * BZ, 2 * EZ), BF16),
             shape((VU, 3 * EX), BF16),
             shape((VIEWS, 3 * NY, NY), BF16),
-            shape((VIEWS * EZ + 3 * EX + VIEWS * 3 * NY, NY), BF16),
+            shape((VIEWS * EZ + 2 * EX + VIEWS * 3 * NY, NY), BF16),
         ],
         in_specs=[SMEM] * 3,
         out_specs=[VMEM] * 4,
@@ -167,6 +167,19 @@
 
 def dot(left, right):
     return jnp.dot(left, right, preferred_element_type=F32)
+
+
+def by_rows(value):
+    high, low = split(value)
+    upper = jnp.concatenate([high, high], axis=1)
+    return jnp.concatenate([upper, jnp.concatenate([low, jnp.zeros_like(low)], axis=1)], axis=0)
+
+
+def dot_by_rows(matrix, values):
+    pairs = [jnp.concatenate(split(value), axis=0) for value in values]
+    product = dot(matrix, jnp.concatenate(pairs, axis=1))
+    half = product.shape[0] // 2
+    return product[:half] + product[half:]
 
 
 def terms(value):
@@ -190,7 +203,7 @@
         for first in range(0, BX, AT_ONCE):
             columns = range(first, first + AT_ONCE)
             loaded = [wide[pl.ds(view * BX + c, EZ, stride=PITCH), :] for c in columns]
-            product = dot(matrix[view], jnp.concatenate([terms(v) for v in loaded], axis=1))
+            product = dot_by_rows(matrix[view], loaded)
             for i, column in enumerate(columns):
                 rows = pl.ds(view * BZ * LINE + column, BZ, stride=LINE)
                 narrow[rows, :] = product[:, i * NY : (i + 1) * NY]
@@ -213,32 +226,33 @@
     return dot(jnp.concatenate([high, high, low], axis=1), matrix)
 
 
-def placed(core):
+def placed():
+    core = lax.rem(lax.axis_index("gz"), 2)
     inside = jnp.where(core == 0, 2 * R, 0)
     outside = jnp.where(core == 0, 0, 2 * R)
     return [R, inside, outside]
 
 
 def forward_kernel(
-    core, background, z_fwd, x_fwd, y_fwd, own, inside, outside, blur, wide, narrow
+    background, z_fwd, x_fwd, y_fwd, own, inside, outside, blur, wide, narrow
 ):
-    along_x_fwd(x_fwd, [own, inside, outside], placed(core[0]), wide)
+    along_x_fwd(x_fwd, [own, inside, outside], placed(), wide)
     along_z_fwd(z_fwd, wide, narrow)
     for view in range(VIEWS):
         value = jnp.concatenate([narrow[rows, :] for rows in planes_of(view)], axis=0)
-        blur[rows_of(view), :] = along_y(y_fwd[view], value) + background[view]
-
-
-def forward(core, background, z_fwd, x_fwd, y_fwd, own, inside, outside):
+        blur[rows_of(view), :] = along_y(y_fwd[view], value) + background[view : view + 1, :]
+
+
+def forward(background, z_fwd, x_fwd, y_fwd, own, inside, outside):
     return pl.pallas_call(
         forward_kernel,
         out_shape=shape((SLOTS * BX, NY)),
-        in_specs=[SMEM] * 2 + [VMEM] * 6,
+        in_specs=[VMEM] * 7,
         out_specs=VMEM,
         scratch_shapes=[pltpu.VMEM((EZ * PITCH, NY), F32), pltpu.VMEM((SLOTS * LINE, NY), F32)],
         compiler_params=params(24),
         name="forward",
-    )(core, background, z_fwd, x_fwd, y_fwd, own, inside, outside)
+    )(background, z_fwd, x_fwd, y_fwd, own, inside, outside)
 
 
 def along_z_back(matrix, narrow, wide):
@@ -262,20 +276,22 @@
 
 
 def along_x_back(matrix, wide, pieces, starts):
-    parts = [matrix[pl.ds(i * EX, EX), :VU] for i in range(3)]
-    matrix = jnp.concatenate(parts, axis=1)
+    high, low = [matrix[pl.ds(i * EX, EX), :VU] for i in range(2)]
+    upper = jnp.concatenate([high, high], axis=1)
+    lower = jnp.concatenate([low, jnp.zeros_like(low)], axis=1)
+    matrix = jnp.concatenate([upper, lower], axis=0)
     for piece, start in zip(pieces, starts):
         for first in range(0, BZ, AT_ONCE):
             planes = range(first, first + AT_ONCE)
             loaded = [
                 wide[pl.ds(pl.multiple_of((start + p) * PITCH, 8), VU), :] for p in planes
             ]
-            product = dot(matrix, jnp.concatenate([terms(v) for v in loaded], axis=1))
+            product = dot_by_rows(matrix, loaded)
             for i, plane in enumerate(planes):
                 piece[plane] = product[:, i * NY : (i + 1) * NY]
 
 
-def back_steps(core, where, back, got, blur, own, inside, outside, wide, narrow):
+def back_steps(where, back, got, blur, own, inside, outside, wide, narrow):
     z_back, x_back, y_back = views_of(back)
     for view in range(VIEWS):
         data = [got[pl.ds(where[view * BZ + plane], BX), :] for plane in range(BZ)]
@@ -284,66 +300,77 @@
         for plane, rows in enumerate(planes_of(view)):
             narrow[rows, :] = value[plane * BX : (plane + 1) * BX]
     along_z_back(z_back, narrow, wide)
-    along_x_back(x_back, wide, [own, inside, outside], placed(core[0]))
-
-
-def first_back_kernel(
-    core, back, got, blur, where, own, inside, outside,
-    wide, narrow, names, slots, sem,
-):
+    along_x_back(x_back, wide, [own, inside, outside], placed())
+
+
+def slot_copy(got, names, slots, sem):
     named = got[pl.ds(SEND * BX, PEERS, stride=CHUNK), :].astype(jnp.int32)
     names[...] = jnp.transpose(jnp.concatenate([named, named], axis=0))[:8]
-    copy = pltpu.make_async_copy(names, slots, sem)
-    copy.start()
-    copy.wait()
+    return pltpu.make_async_copy(names, slots, sem)
+
+
+def fill_table(slots, where):
     for peer in range(PEERS):
         for rank in range(SEND):
             where[slots[rank, peer]] = peer * CHUNK + rank * BX
-    back_steps(core, where, back, got, blur, own, inside, outside, wide, narrow)
-
-
-def first_back(core, back, got, blur):
+
+
+SCRATCH = [
+    pltpu.VMEM((EZ * PITCH, NY), F32),
+    pltpu.VMEM((SLOTS * LINE, NY), F32),
+    pltpu.VMEM((8, NY), jnp.int32),
+    pltpu.SMEM((8, NY), jnp.int32),
+    pltpu.SMEM((NY,), jnp.int32),
+    pltpu.SemaphoreType.DMA,
+]
+
+
+def first_back_kernel(
+    back, got, blur, own, inside, outside, wide, narrow, names, slots, where, sem
+):
+    copy = slot_copy(got, names, slots, sem)
+    copy.start()
+    copy.wait()
+    fill_table(slots, where)
+    back_steps(where, back, got, blur, own, inside, outside, wide, narrow)
+
+
+def first_back(back, got, blur):
     return pl.pallas_call(
         first_back_kernel,
-        out_shape=[shape((NY,), jnp.int32)] + [shape((BZ, EX, NY))] * 3,
-        in_specs=[SMEM] + [VMEM] * 3,
-        out_specs=[SMEM] + [VMEM] * 3,
-        scratch_shapes=[
-            pltpu.VMEM((EZ * PITCH, NY), F32),
-            pltpu.VMEM((SLOTS * LINE, NY), F32),
-            pltpu.VMEM((8, NY), jnp.int32),
-            pltpu.SMEM((8, NY), jnp.int32),
-            pltpu.SemaphoreType.DMA,
-        ],
+        out_shape=[shape((BZ, EX, NY))] * 3,
+        in_specs=[VMEM] * 3,
+        out_specs=[VMEM] * 3,
+        scratch_shapes=SCRATCH,
         compiler_params=params(24),
         name="first_back",
-    )(core, back, got, blur)
+    )(back, got, blur)
 
 
 def later_kernel(
-    core, background, where, z_fwd, x_fwd, y_fwd, back,
-    e_own, e_inside, e_outside, got, own, inside, outside, wide, narrow, blur,
+    background, z_fwd, x_fwd, y_fwd, back, e_own, e_inside, e_outside, got, own, inside, outside,
+    wide, narrow, names, slots, where, sem, blur,
 ):
+    copy = slot_copy(got, names, slots, sem)
+    copy.start()
     forward_kernel(
-        core, background, z_fwd, x_fwd, y_fwd, e_own, e_inside, e_outside, blur, wide, narrow
-    )
-    back_steps(core, where, back, got, blur, own, inside, outside, wide, narrow)
-
-
-def later(core, background, where, forth, back, pieces, got):
+        background, z_fwd, x_fwd, y_fwd, e_own, e_inside, e_outside, blur, wide, narrow
+    )
+    copy.wait()
+    fill_table(slots, where)
+    back_steps(where, back, got, blur, own, inside, outside, wide, narrow)
+
+
+def later(background, forth, back, pieces, got):
     return pl.pallas_call(
         later_kernel,
         out_shape=[shape((BZ, EX, NY))] * 3,
-        in_specs=[SMEM] * 3 + [VMEM] * 8,
+        in_specs=[VMEM] * 9,
         out_specs=[VMEM] * 3,
-        scratch_shapes=[
-            pltpu.VMEM((EZ * PITCH, NY), F32),
-            pltpu.VMEM((SLOTS * LINE, NY), F32),
-            pltpu.VMEM((SLOTS * BX, NY), F32),
-        ],
+        scratch_shapes=SCRATCH + [pltpu.VMEM((SLOTS * BX, NY), F32)],
         compiler_params=params(24),
         name="forward_and_back",
-    )(core, background, where, *forth, back, *pieces, got)
+    )(background, *forth, back, *pieces, got)
 
 
 def swaps(first, count):
@@ -405,7 +432,6 @@
     background,
     initial_estimate,
 ):
-    core = lax.rem(lax.axis_index("gz"), 2).astype(jnp.int32).reshape(1)
     index = lax.axis_index("xy").astype(jnp.int32).reshape(1)
     send = pack(plane_owner.reshape(SRC) * NY + plane_slot.reshape(SRC), tile_planes[0])
     even, odd = to_partners(initial_estimate, initial_estimate)
@@ -416,14 +442,15 @@
     psf = jnp.concatenate([psf_z, psf_x, psf_y], axis=0)
     taps = psf / jnp.sum(psf, axis=1, keepdims=True)
     *forth, back = weights(index, taps, view_shift)
+    levels = jnp.broadcast_to(background[:, None], (VIEWS, NY))
     bricks = jnp.concatenate([even, initial_estimate, odd], axis=1)
     for step in range(ITERS):
         pieces = (bricks, *above_and_below(bricks))
         if step == 0:
-            blur = forward(core, background, *forth, *pieces)
-            where, *parts = first_back(core, back, got, blur)
+            blur = forward(levels, *forth, *pieces)
+            parts = first_back(back, got, blur)
         else:
-            parts = later(core, background, where, forth, back, pieces, got)
+            parts = later(levels, forth, back, pieces, got)
         total = slab_sum(*parts)
         if step + 1 < ITERS:
             bricks = bricks * (three_sums(total) / VIEWS)

time: 138 us -> 139 us (level)
  starting transfers between devices: 68.8 us -> 70.4 us
    ppermute x3, starting transfers between devices: 21.7 us -> 23.2 us  [to_partners(): lax.ppermute(to_odd, 'xy', swaps(1, PEERS))]
where the time goes in v3:
time: 139 us; the launch traced here: 138 us
  starting transfers between devices  70.4 us (51%)
  waiting for transfers between devices  46.8 us (34%)
  Pallas kernels  12.1 us (9%)
  local copies, waits for them, and re-layouts  6.27 us (5%)
  other arithmetic  1.84 us (1%)
    ppermute x3, starting transfers between devices, to_partners(): lax.ppermute(to_odd, 'xy', swaps(1, PEERS))  23.2 us
    all_to_all x1, waiting for transfers between devices, local(): lax.all_to_all(send.reshape(PEERS, 1, CHUNK * NY), 'xy', split_axis=0, co...  22.7 us
    all_to_all x1, starting transfers between devices, local(): lax.all_to_all(send.reshape(PEERS, 1, CHUNK * NY), 'xy', split_axis=0, co...  10.6 us
    ppermute x3, starting transfers between devices, to_partners(): lax.ppermute(to_even, 'xy', swaps(0, PEERS))  8.11 us
    ppermute x2, waiting for transfers between devices, slab_sum(): lax.ppermute(outside, 'gz', swaps(1, count))  7.3 us
    ppermute x2, starting transfers between devices, slab_sum(): lax.ppermute(inside, 'gz', swaps(0, count))  7.02 us
    ppermute x2, starting transfers between devices, above_and_below(): lax.ppermute(block, 'gz', swaps(0, count))  7.01 us
    unnamed x32, local copies, waits for them, and re-layouts  6.11 us
  transfers between devices with their start and end apart: 17, of which 8 were waited for; matrix products, arithmetic and copies ran while one was open for 1% of the time, Pallas kernels for 5%

profile of v3, /device:TPU:34, one launch (start us, length us, event | category | flops | bytes accessed | tf_op | source)
XLA Modules:
  0.0 137.8 jit_solution(2873614154680305095)
XLA Ops:
  0.0 4.3 %collective-permute-start = (f32[16,16,128]{2,1,0:T(8,128)}, f32[16,16,128]{2,1,0:T(8,128)S(1)}, u32[]{:S(2)}, u32[]{:S(2)}) collective-permute-start(f32[16,16,128]{2,1,0:T(8,128)} %param.17), channel_id=1, source_target_pairs={{0,1},{2,3},{4,5},{6,7},{8,9},{10,11},{12,13},{14,15},{16,17},{18,... | collective-permute-start | bytes 393224 | tf_op jit(solution)/shard_map/ppermute | solution.py:382
  4.3 9.0 %collective-permute-start.1 = (f32[16,16,128]{2,1,0:T(8,128)}, f32[16,16,128]{2,1,0:T(8,128)S(1)}, u32[]{:S(2)}, u32[]{:S(2)}) collective-permute-start(f32[16,16,128]{2,1,0:T(8,128)} %param.17), channel_id=1, source_target_pairs={{1,2},{3,4},{5,6},{7,8},{9,10},{11,12},{13,14},{15,16},{17,18},{19... | collective-permute-start | bytes 393224 | tf_op jit(solution)/shard_map/ppermute | solution.py:382
  13.3 0.7 bitcast_add_fusion.named
  14.0 1.1 copy-done.2
  15.1 2.4 %pack_planes.1 = f32[3136,128]{1,0:T(8,128)} custom-call(s32[96]{0:T(128)S(1)} %bitcast_add_fusion.named, f32[96,2048]{1,0:T(8,128)S(1)} %bitcast.10), custom_call_target="tpu_custom_call" | custom-call | tf_op jit(solution)/shard_map/pack_planes/pallas_call | solution.py:74
  17.5 0.0 collective-permute-done
  17.5 0.0 collective-permute-done.1
  17.5 0.0 copy-start.11
  17.5 0.0 copy-start.12
  17.5 0.0 copy-start.13
  17.5 0.0 copy-start.9
  17.5 0.0 copy-start.14
  17.5 10.6 %all-to-all-start = ((f32[64,1,6272]{2,1,0:T(1,128)}), f32[64,1,6272]{2,1,0:T(1,128)S(1)}, u32[]{:S(2)}, u32[]{:S(2)}) async-start(f32[64,1,6272]{2,1,0:T(1,128)} %bitcast.4), calls=%async_computation | async-start | bytes 3211264 | tf_op jit(solution)/shard_map/all_to_all | solution.py:439
  28.2 0.0 copy-done.10
  28.2 1.9 %collective-permute-start.3 = (f32[16,48,128]{2,1,0:T(8,128)S(1)}, f32[16,48,128]{2,1,0:T(8,128)S(1)}, u32[]{:S(2)}, u32[]{:S(2)}) collective-permute-start(f32[16,48,128]{2,1,0:T(8,128)S(1)} %constant_dynamic-update-slice_fusion.own), channel_id=1, source_target_pairs={{64,128},{192,256},{320,384},{128,64},{256,192},{384,320},{65,129}... | collective-permute-start | bytes 1179656 | tf_op jit(solution)/shard_map/ppermute | solution.py:394
  30.2 3.5 %collective-permute-start.2 = (f32[16,48,128]{2,1,0:T(8,128)S(1)}, f32[16,48,128]{2,1,0:T(8,128)S(1)}, u32[]{:S(2)}, u32[]{:S(2)}) collective-permute-start(f32[16,48,128]{2,1,0:T(8,128)S(1)} %constant_dynamic-update-slice_fusion.own), channel_id=1, source_target_pairs={{0,64},{128,192},{256,320},{384,448},{64,0},{192,128},{320,256},{4... | collective-permute-start | bytes 1179656 | tf_op jit(solution)/shard_map/ppermute | solution.py:394
  33.7 0.1 fusion.7
  33.8 0.1 fusion.6.taps
  33.9 2.6 %operator_matrices.1 = (bf16[6,32,96]{2,1,0:T(8,128)(2,1)S(1)}, bf16[96,144]{1,0:T(8,128)(2,1)S(1)}, bf16[6,384,128]{2,1,0:T(8,128)(2,1)S(1)}, bf16[2688,128]{1,0:T(8,128)(2,1)S(1)}) custom-call(s32[1]{0:T(128)} %bitcast.3.index, f32[18,33]{1,0:T(8,128)S(1)} %fusion.6.taps, s32[6]{0:T(128)S(1)} %copy-done.9), custom_call_target="tpu_custom_call" | custom-call | tf_op jit(solution)/shard_map/operator_matrices/pallas_call | solution.py:153
  36.5 0.9 collective-permute-done.3.outside
  37.3 0.7 copy-done.3
  38.1 0.0 collective-permute-done.2.inside
  38.1 0.7 copy-done.5
  38.8 0.0 copy-done.14
  38.8 0.1 broadcast_in_dim.2.background
  38.9 1.0 copy-done.4
  39.9 1.0 copy-done.6
  40.9 1.4 %forward.1.blur = f32[1536,128]{1,0:T(8,128)S(1)} custom-call(f32[6,128]{1,0:T(8,128)S(1)} %broadcast_in_dim.2.background, bf16[6,32,96]{2,1,0:T(8,128)(2,1)S(1)} %get-tuple-element.22.z_fwd, bf16[96,144]{1,0:T(8,128)(2,1)S(1)} %get-tuple-element.23.x_fwd, bf16[6,384,128]{2,1,0:T(8,128)(2,1)S(1)} %get-tuple-element.24.y_fwd, ...), custom_call_target="tpu_custom_call" | custom-call | tf_op jit(solution)/shard_map/forward/pallas_call | solution.py:247
  42.3 0.8 copy-done
  43.1 0.6 copy-done.7
  43.7 22.7 %all-to-all-done = f32[64,1,6272]{2,1,0:T(1,128)S(1)} async-done(((f32[64,1,6272]{2,1,0:T(1,128)}), f32[64,1,6272]{2,1,0:T(1,128)S(1)}, u32[]{:S(2)}, u32[]{:S(2)}) %all-to-all-start) | async-done | bytes 1605664 | tf_op jit(solution)/shard_map/all_to_all | solution.py:439
  66.4 2.3 %first_back.1 = (f32[16,48,128]{2,1,0:T(8,128)S(1)}, f32[16,48,128]{2,1,0:T(8,128)S(1)}, f32[16,48,128]{2,1,0:T(8,128)S(1)}) custom-call(bf16[2688,128]{1,0:T(8,128)(2,1)S(1)} %get-tuple-element.20.back, f32[3136,128]{1,0:T(8,128)S(1)} %bitcast.8, f32[1536,128]{1,0:T(8,128)S(1)} %forward.1.blur), custom_call_target="tpu_custom_call" | custom-call | tf_op jit(solution)/shard_map/first_back/pallas_call | solution.py:339
  68.7 1.9 %collective-permute-start.4 = (f32[16,48,128]{2,1,0:T(8,128)S(1)}, f32[16,48,128]{2,1,0:T(8,128)S(1)}, u32[]{:S(2)}, u32[]{:S(2)}) collective-permute-start(f32[16,48,128]{2,1,0:T(8,128)S(1)} %get-tuple-element.26), channel_id=1, source_target_pairs={{64,128},{192,256},{320,384},{128,64},{256,192},{384,320},{65,129}... | collective-permute-start | bytes 1179656 | tf_op jit(solution)/shard_map/ppermute | solution.py:401
  70.7 3.5 %collective-permute-start.5 = (f32[16,48,128]{2,1,0:T(8,128)S(1)}, f32[16,48,128]{2,1,0:T(8,128)S(1)}, u32[]{:S(2)}, u32[]{:S(2)}) collective-permute-start(f32[16,48,128]{2,1,0:T(8,128)S(1)} %get-tuple-element.27), channel_id=1, source_target_pairs={{0,64},{128,192},{256,320},{384,448},{64,0},{192,128},{320,256},{4... | collective-permute-start | bytes 1179656 | tf_op jit(solution)/shard_map/ppermute | solution.py:402
  74.2 3.7 %collective-permute-done.4 = f32[16,48,128]{2,1,0:T(8,128)S(1)} collective-permute-done((f32[16,48,128]{2,1,0:T(8,128)S(1)}, f32[16,48,128]{2,1,0:T(8,128)S(1)}, u32[]{:S(2)}, u32[]{:S(2)}) %collective-permute-start.4) | collective-permute-done | bytes 393248 | tf_op jit(solution)/shard_map/ppermute | solution.py:401
  77.8 0.0 collective-permute-done.5
  77.8 0.1 add_add_fusion.1
  77.9 1.9 %collective-permute-start.6 = (f32[16,32,128]{2,1,0:T(8,128)S(1)}, f32[16,32,128]{2,1,0:T(8,128)S(1)}, u32[]{:S(2)}, u32[]{:S(2)}) collective-permute-start(f32[16,32,128]{2,1,0:T(8,128)S(1)} %get-tuple-element.38), channel_id=1, source_target_pairs={{0,1},{2,3},{4,5},{6,7},{8,9},{10,11},{12,13},{14,15},{16,17},{18,... | collective-permute-start | bytes 786440 | tf_op jit(solution)/shard_map/ppermute | solution.py:382
  79.9 0.0 copy-start.8
  79.9 8.0 %collective-permute-start.8 = (f32[16,32,128]{2,1,0:T(8,128)S(1)}, f32[16,32,128]{2,1,0:T(8,128)S(1)}, u32[]{:S(2)}, u32[]{:S(2)}) collective-permute-start(f32[16,32,128]{2,1,0:T(8,128)S(1)} %get-tuple-element.39), channel_id=1, source_target_pairs={{1,2},{3,4},{5,6},{7,8},{9,10},{11,12},{13,14},{15,16},{17,18},{19... | collective-permute-start | bytes 786440 | tf_op jit(solution)/shard_map/ppermute | solution.py:382
  88.0 3.4 %collective-permute-start.7 = (f32[16,16,128]{2,1,0:T(8,128)S(1)}, f32[16,16,128]{2,1,0:T(8,128)S(1)}, u32[]{:S(2)}, u32[]{:S(2)}) collective-permute-start(f32[16,16,128]{2,1,0:T(8,128)S(1)} %get-tuple-element.36), channel_id=1, source_target_pairs={{2,0},{4,2},{6,4},{8,6},{10,8},{12,10},{14,12},{16,14},{18,16},{20... | collective-permute-start | bytes 393224 | tf_op jit(solution)/shard_map/ppermute | solution.py:389
  91.3 3.4 %collective-permute-start.9 = (f32[16,16,128]{2,1,0:T(8,128)S(1)}, f32[16,16,128]{2,1,0:T(8,128)S(1)}, u32[]{:S(2)}, u32[]{:S(2)}) collective-permute-start(f32[16,16,128]{2,1,0:T(8,128)S(1)} %get-tuple-element.37), channel_id=1, source_target_pairs={{0,2},{2,4},{4,6},{6,8},{8,10},{10,12},{12,14},{14,16},{16,18},{18... | collective-permute-start | bytes 393224 | tf_op jit(solution)/shard_map/ppermute | solution.py:389
  94.7 4.2 %collective-permute-done.7 = f32[16,16,128]{2,1,0:T(8,128)S(1)} collective-permute-done((f32[16,16,128]{2,1,0:T(8,128)S(1)}, f32[16,16,128]{2,1,0:T(8,128)S(1)}, u32[]{:S(2)}, u32[]{:S(2)}) %collective-permute-start.7) | collective-permute-done | bytes 131104 | tf_op jit(solution)/shard_map/ppermute | solution.py:389
  98.9 3.5 %collective-permute-done.9 = f32[16,16,128]{2,1,0:T(8,128)S(1)} collective-permute-done((f32[16,16,128]{2,1,0:T(8,128)S(1)}, f32[16,16,128]{2,1,0:T(8,128)S(1)}, u32[]{:S(2)}, u32[]{:S(2)}) %collective-permute-start.9) | collective-permute-done | bytes 131104 | tf_op jit(solution)/shard_map/ppermute | solution.py:389
  102.4 0.0 collective-permute-done.6
  102.4 0.0 collective-permute-done.8
  102.4 0.1 fusion.5
  102.5 0.1 fusion.e_own
  102.6 1.9 %collective-permute-start.11 = (f32[16,48,128]{2,1,0:T(8,128)S(1)}, f32[16,48,128]{2,1,0:T(8,128)S(1)}, u32[]{:S(2)}, u32[]{:S(2)}) collective-permute-start(f32[16,48,128]{2,1,0:T(8,128)S(1)} %fusion.e_own), channel_id=1, source_target_pairs={{64,128},{192,256},{320,384},{128,64},{256,192},{384,320},{65,129}... | collective-permute-start | bytes 1179656 | tf_op jit(solution)/shard_map/ppermute | solution.py:394
  104.5 3.5 %collective-permute-start.10 = (f32[16,48,128]{2,1,0:T(8,128)S(1)}, f32[16,48,128]{2,1,0:T(8,128)S(1)}, u32[]{:S(2)}, u32[]{:S(2)}) collective-permute-start(f32[16,48,128]{2,1,0:T(8,128)S(1)} %fusion.e_own), channel_id=1, source_target_pairs={{0,64},{128,192},{256,320},{384,448},{64,0},{192,128},{320,256},{4... | collective-permute-start | bytes 1179656 | tf_op jit(solution)/shard_map/ppermute | solution.py:394
  108.0 3.6 %collective-permute-done.11.e_outside = f32[16,48,128]{2,1,0:T(8,128)S(1)} collective-permute-done((f32[16,48,128]{2,1,0:T(8,128)S(1)}, f32[16,48,128]{2,1,0:T(8,128)S(1)}, u32[]{:S(2)}, u32[]{:S(2)}) %collective-permute-start.11) | collective-permute-done | bytes 393248 | tf_op jit(solution)/shard_map/ppermute | solution.py:394
  111.7 0.0 collective-permute-done.10.e_inside
  111.7 0.0 copy-done.1
  111.7 3.5 %forward_and_back.1 = (f32[16,48,128]{2,1,0:T(8,128)S(1)}, f32[16,48,128]{2,1,0:T(8,128)S(1)}, f32[16,48,128]{2,1,0:T(8,128)S(1)}) custom-call(f32[6,128]{1,0:T(8,128)S(1)} %broadcast_in_dim.2.background, bf16[6,32,96]{2,1,0:T(8,128)(2,1)S(1)} %get-tuple-element.22.z_fwd, bf16[96,144]{1,0:T(8,128)(2,1)S(1)} %copy-done.8, bf16[6,384,128]{2,1,0:T(8,128)(2,1)S(1)} %copy-done.1, ...), custom_call_target="tpu_custom_call" | custom-call | tf_op jit(solution)/shard_map/forward_and_back/pallas_call | solution.py:365
  115.2 1.9 %collective-permute-start.12 = (f32[16,48,128]{2,1,0:T(8,128)S(1)}, f32[16,48,128]{2,1,0:T(8,128)S(1)}, u32[]{:S(2)}, u32[]{:S(2)}) collective-permute-start(f32[16,48,128]{2,1,0:T(8,128)S(1)} %get-tuple-element.29), channel_id=1, source_target_pairs={{64,128},{192,256},{320,384},{128,64},{256,192},{384,320},{65,129}... | collective-permute-start | bytes 1179656 | tf_op jit(solution)/shard_map/ppermute | solution.py:401
  117.1 3.5 %collective-permute-start.13 = (f32[16,48,128]{2,1,0:T(8,128)S(1)}, f32[16,48,128]{2,1,0:T(8,128)S(1)}, u32[]{:S(2)}, u32[]{:S(2)}) collective-permute-start(f32[16,48,128]{2,1,0:T(8,128)S(1)} %get-tuple-element.30), channel_id=1, source_target_pairs={{0,64},{128,192},{256,320},{384,448},{64,0},{192,128},{320,256},{4... | collective-permute-start | bytes 1179656 | tf_op jit(solution)/shard_map/ppermute | solution.py:402
  120.7 3.6 %collective-permute-done.12 = f32[16,48,128]{2,1,0:T(8,128)S(1)} collective-permute-done((f32[16,48,128]{2,1,0:T(8,128)S(1)}, f32[16,48,128]{2,1,0:T(8,128)S(1)}, u32[]{:S(2)}, u32[]{:S(2)}) %collective-permute-start.12) | collective-permute-done | bytes 393248 | tf_op jit(solution)/shard_map/ppermute | solution.py:401
  124.3 0.0 collective-permute-done.13
  124.3 0.1 add_add_fusion
  124.4 1.9 %collective-permute-start.14 = (f32[16,16,128]{2,1,0:T(8,128)S(1)}, f32[16,16,128]{2,1,0:T(8,128)S(1)}, u32[]{:S(2)}, u32[]{:S(2)}) collective-permute-start(f32[16,16,128]{2,1,0:T(8,128)S(1)} %get-tuple-element.34), channel_id=1, source_target_pairs={{0,1},{2,3},{4,5},{6,7},{8,9},{10,11},{12,13},{14,15},{16,17},{18,... | collective-permute-start | bytes 393224 | tf_op jit(solution)/shard_map/ppermute | solution.py:382
  126.3 6.2 %collective-permute-start.15 = (f32[16,16,128]{2,1,0:T(8,128)S(1)}, f32[16,16,128]{2,1,0:T(8,128)S(1)}, u32[]{:S(2)}, u32[]{:S(2)}) collective-permute-start(f32[16,16,128]{2,1,0:T(8,128)S(1)} %get-tuple-element.35), channel_id=1, source_target_pairs={{1,2},{3,4},{5,6},{7,8},{9,10},{11,12},{13,14},{15,16},{17,18},{19... | collective-permute-start | bytes 393224 | tf_op jit(solution)/shard_map/ppermute | solution.py:382
  132.5 0.0 collective-permute-done.14
  132.5 4.6 %collective-permute-done.15 = f32[16,16,128]{2,1,0:T(8,128)S(1)} collective-permute-done((f32[16,16,128]{2,1,0:T(8,128)S(1)}, f32[16,16,128]{2,1,0:T(8,128)S(1)}, u32[]{:S(2)}, u32[]{:S(2)}) %collective-permute-start.15) | collective-permute-done | bytes 131104 | tf_op jit(solution)/shard_map/ppermute | solution.py:382
  137.1 0.7 fusion.3
  (20 shorter events, 0.1 us)
Async XLA Ops:
  0.0 17.5 %collective-permute-start = (f32[16,16,128]{2,1,0:T(8,128)}, f32[16,16,128]{2,1,0:T(8,128)S(1)}, u32[]{:S(2)}, u32[]{:S(2)}) collective-permute-start(f32[16,16,128]{2,1,0:T(8,128)} %param.17), channel_id=1, source_target_pairs={{0,1},{2,3},{4,5},{6,7},{8,9},{10,11},{12,13},{14,15},{16,17},{18,... | collective-permute-start | bytes 393224 | tf_op jit(solution)/shard_map/ppermute | solution.py:382
  4.3 13.2 %collective-permute-start.1 = (f32[16,16,128]{2,1,0:T(8,128)}, f32[16,16,128]{2,1,0:T(8,128)S(1)}, u32[]{:S(2)}, u32[]{:S(2)}) collective-permute-start(f32[16,16,128]{2,1,0:T(8,128)} %param.17), channel_id=1, source_target_pairs={{1,2},{3,4},{5,6},{7,8},{9,10},{11,12},{13,14},{15,16},{17,18},{19... | collective-permute-start | bytes 393224 | tf_op jit(solution)/shard_map/ppermute | solution.py:382
  14.0 1.1 copy-start.2
  17.5 10.7 %copy-start.10 = (f32[16,16,128]{2,1,0:T(8,128)S(1)}, f32[16,16,128]{2,1,0:T(8,128)}, u32[]{:S(2)}) copy-start(f32[16,16,128]{2,1,0:T(8,128)} %param.17) | copy-start | bytes 393220
  17.5 16.2 %copy-start.11 = (f32[6,33]{1,0:T(8,128)S(1)}, f32[6,33]{1,0:T(8,128)}, u32[]{:S(2)}) copy-start(f32[6,33]{1,0:T(8,128)} %param.15) | copy-start | bytes 2380
  17.5 16.2 %copy-start.12 = (f32[6,33]{1,0:T(8,128)S(1)}, f32[6,33]{1,0:T(8,128)}, u32[]{:S(2)}) copy-start(f32[6,33]{1,0:T(8,128)} %param.14) | copy-start | bytes 2380
  17.5 16.2 %copy-start.13 = (f32[6,33]{1,0:T(8,128)S(1)}, f32[6,33]{1,0:T(8,128)}, u32[]{:S(2)}) copy-start(f32[6,33]{1,0:T(8,128)} %param.13) | copy-start | bytes 2380
  17.5 16.4 %copy-start.9 = (s32[6]{0:T(128)S(1)}, s32[6]{0:T(128)}, u32[]{:S(2)}) copy-start(s32[6]{0:T(128)} %shift.1) | copy-start | bytes 76
  17.5 21.3 %copy-start.14 = (f32[6]{0:T(128)S(1)}, f32[6]{0:T(128)}, u32[]{:S(2)}) copy-start(f32[6]{0:T(128)} %param.16) | copy-start | bytes 76
  17.5 48.9 %all-to-all-start = ((f32[64,1,6272]{2,1,0:T(1,128)}), f32[64,1,6272]{2,1,0:T(1,128)S(1)}, u32[]{:S(2)}, u32[]{:S(2)}) async-start(f32[64,1,6272]{2,1,0:T(1,128)} %bitcast.4), calls=%async_computation | async-start | bytes 3211264 | tf_op jit(solution)/shard_map/all_to_all | solution.py:439
  28.2 9.1 %collective-permute-start.3 = (f32[16,48,128]{2,1,0:T(8,128)S(1)}, f32[16,48,128]{2,1,0:T(8,128)S(1)}, u32[]{:S(2)}, u32[]{:S(2)}) collective-permute-start(f32[16,48,128]{2,1,0:T(8,128)S(1)} %constant_dynamic-update-slice_fusion.own), channel_id=1, source_target_pairs={{64,128},{192,256},{320,384},{128,64},{256,192},{384,320},{65,129}... | collective-permute-start | bytes 1179656 | tf_op jit(solution)/shard_map/ppermute | solution.py:394
  30.2 7.9 %collective-permute-start.2 = (f32[16,48,128]{2,1,0:T(8,128)S(1)}, f32[16,48,128]{2,1,0:T(8,128)S(1)}, u32[]{:S(2)}, u32[]{:S(2)}) collective-permute-start(f32[16,48,128]{2,1,0:T(8,128)S(1)} %constant_dynamic-update-slice_fusion.own), channel_id=1, source_target_pairs={{0,64},{128,192},{256,320},{384,448},{64,0},{192,128},{320,256},{4... | collective-permute-start | bytes 1179656 | tf_op jit(solution)/shard_map/ppermute | solution.py:394
  37.3 0.7 copy-start.3
  38.1 0.7 copy-start.5
  38.9 1.0 copy-start.4
  39.9 1.0 copy-start.6
  42.3 0.8 copy-start
  43.1 0.6 copy-start.7
  68.7 9.1 %collective-permute-start.4 = (f32[16,48,128]{2,1,0:T(8,128)S(1)}, f32[16,48,128]{2,1,0:T(8,128)S(1)}, u32[]{:S(2)}, u32[]{:S(2)}) collective-permute-start(f32[16,48,128]{2,1,0:T(8,128)S(1)} %get-tuple-element.26), channel_id=1, source_target_pairs={{64,128},{192,256},{320,384},{128,64},{256,192},{384,320},{65,129}... | collective-permute-start | bytes 1179656 | tf_op jit(solution)/shard_map/ppermute | solution.py:401
  70.7 7.2 %collective-permute-start.5 = (f32[16,48,128]{2,1,0:T(8,128)S(1)}, f32[16,48,128]{2,1,0:T(8,128)S(1)}, u32[]{:S(2)}, u32[]{:S(2)}) collective-permute-start(f32[16,48,128]{2,1,0:T(8,128)S(1)} %get-tuple-element.27), channel_id=1, source_target_pairs={{0,64},{128,192},{256,320},{384,448},{64,0},{192,128},{320,256},{4... | collective-permute-start | bytes 1179656 | tf_op jit(solution)/shard_map/ppermute | solution.py:402
  77.9 24.5 %collective-permute-start.6 = (f32[16,32,128]{2,1,0:T(8,128)S(1)}, f32[16,32,128]{2,1,0:T(8,128)S(1)}, u32[]{:S(2)}, u32[]{:S(2)}) collective-permute-start(f32[16,32,128]{2,1,0:T(8,128)S(1)} %get-tuple-element.38), channel_id=1, source_target_pairs={{0,1},{2,3},{4,5},{6,7},{8,9},{10,11},{12,13},{14,15},{16,17},{18,... | collective-permute-start | bytes 786440 | tf_op jit(solution)/shard_map/ppermute | solution.py:382
  79.9 31.8 %copy-start.1 = (bf16[6,384,128]{2,1,0:T(8,128)(2,1)S(1)}, bf16[6,384,128]{2,1,0:T(8,128)(2,1)}, u32[]{:S(2)}) copy-start(bf16[6,384,128]{2,1,0:T(8,128)(2,1)} %copy-done) | copy-start | bytes 1769476
  79.9 31.8 %copy-start.8 = (bf16[96,144]{1,0:T(8,128)(2,1)S(1)}, bf16[96,144]{1,0:T(8,128)(2,1)}, u32[]{:S(2)}) copy-start(bf16[96,144]{1,0:T(8,128)(2,1)} %copy-done.7) | copy-start | bytes 82948
  79.9 22.5 %collective-permute-start.8 = (f32[16,32,128]{2,1,0:T(8,128)S(1)}, f32[16,32,128]{2,1,0:T(8,128)S(1)}, u32[]{:S(2)}, u32[]{:S(2)}) collective-permute-start(f32[16,32,128]{2,1,0:T(8,128)S(1)} %get-tuple-element.39), channel_id=1, source_target_pairs={{1,2},{3,4},{5,6},{7,8},{9,10},{11,12},{13,14},{15,16},{17,18},{19... | collective-permute-start | bytes 786440 | tf_op jit(solution)/shard_map/ppermute | solution.py:382
  88.0 11.0 %collective-permute-start.7 = (f32[16,16,128]{2,1,0:T(8,128)S(1)}, f32[16,16,128]{2,1,0:T(8,128)S(1)}, u32[]{:S(2)}, u32[]{:S(2)}) collective-permute-start(f32[16,16,128]{2,1,0:T(8,128)S(1)} %get-tuple-element.36), channel_id=1, source_target_pairs={{2,0},{4,2},{6,4},{8,6},{10,8},{12,10},{14,12},{16,14},{18,16},{20... | collective-permute-start | bytes 393224 | tf_op jit(solution)/shard_map/ppermute | solution.py:389
  91.3 11.1 %collective-permute-start.9 = (f32[16,16,128]{2,1,0:T(8,128)S(1)}, f32[16,16,128]{2,1,0:T(8,128)S(1)}, u32[]{:S(2)}, u32[]{:S(2)}) collective-permute-start(f32[16,16,128]{2,1,0:T(8,128)S(1)} %get-tuple-element.37), channel_id=1, source_target_pairs={{0,2},{2,4},{4,6},{6,8},{8,10},{10,12},{12,14},{14,16},{16,18},{18... | collective-permute-start | bytes 393224 | tf_op jit(solution)/shard_map/ppermute | solution.py:389
  102.6 9.1 %collective-permute-start.11 = (f32[16,48,128]{2,1,0:T(8,128)S(1)}, f32[16,48,128]{2,1,0:T(8,128)S(1)}, u32[]{:S(2)}, u32[]{:S(2)}) collective-permute-start(f32[16,48,128]{2,1,0:T(8,128)S(1)} %fusion.e_own), channel_id=1, source_target_pairs={{64,128},{192,256},{320,384},{128,64},{256,192},{384,320},{65,129}... | collective-permute-start | bytes 1179656 | tf_op jit(solution)/shard_map/ppermute | solution.py:394
  104.5 7.2 %collective-permute-start.10 = (f32[16,48,128]{2,1,0:T(8,128)S(1)}, f32[16,48,128]{2,1,0:T(8,128)S(1)}, u32[]{:S(2)}, u32[]{:S(2)}) collective-permute-start(f32[16,48,128]{2,1,0:T(8,128)S(1)} %fusion.e_own), channel_id=1, source_target_pairs={{0,64},{128,192},{256,320},{384,448},{64,0},{192,128},{320,256},{4... | collective-permute-start | bytes 1179656 | tf_op jit(solution)/shard_map/ppermute | solution.py:394
  115.2 9.1 %collective-permute-start.12 = (f32[16,48,128]{2,1,0:T(8,128)S(1)}, f32[16,48,128]{2,1,0:T(8,128)S(1)}, u32[]{:S(2)}, u32[]{:S(2)}) collective-permute-start(f32[16,48,128]{2,1,0:T(8,128)S(1)} %get-tuple-element.29), channel_id=1, source_target_pairs={{64,128},{192,256},{320,384},{128,64},{256,192},{384,320},{65,129}... | collective-permute-start | bytes 1179656 | tf_op jit(solution)/shard_map/ppermute | solution.py:401
  117.1 7.2 %collective-permute-start.13 = (f32[16,48,128]{2,1,0:T(8,128)S(1)}, f32[16,48,128]{2,1,0:T(8,128)S(1)}, u32[]{:S(2)}, u32[]{:S(2)}) collective-permute-start(f32[16,48,128]{2,1,0:T(8,128)S(1)} %get-tuple-element.30), channel_id=1, source_target_pairs={{0,64},{128,192},{256,320},{384,448},{64,0},{192,128},{320,256},{4... | collective-permute-start | bytes 1179656 | tf_op jit(solution)/shard_map/ppermute | solution.py:402
  124.4 8.1 %collective-permute-start.14 = (f32[16,16,128]{2,1,0:T(8,128)S(1)}, f32[16,16,128]{2,1,0:T(8,128)S(1)}, u32[]{:S(2)}, u32[]{:S(2)}) collective-permute-start(f32[16,16,128]{2,1,0:T(8,128)S(1)} %get-tuple-element.34), channel_id=1, source_target_pairs={{0,1},{2,3},{4,5},{6,7},{8,9},{10,11},{12,13},{14,15},{16,17},{18,... | collective-permute-start | bytes 393224 | tf_op jit(solution)/shard_map/ppermute | solution.py:382
  126.3 10.8 %collective-permute-start.15 = (f32[16,16,128]{2,1,0:T(8,128)S(1)}, f32[16,16,128]{2,1,0:T(8,128)S(1)}, u32[]{:S(2)}, u32[]{:S(2)}) collective-permute-start(f32[16,16,128]{2,1,0:T(8,128)S(1)} %get-tuple-element.35), channel_id=1, source_target_pairs={{1,2},{3,4},{5,6},{7,8},{9,10},{11,12},{13,14},{15,16},{17,18},{19... | collective-permute-start | bytes 393224 | tf_op jit(solution)/shard_map/ppermute | solution.py:382

commit v4 on v2

--- a/solution.py
+++ b/solution.py
@@ -43,26 +43,29 @@
     return high, (value - high.astype(F32)).astype(BF16)
 
 
-def pack_kernel(named, planes, send, rows, count):
+def pack_kernel(named_in, planes, send, rows, count, named, sem):
+    copy = pltpu.make_async_copy(named_in, named, sem)
+    copy.start()
     for peer in range(PEERS):
         count[peer] = 0
     send[pl.ds(SEND * BX, PEERS, stride=CHUNK), :] = jnp.full((PEERS, NY), SLOTS, F32)
     for group in range(SRC // 8):
         for column in range(BX):
-            rows[pl.ds(group * 8 * BX + column, 8, stride=BX), :] = planes[
+            rows[pl.ds(group * 8 * LINE + column, 8, stride=LINE), :] = planes[
                 group * 8 : group * 8 + 8, column * NY : (column + 1) * NY
             ]
     lane = lax.broadcasted_iota(jnp.int32, (1, NY), 1)
+    copy.wait()
 
     def place(plane, carry):
-        peer = named[plane] >> 7
+        peer = named[0, plane] >> 7
         rank = count[peer]
         count[peer] = rank + 1
         start = peer * CHUNK
-        send[pl.ds(start + rank * BX, BX), :] = rows[pl.ds(pl.multiple_of(plane * BX, BX), BX), :]
+        send[pl.ds(start + rank * BX, BX), :] = rows[pl.ds(pl.multiple_of(plane * LINE, 8), BX), :]
         pltpu.store(
             send.at[pl.ds(start + SEND * BX, 1), :],
-            jnp.full((1, NY), named[plane] & (NY - 1), jnp.int32).astype(F32),
+            jnp.full((1, NY), named[0, plane] & (NY - 1), jnp.int32).astype(F32),
             mask=lane == rank,
         )
         return carry
@@ -74,11 +77,13 @@
     return pl.pallas_call(
         pack_kernel,
         out_shape=shape((PEERS * CHUNK, NY)),
-        in_specs=[SMEM, VMEM],
+        in_specs=[VMEM, VMEM],
         out_specs=VMEM,
         scratch_shapes=[
-            pltpu.VMEM((SRC * BX, NY), F32),
+            pltpu.VMEM((SRC * LINE, NY), F32),
             pltpu.SMEM((PEERS,), jnp.int32),
+            pltpu.SMEM((1, NY), jnp.int32),
+            pltpu.SemaphoreType.DMA,
         ],
         compiler_params=params(16),
         name="pack_planes",
@@ -407,7 +412,8 @@
 ):
     core = lax.rem(lax.axis_index("gz"), 2).astype(jnp.int32).reshape(1)
     index = lax.axis_index("xy").astype(jnp.int32).reshape(1)
-    send = pack(plane_owner.reshape(SRC) * NY + plane_slot.reshape(SRC), tile_planes[0])
+    named = plane_owner.reshape(1, SRC) * NY + plane_slot.reshape(1, SRC)
+    send = pack(jnp.pad(named, ((0, 0), (0, NY - SRC))), tile_planes[0])
     even, odd = to_partners(initial_estimate, initial_estimate)
     send, even, odd = lax.optimization_barrier((send, even, odd))
     got = lax.all_to_all(

time: 138 us -> 138 us (level)
  the two profiles are of different devices: /device:TPU:34 before, /device:TPU:36 now
where the time goes in v4:
time: 138 us
  starting transfers between devices  68.9 us (50%)
  waiting for transfers between devices  47.5 us (34%)
  Pallas kernels  12.9 us (9%)
  local copies, waits for them, and re-layouts  6.21 us (4%)
  other arithmetic  1.87 us (1%)
    ppermute x3, starting transfers between devices, to_partners(): lax.ppermute(to_odd, 'xy', swaps(1, PEERS))  22.5 us
    all_to_all x1, waiting for transfers between devices, local(): lax.all_to_all(send.reshape(PEERS, 1, CHUNK * NY), 'xy', split_axis=0, co...  21.8 us
    all_to_all x1, starting transfers between devices, local(): lax.all_to_all(send.reshape(PEERS, 1, CHUNK * NY), 'xy', split_axis=0, co...  10.7 us
    ppermute x3, starting transfers between devices, to_partners(): lax.ppermute(to_even, 'xy', swaps(0, PEERS))  8.4 us
    ppermute x2, waiting for transfers between devices, slab_sum(): lax.ppermute(outside, 'gz', swaps(1, count))  7.89 us
    ppermute x2, starting transfers between devices, above_and_below(): lax.ppermute(block, 'gz', swaps(0, count))  6.41 us
    ppermute x2, starting transfers between devices, slab_sum(): lax.ppermute(inside, 'gz', swaps(0, count))  6.21 us
    unnamed x32, local copies, waits for them, and re-layouts  6.11 us
  transfers between devices with their start and end apart: 17, of which 8 were waited for; matrix products, arithmetic and copies ran while one was open for 1% of the time, Pallas kernels for 5%

profile of v4, /device:TPU:36, one launch (start us, length us, event | category | flops | bytes accessed | tf_op | source)
XLA Modules:
  0.0 137.7 jit_solution(3404932281687258245)
XLA Ops:
  0.0 4.3 %collective-permute-start = (f32[16,16,128]{2,1,0:T(8,128)}, f32[16,16,128]{2,1,0:T(8,128)S(1)}, u32[]{:S(2)}, u32[]{:S(2)}) collective-permute-start(f32[16,16,128]{2,1,0:T(8,128)} %param.17), channel_id=1, source_target_pairs={{0,1},{2,3},{4,5},{6,7},{8,9},{10,11},{12,13},{14,15},{16,17},{18,... | collective-permute-start | bytes 393224 | tf_op jit(solution)/shard_map/ppermute | solution.py:360
  4.3 9.0 %collective-permute-start.1 = (f32[16,16,128]{2,1,0:T(8,128)}, f32[16,16,128]{2,1,0:T(8,128)S(1)}, u32[]{:S(2)}, u32[]{:S(2)}) collective-permute-start(f32[16,16,128]{2,1,0:T(8,128)} %param.17), channel_id=1, source_target_pairs={{1,2},{3,4},{5,6},{7,8},{9,10},{11,12},{13,14},{15,16},{17,18},{19... | collective-permute-start | bytes 393224 | tf_op jit(solution)/shard_map/ppermute | solution.py:360
  13.3 0.7 bitcast_add_fusion
  14.0 1.1 copy-done.2
  15.1 2.2 %pack_planes.1 = f32[3136,128]{1,0:T(8,128)} custom-call(s32[1,128]{1,0:T(1,128)S(1)} %pad.4.named_in, f32[96,2048]{1,0:T(8,128)S(1)} %bitcast.9), custom_call_target="tpu_custom_call" | custom-call | tf_op jit(solution)/shard_map/pack_planes/pallas_call | solution.py:77
  17.4 0.0 collective-permute-done
  17.4 0.0 collective-permute-done.1
  17.4 0.0 copy-start.11
  17.4 0.0 copy-start.12
  17.4 0.0 copy-start.13
  17.4 0.0 copy-start.14
  17.4 0.0 copy-start.10
  17.4 0.0 copy-start.9
  17.4 10.7 %all-to-all-start = ((f32[64,1,6272]{2,1,0:T(1,128)}), f32[64,1,6272]{2,1,0:T(1,128)S(1)}, u32[]{:S(2)}, u32[]{:S(2)}) async-start(f32[64,1,6272]{2,1,0:T(1,128)} %bitcast.4), calls=%async_computation | async-start | bytes 3211264 | tf_op jit(solution)/shard_map/all_to_all | solution.py:419
  28.2 0.0 copy-done.11
  28.2 1.9 %collective-permute-start.3 = (f32[16,48,128]{2,1,0:T(8,128)S(1)}, f32[16,48,128]{2,1,0:T(8,128)S(1)}, u32[]{:S(2)}, u32[]{:S(2)}) collective-permute-start(f32[16,48,128]{2,1,0:T(8,128)S(1)} %constant_dynamic-update-slice_fusion.own), channel_id=1, source_target_pairs={{64,128},{192,256},{320,384},{128,64},{256,192},{384,320},{65,129}... | collective-permute-start | bytes 1179656 | tf_op jit(solution)/shard_map/ppermute | solution.py:372
  30.2 3.2 %collective-permute-start.2 = (f32[16,48,128]{2,1,0:T(8,128)S(1)}, f32[16,48,128]{2,1,0:T(8,128)S(1)}, u32[]{:S(2)}, u32[]{:S(2)}) collective-permute-start(f32[16,48,128]{2,1,0:T(8,128)S(1)} %constant_dynamic-update-slice_fusion.own), channel_id=1, source_target_pairs={{0,64},{128,192},{256,320},{384,448},{64,0},{192,128},{320,256},{4... | collective-permute-start | bytes 1179656 | tf_op jit(solution)/shard_map/ppermute | solution.py:372
  33.4 0.0 copy-done.12
  33.4 0.0 copy-done.13
  33.4 0.1 fusion.7
  33.5 0.1 fusion.6.taps
  33.6 2.6 %operator_matrices.1 = (bf16[6,16,144]{2,1,0:T(8,128)(2,1)S(1)}, bf16[96,144]{1,0:T(8,128)(2,1)S(1)}, bf16[6,384,128]{2,1,0:T(8,128)(2,1)S(1)}, bf16[2736,128]{1,0:T(8,128)(2,1)S(1)}) custom-call(s32[1]{0:T(128)} %bitcast.3.index, f32[18,33]{1,0:T(8,128)S(1)} %fusion.6.taps, s32[6]{0:T(128)S(1)} %copy-done.10), custom_call_target="tpu_custom_call" | custom-call | tf_op jit(solution)/shard_map/operator_matrices/pallas_call | solution.py:158
  36.2 1.1 collective-permute-done.3.outside
  37.3 0.7 copy-done.3
  38.1 0.0 collective-permute-done.2.inside
  38.1 0.7 copy-done.5
  38.8 1.0 copy-done.4
  39.8 1.0 copy-done.6
  40.8 2.0 %forward.1.blur = f32[1536,128]{1,0:T(8,128)S(1)} custom-call(s32[1]{0:T(128)} %bitcast.2.core, f32[6]{0:T(128)S(1)} %copy-done.9, bf16[6,16,144]{2,1,0:T(8,128)(2,1)S(1)} %get-tuple-element.23.z_fwd, bf16[96,144]{1,0:T(8,128)(2,1)S(1)} %get-tuple-element.24.x_fwd, bf16[6,384,128]{2,1,0:T(8,128)(2,1)S(1)} %get-tuple-element.25.y_fwd, ...), custom_call_target="tpu_custom_call" | custom-call | tf_op jit(solution)/shard_map/forward/pallas_call | solution.py:238
  42.8 0.8 copy-done
  43.6 0.6 copy-done.7
  44.2 21.8 %all-to-all-done = f32[64,1,6272]{2,1,0:T(1,128)S(1)} async-done(((f32[64,1,6272]{2,1,0:T(1,128)}), f32[64,1,6272]{2,1,0:T(1,128)S(1)}, u32[]{:S(2)}, u32[]{:S(2)}) %all-to-all-start) | async-done | bytes 1605664 | tf_op jit(solution)/shard_map/all_to_all | solution.py:419
  66.1 2.6 %first_back.1 = (s32[128]{0:T(128)S(1)}, f32[16,48,128]{2,1,0:T(8,128)S(1)}, f32[16,48,128]{2,1,0:T(8,128)S(1)}, f32[16,48,128]{2,1,0:T(8,128)S(1)}) custom-call(s32[1]{0:T(128)} %bitcast.2.core, bf16[2736,128]{1,0:T(8,128)(2,1)S(1)} %get-tuple-element.21.back, f32[3136,128]{1,0:T(8,128)S(1)} %bitcast.7, f32[1536,128]{1,0:T(8,128)S(1)} %forward.1.blur), custom_call_target="tpu_custom_call" | custom-call | tf_op jit(solution)/shard_map/first_back/pallas_call | solution.py:311
  68.7 1.9 %collective-permute-start.4 = (f32[16,48,128]{2,1,0:T(8,128)S(1)}, f32[16,48,128]{2,1,0:T(8,128)S(1)}, u32[]{:S(2)}, u32[]{:S(2)}) collective-permute-start(f32[16,48,128]{2,1,0:T(8,128)S(1)} %get-tuple-element.27), channel_id=1, source_target_pairs={{64,128},{192,256},{320,384},{128,64},{256,192},{384,320},{65,129}... | collective-permute-start | bytes 1179656 | tf_op jit(solution)/shard_map/ppermute | solution.py:379
  70.6 3.2 %collective-permute-start.5 = (f32[16,48,128]{2,1,0:T(8,128)S(1)}, f32[16,48,128]{2,1,0:T(8,128)S(1)}, u32[]{:S(2)}, u32[]{:S(2)}) collective-permute-start(f32[16,48,128]{2,1,0:T(8,128)S(1)} %get-tuple-element.28), channel_id=1, source_target_pairs={{0,64},{128,192},{256,320},{384,448},{64,0},{192,128},{320,256},{4... | collective-permute-start | bytes 1179656 | tf_op jit(solution)/shard_map/ppermute | solution.py:380
  73.9 3.9 %collective-permute-done.4 = f32[16,48,128]{2,1,0:T(8,128)S(1)} collective-permute-done((f32[16,48,128]{2,1,0:T(8,128)S(1)}, f32[16,48,128]{2,1,0:T(8,128)S(1)}, u32[]{:S(2)}, u32[]{:S(2)}) %collective-permute-start.4) | collective-permute-done | bytes 393248 | tf_op jit(solution)/shard_map/ppermute | solution.py:379
  77.8 0.0 collective-permute-done.5
  77.8 0.1 add_add_fusion.1
  77.9 2.2 %collective-permute-start.6 = (f32[16,32,128]{2,1,0:T(8,128)S(1)}, f32[16,32,128]{2,1,0:T(8,128)S(1)}, u32[]{:S(2)}, u32[]{:S(2)}) collective-permute-start(f32[16,32,128]{2,1,0:T(8,128)S(1)} %get-tuple-element.40), channel_id=1, source_target_pairs={{0,1},{2,3},{4,5},{6,7},{8,9},{10,11},{12,13},{14,15},{16,17},{18,... | collective-permute-start | bytes 786440 | tf_op jit(solution)/shard_map/ppermute | solution.py:360
  80.2 0.0 copy-start.8
  80.2 7.7 %collective-permute-start.8 = (f32[16,32,128]{2,1,0:T(8,128)S(1)}, f32[16,32,128]{2,1,0:T(8,128)S(1)}, u32[]{:S(2)}, u32[]{:S(2)}) collective-permute-start(f32[16,32,128]{2,1,0:T(8,128)S(1)} %get-tuple-element.41), channel_id=1, source_target_pairs={{1,2},{3,4},{5,6},{7,8},{9,10},{11,12},{13,14},{15,16},{17,18},{19... | collective-permute-start | bytes 786440 | tf_op jit(solution)/shard_map/ppermute | solution.py:360
  87.9 3.4 %collective-permute-start.7 = (f32[16,16,128]{2,1,0:T(8,128)S(1)}, f32[16,16,128]{2,1,0:T(8,128)S(1)}, u32[]{:S(2)}, u32[]{:S(2)}) collective-permute-start(f32[16,16,128]{2,1,0:T(8,128)S(1)} %get-tuple-element.38), channel_id=1, source_target_pairs={{2,0},{4,2},{6,4},{8,6},{10,8},{12,10},{14,12},{16,14},{18,16},{20... | collective-permute-start | bytes 393224 | tf_op jit(solution)/shard_map/ppermute | solution.py:367
  91.3 3.4 %collective-permute-start.9 = (f32[16,16,128]{2,1,0:T(8,128)S(1)}, f32[16,16,128]{2,1,0:T(8,128)S(1)}, u32[]{:S(2)}, u32[]{:S(2)}) collective-permute-start(f32[16,16,128]{2,1,0:T(8,128)S(1)} %get-tuple-element.39), channel_id=1, source_target_pairs={{0,2},{2,4},{4,6},{6,8},{8,10},{10,12},{12,14},{14,16},{16,18},{18... | collective-permute-start | bytes 393224 | tf_op jit(solution)/shard_map/ppermute | solution.py:367
  94.6 4.1 %collective-permute-done.7 = f32[16,16,128]{2,1,0:T(8,128)S(1)} collective-permute-done((f32[16,16,128]{2,1,0:T(8,128)S(1)}, f32[16,16,128]{2,1,0:T(8,128)S(1)}, u32[]{:S(2)}, u32[]{:S(2)}) %collective-permute-start.7) | collective-permute-done | bytes 131104 | tf_op jit(solution)/shard_map/ppermute | solution.py:367
  98.7 3.6 %collective-permute-done.9 = f32[16,16,128]{2,1,0:T(8,128)S(1)} collective-permute-done((f32[16,16,128]{2,1,0:T(8,128)S(1)}, f32[16,16,128]{2,1,0:T(8,128)S(1)}, u32[]{:S(2)}, u32[]{:S(2)}) %collective-permute-start.9) | collective-permute-done | bytes 131104 | tf_op jit(solution)/shard_map/ppermute | solution.py:367
  102.3 0.0 collective-permute-done.6
  102.3 0.0 collective-permute-done.8
  102.3 0.1 fusion.5
  102.4 0.1 fusion.e_own
  102.5 1.9 %collective-permute-start.11 = (f32[16,48,128]{2,1,0:T(8,128)S(1)}, f32[16,48,128]{2,1,0:T(8,128)S(1)}, u32[]{:S(2)}, u32[]{:S(2)}) collective-permute-start(f32[16,48,128]{2,1,0:T(8,128)S(1)} %fusion.e_own), channel_id=1, source_target_pairs={{64,128},{192,256},{320,384},{128,64},{256,192},{384,320},{65,129}... | collective-permute-start | bytes 1179656 | tf_op jit(solution)/shard_map/ppermute | solution.py:372
  104.4 3.2 %collective-permute-start.10 = (f32[16,48,128]{2,1,0:T(8,128)S(1)}, f32[16,48,128]{2,1,0:T(8,128)S(1)}, u32[]{:S(2)}, u32[]{:S(2)}) collective-permute-start(f32[16,48,128]{2,1,0:T(8,128)S(1)} %fusion.e_own), channel_id=1, source_target_pairs={{0,64},{128,192},{256,320},{384,448},{64,0},{192,128},{320,256},{4... | collective-permute-start | bytes 1179656 | tf_op jit(solution)/shard_map/ppermute | solution.py:372
  107.6 4.0 %collective-permute-done.11.e_outside = f32[16,48,128]{2,1,0:T(8,128)S(1)} collective-permute-done((f32[16,48,128]{2,1,0:T(8,128)S(1)}, f32[16,48,128]{2,1,0:T(8,128)S(1)}, u32[]{:S(2)}, u32[]{:S(2)}) %collective-permute-start.11) | collective-permute-done | bytes 393248 | tf_op jit(solution)/shard_map/ppermute | solution.py:372
  111.6 0.0 collective-permute-done.10.e_inside
  111.6 3.6 %forward_and_back.1 = (f32[16,48,128]{2,1,0:T(8,128)S(1)}, f32[16,48,128]{2,1,0:T(8,128)S(1)}, f32[16,48,128]{2,1,0:T(8,128)S(1)}) custom-call(s32[1]{0:T(128)} %bitcast.2.core, f32[6]{0:T(128)S(1)} %copy-done.9, s32[128]{0:T(128)S(1)} %get-tuple-element.29.where, bf16[6,16,144]{2,1,0:T(8,128)(2,1)S(1)} %get-tuple-element.23.z_fwd, ...), custom_call_target="tpu_custom_call" | custom-call | tf_op jit(solution)/shard_map/forward_and_back/pallas_call | solution.py:339
  115.2 2.1 %collective-permute-start.12 = (f32[16,48,128]{2,1,0:T(8,128)S(1)}, f32[16,48,128]{2,1,0:T(8,128)S(1)}, u32[]{:S(2)}, u32[]{:S(2)}) collective-permute-start(f32[16,48,128]{2,1,0:T(8,128)S(1)} %get-tuple-element.31), channel_id=1, source_target_pairs={{64,128},{192,256},{320,384},{128,64},{256,192},{384,320},{65,129}... | collective-permute-start | bytes 1179656 | tf_op jit(solution)/shard_map/ppermute | solution.py:379
  117.3 3.0 %collective-permute-start.13 = (f32[16,48,128]{2,1,0:T(8,128)S(1)}, f32[16,48,128]{2,1,0:T(8,128)S(1)}, u32[]{:S(2)}, u32[]{:S(2)}) collective-permute-start(f32[16,48,128]{2,1,0:T(8,128)S(1)} %get-tuple-element.32), channel_id=1, source_target_pairs={{0,64},{128,192},{256,320},{384,448},{64,0},{192,128},{320,256},{4... | collective-permute-start | bytes 1179656 | tf_op jit(solution)/shard_map/ppermute | solution.py:380
  120.3 3.9 %collective-permute-done.12 = f32[16,48,128]{2,1,0:T(8,128)S(1)} collective-permute-done((f32[16,48,128]{2,1,0:T(8,128)S(1)}, f32[16,48,128]{2,1,0:T(8,128)S(1)}, u32[]{:S(2)}, u32[]{:S(2)}) %collective-permute-start.12) | collective-permute-done | bytes 393248 | tf_op jit(solution)/shard_map/ppermute | solution.py:379
  124.3 0.0 collective-permute-done.13
  124.3 0.1 add_add_fusion
  124.4 1.9 %collective-permute-start.14 = (f32[16,16,128]{2,1,0:T(8,128)S(1)}, f32[16,16,128]{2,1,0:T(8,128)S(1)}, u32[]{:S(2)}, u32[]{:S(2)}) collective-permute-start(f32[16,16,128]{2,1,0:T(8,128)S(1)} %get-tuple-element.36), channel_id=1, source_target_pairs={{0,1},{2,3},{4,5},{6,7},{8,9},{10,11},{12,13},{14,15},{16,17},{18,... | collective-permute-start | bytes 393224 | tf_op jit(solution)/shard_map/ppermute | solution.py:360
  126.3 5.8 %collective-permute-start.15 = (f32[16,16,128]{2,1,0:T(8,128)S(1)}, f32[16,16,128]{2,1,0:T(8,128)S(1)}, u32[]{:S(2)}, u32[]{:S(2)}) collective-permute-start(f32[16,16,128]{2,1,0:T(8,128)S(1)} %get-tuple-element.37), channel_id=1, source_target_pairs={{1,2},{3,4},{5,6},{7,8},{9,10},{11,12},{13,14},{15,16},{17,18},{19... | collective-permute-start | bytes 393224 | tf_op jit(solution)/shard_map/ppermute | solution.py:360
  132.1 0.0 collective-permute-done.14
  132.1 4.9 %collective-permute-done.15 = f32[16,16,128]{2,1,0:T(8,128)S(1)} collective-permute-done((f32[16,16,128]{2,1,0:T(8,128)S(1)}, f32[16,16,128]{2,1,0:T(8,128)S(1)}, u32[]{:S(2)}, u32[]{:S(2)}) %collective-permute-start.15) | collective-permute-done | bytes 131104 | tf_op jit(solution)/shard_map/ppermute | solution.py:360
  137.1 0.7 fusion.3
  (20 shorter events, 0.1 us)
Async XLA Ops:
  0.0 17.4 %collective-permute-start = (f32[16,16,128]{2,1,0:T(8,128)}, f32[16,16,128]{2,1,0:T(8,128)S(1)}, u32[]{:S(2)}, u32[]{:S(2)}) collective-permute-start(f32[16,16,128]{2,1,0:T(8,128)} %param.17), channel_id=1, source_target_pairs={{0,1},{2,3},{4,5},{6,7},{8,9},{10,11},{12,13},{14,15},{16,17},{18,... | collective-permute-start | bytes 393224 | tf_op jit(solution)/shard_map/ppermute | solution.py:360
  4.3 13.1 %collective-permute-start.1 = (f32[16,16,128]{2,1,0:T(8,128)}, f32[16,16,128]{2,1,0:T(8,128)S(1)}, u32[]{:S(2)}, u32[]{:S(2)}) collective-permute-start(f32[16,16,128]{2,1,0:T(8,128)} %param.17), channel_id=1, source_target_pairs={{1,2},{3,4},{5,6},{7,8},{9,10},{11,12},{13,14},{15,16},{17,18},{19... | collective-permute-start | bytes 393224 | tf_op jit(solution)/shard_map/ppermute | solution.py:360
  14.0 1.1 copy-start.2
  17.4 10.8 %copy-start.11 = (f32[16,16,128]{2,1,0:T(8,128)S(1)}, f32[16,16,128]{2,1,0:T(8,128)}, u32[]{:S(2)}) copy-start(f32[16,16,128]{2,1,0:T(8,128)} %param.17) | copy-start | bytes 393220
  17.4 16.0 %copy-start.12 = (f32[6,33]{1,0:T(8,128)S(1)}, f32[6,33]{1,0:T(8,128)}, u32[]{:S(2)}) copy-start(f32[6,33]{1,0:T(8,128)} %param.15) | copy-start | bytes 2380
  17.4 16.0 %copy-start.13 = (f32[6,33]{1,0:T(8,128)S(1)}, f32[6,33]{1,0:T(8,128)}, u32[]{:S(2)}) copy-start(f32[6,33]{1,0:T(8,128)} %param.14) | copy-start | bytes 2380
  17.4 16.0 %copy-start.14 = (f32[6,33]{1,0:T(8,128)S(1)}, f32[6,33]{1,0:T(8,128)}, u32[]{:S(2)}) copy-start(f32[6,33]{1,0:T(8,128)} %param.13) | copy-start | bytes 2380
  17.4 16.2 %copy-start.10 = (s32[6]{0:T(128)S(1)}, s32[6]{0:T(128)}, u32[]{:S(2)}) copy-start(s32[6]{0:T(128)} %shift.1) | copy-start | bytes 76
  17.4 21.4 %copy-start.9 = (f32[6]{0:T(128)S(1)}, f32[6]{0:T(128)}, u32[]{:S(2)}) copy-start(f32[6]{0:T(128)} %background.3) | copy-start | bytes 76
  17.4 48.6 %all-to-all-start = ((f32[64,1,6272]{2,1,0:T(1,128)}), f32[64,1,6272]{2,1,0:T(1,128)S(1)}, u32[]{:S(2)}, u32[]{:S(2)}) async-start(f32[64,1,6272]{2,1,0:T(1,128)} %bitcast.4), calls=%async_computation | async-start | bytes 3211264 | tf_op jit(solution)/shard_map/all_to_all | solution.py:419
  28.2 9.1 %collective-permute-start.3 = (f32[16,48,128]{2,1,0:T(8,128)S(1)}, f32[16,48,128]{2,1,0:T(8,128)S(1)}, u32[]{:S(2)}, u32[]{:S(2)}) collective-permute-start(f32[16,48,128]{2,1,0:T(8,128)S(1)} %constant_dynamic-update-slice_fusion.own), channel_id=1, source_target_pairs={{64,128},{192,256},{320,384},{128,64},{256,192},{384,320},{65,129}... | collective-permute-start | bytes 1179656 | tf_op jit(solution)/shard_map/ppermute | solution.py:372
  30.2 7.9 %collective-permute-start.2 = (f32[16,48,128]{2,1,0:T(8,128)S(1)}, f32[16,48,128]{2,1,0:T(8,128)S(1)}, u32[]{:S(2)}, u32[]{:S(2)}) collective-permute-start(f32[16,48,128]{2,1,0:T(8,128)S(1)} %constant_dynamic-update-slice_fusion.own), channel_id=1, source_target_pairs={{0,64},{128,192},{256,320},{384,448},{64,0},{192,128},{320,256},{4... | collective-permute-start | bytes 1179656 | tf_op jit(solution)/shard_map/ppermute | solution.py:372
  37.3 0.7 copy-start.3
  38.1 0.7 copy-start.5
  38.8 1.0 copy-start.4
  39.8 1.0 copy-start.6
  42.8 0.8 copy-start
  43.6 0.6 copy-start.7
  68.7 9.1 %collective-permute-start.4 = (f32[16,48,128]{2,1,0:T(8,128)S(1)}, f32[16,48,128]{2,1,0:T(8,128)S(1)}, u32[]{:S(2)}, u32[]{:S(2)}) collective-permute-start(f32[16,48,128]{2,1,0:T(8,128)S(1)} %get-tuple-element.27), channel_id=1, source_target_pairs={{64,128},{192,256},{320,384},{128,64},{256,192},{384,320},{65,129}... | collective-permute-start | bytes 1179656 | tf_op jit(solution)/shard_map/ppermute | solution.py:379
  70.6 7.2 %collective-permute-start.5 = (f32[16,48,128]{2,1,0:T(8,128)S(1)}, f32[16,48,128]{2,1,0:T(8,128)S(1)}, u32[]{:S(2)}, u32[]{:S(2)}) collective-permute-start(f32[16,48,128]{2,1,0:T(8,128)S(1)} %get-tuple-element.28), channel_id=1, source_target_pairs={{0,64},{128,192},{256,320},{384,448},{64,0},{192,128},{320,256},{4... | collective-permute-start | bytes 1179656 | tf_op jit(solution)/shard_map/ppermute | solution.py:380
  77.9 24.4 %collective-permute-start.6 = (f32[16,32,128]{2,1,0:T(8,128)S(1)}, f32[16,32,128]{2,1,0:T(8,128)S(1)}, u32[]{:S(2)}, u32[]{:S(2)}) collective-permute-start(f32[16,32,128]{2,1,0:T(8,128)S(1)} %get-tuple-element.40), channel_id=1, source_target_pairs={{0,1},{2,3},{4,5},{6,7},{8,9},{10,11},{12,13},{14,15},{16,17},{18,... | collective-permute-start | bytes 786440 | tf_op jit(solution)/shard_map/ppermute | solution.py:360
  80.1 31.4 %copy-start.1 = (bf16[6,384,128]{2,1,0:T(8,128)(2,1)S(1)}, bf16[6,384,128]{2,1,0:T(8,128)(2,1)}, u32[]{:S(2)}) copy-start(bf16[6,384,128]{2,1,0:T(8,128)(2,1)} %copy-done) | copy-start | bytes 1769476
  80.2 31.4 %copy-start.8 = (bf16[96,144]{1,0:T(8,128)(2,1)S(1)}, bf16[96,144]{1,0:T(8,128)(2,1)}, u32[]{:S(2)}) copy-start(bf16[96,144]{1,0:T(8,128)(2,1)} %copy-done.7) | copy-start | bytes 82948
  80.2 22.2 %collective-permute-start.8 = (f32[16,32,128]{2,1,0:T(8,128)S(1)}, f32[16,32,128]{2,1,0:T(8,128)S(1)}, u32[]{:S(2)}, u32[]{:S(2)}) collective-permute-start(f32[16,32,128]{2,1,0:T(8,128)S(1)} %get-tuple-element.41), channel_id=1, source_target_pairs={{1,2},{3,4},{5,6},{7,8},{9,10},{11,12},{13,14},{15,16},{17,18},{19... | collective-permute-start | bytes 786440 | tf_op jit(solution)/shard_map/ppermute | solution.py:360
  87.9 10.8 %collective-permute-start.7 = (f32[16,16,128]{2,1,0:T(8,128)S(1)}, f32[16,16,128]{2,1,0:T(8,128)S(1)}, u32[]{:S(2)}, u32[]{:S(2)}) collective-permute-start(f32[16,16,128]{2,1,0:T(8,128)S(1)} %get-tuple-element.38), channel_id=1, source_target_pairs={{2,0},{4,2},{6,4},{8,6},{10,8},{12,10},{14,12},{16,14},{18,16},{20... | collective-permute-start | bytes 393224 | tf_op jit(solution)/shard_map/ppermute | solution.py:367
  91.3 11.1 %collective-permute-start.9 = (f32[16,16,128]{2,1,0:T(8,128)S(1)}, f32[16,16,128]{2,1,0:T(8,128)S(1)}, u32[]{:S(2)}, u32[]{:S(2)}) collective-permute-start(f32[16,16,128]{2,1,0:T(8,128)S(1)} %get-tuple-element.39), channel_id=1, source_target_pairs={{0,2},{2,4},{4,6},{6,8},{8,10},{10,12},{12,14},{14,16},{16,18},{18... | collective-permute-start | bytes 393224 | tf_op jit(solution)/shard_map/ppermute | solution.py:367
  102.5 9.1 %collective-permute-start.11 = (f32[16,48,128]{2,1,0:T(8,128)S(1)}, f32[16,48,128]{2,1,0:T(8,128)S(1)}, u32[]{:S(2)}, u32[]{:S(2)}) collective-permute-start(f32[16,48,128]{2,1,0:T(8,128)S(1)} %fusion.e_own), channel_id=1, source_target_pairs={{64,128},{192,256},{320,384},{128,64},{256,192},{384,320},{65,129}... | collective-permute-start | bytes 1179656 | tf_op jit(solution)/shard_map/ppermute | solution.py:372
  104.4 7.2 %collective-permute-start.10 = (f32[16,48,128]{2,1,0:T(8,128)S(1)}, f32[16,48,128]{2,1,0:T(8,128)S(1)}, u32[]{:S(2)}, u32[]{:S(2)}) collective-permute-start(f32[16,48,128]{2,1,0:T(8,128)S(1)} %fusion.e_own), channel_id=1, source_target_pairs={{0,64},{128,192},{256,320},{384,448},{64,0},{192,128},{320,256},{4... | collective-permute-start | bytes 1179656 | tf_op jit(solution)/shard_map/ppermute | solution.py:372
  115.2 9.1 %collective-permute-start.12 = (f32[16,48,128]{2,1,0:T(8,128)S(1)}, f32[16,48,128]{2,1,0:T(8,128)S(1)}, u32[]{:S(2)}, u32[]{:S(2)}) collective-permute-start(f32[16,48,128]{2,1,0:T(8,128)S(1)} %get-tuple-element.31), channel_id=1, source_target_pairs={{64,128},{192,256},{320,384},{128,64},{256,192},{384,320},{65,129}... | collective-permute-start | bytes 1179656 | tf_op jit(solution)/shard_map/ppermute | solution.py:379
  117.3 6.9 %collective-permute-start.13 = (f32[16,48,128]{2,1,0:T(8,128)S(1)}, f32[16,48,128]{2,1,0:T(8,128)S(1)}, u32[]{:S(2)}, u32[]{:S(2)}) collective-permute-start(f32[16,48,128]{2,1,0:T(8,128)S(1)} %get-tuple-element.32), channel_id=1, source_target_pairs={{0,64},{128,192},{256,320},{384,448},{64,0},{192,128},{320,256},{4... | collective-permute-start | bytes 1179656 | tf_op jit(solution)/shard_map/ppermute | solution.py:380
  124.4 7.7 %collective-permute-start.14 = (f32[16,16,128]{2,1,0:T(8,128)S(1)}, f32[16,16,128]{2,1,0:T(8,128)S(1)}, u32[]{:S(2)}, u32[]{:S(2)}) collective-permute-start(f32[16,16,128]{2,1,0:T(8,128)S(1)} %get-tuple-element.36), channel_id=1, source_target_pairs={{0,1},{2,3},{4,5},{6,7},{8,9},{10,11},{12,13},{14,15},{16,17},{18,... | collective-permute-start | bytes 393224 | tf_op jit(solution)/shard_map/ppermute | solution.py:360
  126.3 10.7 %collective-permute-start.15 = (f32[16,16,128]{2,1,0:T(8,128)S(1)}, f32[16,16,128]{2,1,0:T(8,128)S(1)}, u32[]{:S(2)}, u32[]{:S(2)}) collective-permute-start(f32[16,16,128]{2,1,0:T(8,128)S(1)} %get-tuple-element.37), channel_id=1, source_target_pairs={{1,2},{3,4},{5,6},{7,8},{9,10},{11,12},{13,14},{15,16},{17,18},{19... | collective-permute-start | bytes 393224 | tf_op jit(solution)/shard_map/ppermute | solution.py:360

commit v5 on v3

--- a/solution.py
+++ b/solution.py
@@ -43,7 +43,9 @@
     return high, (value - high.astype(F32)).astype(BF16)
 
 
-def pack_kernel(named, planes, send, rows, count):
+def pack_kernel(named_in, planes, send, rows, count, named, sem):
+    copy = pltpu.make_async_copy(named_in, named, sem)
+    copy.start()
     for peer in range(PEERS):
         count[peer] = 0
     send[pl.ds(SEND * BX, PEERS, stride=CHUNK), :] = jnp.full((PEERS, NY), SLOTS, F32)
@@ -53,16 +55,17 @@
                 group * 8 : group * 8 + 8, column * NY : (column + 1) * NY
             ]
     lane = lax.broadcasted_iota(jnp.int32, (1, NY), 1)
+    copy.wait()
 
     def place(plane, carry):
-        peer = named[plane] >> 7
+        peer = named[0, plane] >> 7
         rank = count[peer]
         count[peer] = rank + 1
         start = peer * CHUNK
         send[pl.ds(start + rank * BX, BX), :] = rows[pl.ds(pl.multiple_of(plane * LINE, 8), BX), :]
         pltpu.store(
             send.at[pl.ds(start + SEND * BX, 1), :],
-            jnp.full((1, NY), named[plane] & (NY - 1), jnp.int32).astype(F32),
+            jnp.full((1, NY), named[0, plane] & (NY - 1), jnp.int32).astype(F32),
             mask=lane == rank,
         )
         return carry
@@ -74,11 +77,13 @@
     return pl.pallas_call(
         pack_kernel,
         out_shape=shape((PEERS * CHUNK, NY)),
-        in_specs=[SMEM, VMEM],
+        in_specs=[VMEM, VMEM],
         out_specs=VMEM,
         scratch_shapes=[
             pltpu.VMEM((SRC * LINE, NY), F32),
             pltpu.SMEM((PEERS,), jnp.int32),
+            pltpu.SMEM((1, NY), jnp.int32),
+            pltpu.SemaphoreType.DMA,
         ],
         compiler_params=params(16),
         name="pack_planes",
@@ -433,7 +438,8 @@
     initial_estimate,
 ):
     index = lax.axis_index("xy").astype(jnp.int32).reshape(1)
-    send = pack(plane_owner.reshape(SRC) * NY + plane_slot.reshape(SRC), tile_planes[0])
+    named = plane_owner.reshape(1, SRC) * NY + plane_slot.reshape(1, SRC)
+    send = pack(jnp.pad(named, ((0, 0), (0, NY - SRC))), tile_planes[0])
     even, odd = to_partners(initial_estimate, initial_estimate)
     send, even, odd = lax.optimization_barrier((send, even, odd))
     got = lax.all_to_all(

time: 139 us -> 138 us (level)
  no operation moved by 1% of the time
where the time goes in v5:
time: 138 us; the launch traced here: 137 us
  starting transfers between devices  70.4 us (51%)
  waiting for transfers between devices  46.4 us (34%)
  Pallas kernels  12 us (9%)
  local copies, waits for them, and re-layouts  6.28 us (5%)
  other arithmetic  1.84 us (1%)
    ppermute x3, starting transfers between devices, to_partners(): lax.ppermute(to_odd, 'xy', swaps(1, PEERS))  22.8 us
    all_to_all x1, waiting for transfers between devices, local(): lax.all_to_all(send.reshape(PEERS, 1, CHUNK * NY), 'xy', split_axis=0, co...  22.3 us
    all_to_all x1, starting transfers between devices, local(): lax.all_to_all(send.reshape(PEERS, 1, CHUNK * NY), 'xy', split_axis=0, co...  10.7 us
    ppermute x3, starting transfers between devices, to_partners(): lax.ppermute(to_even, 'xy', swaps(0, PEERS))  8.39 us
    ppermute x2, waiting for transfers between devices, slab_sum(): lax.ppermute(outside, 'gz', swaps(1, count))  7.3 us
    ppermute x2, starting transfers between devices, slab_sum(): lax.ppermute(inside, 'gz', swaps(0, count))  7.01 us
    ppermute x2, starting transfers between devices, above_and_below(): lax.ppermute(block, 'gz', swaps(0, count))  7.01 us
    unnamed x32, local copies, waits for them, and re-layouts  6.11 us
  transfers between devices with their start and end apart: 17, of which 8 were waited for; matrix products, arithmetic and copies ran while one was open for 1% of the time, Pallas kernels for 5%

profile of v5, /device:TPU:34, one launch (start us, length us, event | category | flops | bytes accessed | tf_op | source)
XLA Modules:
  0.0 137.3 jit_solution(10926458201702898997)
XLA Ops:
  0.0 4.3 %collective-permute-start = (f32[16,16,128]{2,1,0:T(8,128)}, f32[16,16,128]{2,1,0:T(8,128)S(1)}, u32[]{:S(2)}, u32[]{:S(2)}) collective-permute-start(f32[16,16,128]{2,1,0:T(8,128)} %param.17), channel_id=1, source_target_pairs={{0,1},{2,3},{4,5},{6,7},{8,9},{10,11},{12,13},{14,15},{16,17},{18,... | collective-permute-start | bytes 393224 | tf_op jit(solution)/shard_map/ppermute | solution.py:387
  4.3 9.0 %collective-permute-start.1 = (f32[16,16,128]{2,1,0:T(8,128)}, f32[16,16,128]{2,1,0:T(8,128)S(1)}, u32[]{:S(2)}, u32[]{:S(2)}) collective-permute-start(f32[16,16,128]{2,1,0:T(8,128)} %param.17), channel_id=1, source_target_pairs={{1,2},{3,4},{5,6},{7,8},{9,10},{11,12},{13,14},{15,16},{17,18},{19... | collective-permute-start | bytes 393224 | tf_op jit(solution)/shard_map/ppermute | solution.py:387
  13.3 0.7 bitcast_add_fusion
  14.0 1.1 copy-done.2
  15.1 2.2 %pack_planes.1 = f32[3136,128]{1,0:T(8,128)} custom-call(s32[1,128]{1,0:T(1,128)S(1)} %pad.4.named_in, f32[96,2048]{1,0:T(8,128)S(1)} %bitcast.8), custom_call_target="tpu_custom_call" | custom-call | tf_op jit(solution)/shard_map/pack_planes/pallas_call | solution.py:77
  17.4 0.0 collective-permute-done
  17.4 0.0 collective-permute-done.1
  17.4 0.0 copy-start.10
  17.4 0.0 copy-start.11
  17.4 0.0 copy-start.12
  17.4 0.0 copy-start.13
  17.4 0.0 copy-start.9
  17.4 0.0 copy-start.14
  17.4 10.7 %all-to-all-start = ((f32[64,1,6272]{2,1,0:T(1,128)}), f32[64,1,6272]{2,1,0:T(1,128)S(1)}, u32[]{:S(2)}, u32[]{:S(2)}) async-start(f32[64,1,6272]{2,1,0:T(1,128)} %bitcast.3), calls=%async_computation | async-start | bytes 3211264 | tf_op jit(solution)/shard_map/all_to_all | solution.py:445
  28.2 0.0 copy-done.10
  28.2 1.9 %collective-permute-start.3 = (f32[16,48,128]{2,1,0:T(8,128)S(1)}, f32[16,48,128]{2,1,0:T(8,128)S(1)}, u32[]{:S(2)}, u32[]{:S(2)}) collective-permute-start(f32[16,48,128]{2,1,0:T(8,128)S(1)} %constant_dynamic-update-slice_fusion.own), channel_id=1, source_target_pairs={{64,128},{192,256},{320,384},{128,64},{256,192},{384,320},{65,129}... | collective-permute-start | bytes 1179656 | tf_op jit(solution)/shard_map/ppermute | solution.py:399
  30.2 3.5 %collective-permute-start.2 = (f32[16,48,128]{2,1,0:T(8,128)S(1)}, f32[16,48,128]{2,1,0:T(8,128)S(1)}, u32[]{:S(2)}, u32[]{:S(2)}) collective-permute-start(f32[16,48,128]{2,1,0:T(8,128)S(1)} %constant_dynamic-update-slice_fusion.own), channel_id=1, source_target_pairs={{0,64},{128,192},{256,320},{384,448},{64,0},{192,128},{320,256},{4... | collective-permute-start | bytes 1179656 | tf_op jit(solution)/shard_map/ppermute | solution.py:399
  33.7 0.1 fusion.7
  33.8 0.1 fusion.6.taps
  33.9 2.6 %operator_matrices.1 = (bf16[6,32,96]{2,1,0:T(8,128)(2,1)S(1)}, bf16[96,144]{1,0:T(8,128)(2,1)S(1)}, bf16[6,384,128]{2,1,0:T(8,128)(2,1)S(1)}, bf16[2688,128]{1,0:T(8,128)(2,1)S(1)}) custom-call(s32[1]{0:T(128)} %bitcast.2.index, f32[18,33]{1,0:T(8,128)S(1)} %fusion.6.taps, s32[6]{0:T(128)S(1)} %copy-done.9), custom_call_target="tpu_custom_call" | custom-call | tf_op jit(solution)/shard_map/operator_matrices/pallas_call | solution.py:158
  36.5 0.9 collective-permute-done.3.outside
  37.3 0.7 copy-done.3
  38.1 0.0 collective-permute-done.2.inside
  38.1 0.7 copy-done.5
  38.8 0.1 broadcast_in_dim.2.background
  38.9 1.0 copy-done.4
  39.9 1.0 copy-done.6
  40.9 1.4 %forward.1.blur = f32[1536,128]{1,0:T(8,128)S(1)} custom-call(f32[6,128]{1,0:T(8,128)S(1)} %broadcast_in_dim.2.background, bf16[6,32,96]{2,1,0:T(8,128)(2,1)S(1)} %get-tuple-element.22.z_fwd, bf16[96,144]{1,0:T(8,128)(2,1)S(1)} %get-tuple-element.23.x_fwd, bf16[6,384,128]{2,1,0:T(8,128)(2,1)S(1)} %get-tuple-element.24.y_fwd, ...), custom_call_target="tpu_custom_call" | custom-call | tf_op jit(solution)/shard_map/forward/pallas_call | solution.py:252
  42.3 0.8 copy-done
  43.1 0.6 copy-done.7
  43.7 22.3 %all-to-all-done = f32[64,1,6272]{2,1,0:T(1,128)S(1)} async-done(((f32[64,1,6272]{2,1,0:T(1,128)}), f32[64,1,6272]{2,1,0:T(1,128)S(1)}, u32[]{:S(2)}, u32[]{:S(2)}) %all-to-all-start) | async-done | bytes 1605664 | tf_op jit(solution)/shard_map/all_to_all | solution.py:445
  66.1 2.3 %first_back.1 = (f32[16,48,128]{2,1,0:T(8,128)S(1)}, f32[16,48,128]{2,1,0:T(8,128)S(1)}, f32[16,48,128]{2,1,0:T(8,128)S(1)}) custom-call(bf16[2688,128]{1,0:T(8,128)(2,1)S(1)} %get-tuple-element.20.back, f32[3136,128]{1,0:T(8,128)S(1)} %bitcast.6, f32[1536,128]{1,0:T(8,128)S(1)} %forward.1.blur), custom_call_target="tpu_custom_call" | custom-call | tf_op jit(solution)/shard_map/first_back/pallas_call | solution.py:344
  68.4 1.9 %collective-permute-start.4 = (f32[16,48,128]{2,1,0:T(8,128)S(1)}, f32[16,48,128]{2,1,0:T(8,128)S(1)}, u32[]{:S(2)}, u32[]{:S(2)}) collective-permute-start(f32[16,48,128]{2,1,0:T(8,128)S(1)} %get-tuple-element.26), channel_id=1, source_target_pairs={{64,128},{192,256},{320,384},{128,64},{256,192},{384,320},{65,129}... | collective-permute-start | bytes 1179656 | tf_op jit(solution)/shard_map/ppermute | solution.py:406
  70.3 3.5 %collective-permute-start.5 = (f32[16,48,128]{2,1,0:T(8,128)S(1)}, f32[16,48,128]{2,1,0:T(8,128)S(1)}, u32[]{:S(2)}, u32[]{:S(2)}) collective-permute-start(f32[16,48,128]{2,1,0:T(8,128)S(1)} %get-tuple-element.27), channel_id=1, source_target_pairs={{0,64},{128,192},{256,320},{384,448},{64,0},{192,128},{320,256},{4... | collective-permute-start | bytes 1179656 | tf_op jit(solution)/shard_map/ppermute | solution.py:407
  73.8 3.7 %collective-permute-done.4 = f32[16,48,128]{2,1,0:T(8,128)S(1)} collective-permute-done((f32[16,48,128]{2,1,0:T(8,128)S(1)}, f32[16,48,128]{2,1,0:T(8,128)S(1)}, u32[]{:S(2)}, u32[]{:S(2)}) %collective-permute-start.4) | collective-permute-done | bytes 393248 | tf_op jit(solution)/shard_map/ppermute | solution.py:406
  77.4 0.0 collective-permute-done.5
  77.5 0.1 add_add_fusion.1
  77.6 2.2 %collective-permute-start.6 = (f32[16,32,128]{2,1,0:T(8,128)S(1)}, f32[16,32,128]{2,1,0:T(8,128)S(1)}, u32[]{:S(2)}, u32[]{:S(2)}) collective-permute-start(f32[16,32,128]{2,1,0:T(8,128)S(1)} %get-tuple-element.38), channel_id=1, source_target_pairs={{0,1},{2,3},{4,5},{6,7},{8,9},{10,11},{12,13},{14,15},{16,17},{18,... | collective-permute-start | bytes 786440 | tf_op jit(solution)/shard_map/ppermute | solution.py:387
  79.8 0.0 copy-start.8
  79.8 7.7 %collective-permute-start.8 = (f32[16,32,128]{2,1,0:T(8,128)S(1)}, f32[16,32,128]{2,1,0:T(8,128)S(1)}, u32[]{:S(2)}, u32[]{:S(2)}) collective-permute-start(f32[16,32,128]{2,1,0:T(8,128)S(1)} %get-tuple-element.39), channel_id=1, source_target_pairs={{1,2},{3,4},{5,6},{7,8},{9,10},{11,12},{13,14},{15,16},{17,18},{19... | collective-permute-start | bytes 786440 | tf_op jit(solution)/shard_map/ppermute | solution.py:387
  87.5 3.4 %collective-permute-start.7 = (f32[16,16,128]{2,1,0:T(8,128)S(1)}, f32[16,16,128]{2,1,0:T(8,128)S(1)}, u32[]{:S(2)}, u32[]{:S(2)}) collective-permute-start(f32[16,16,128]{2,1,0:T(8,128)S(1)} %get-tuple-element.36), channel_id=1, source_target_pairs={{2,0},{4,2},{6,4},{8,6},{10,8},{12,10},{14,12},{16,14},{18,16},{20... | collective-permute-start | bytes 393224 | tf_op jit(solution)/shard_map/ppermute | solution.py:394
  90.9 3.4 %collective-permute-start.9 = (f32[16,16,128]{2,1,0:T(8,128)S(1)}, f32[16,16,128]{2,1,0:T(8,128)S(1)}, u32[]{:S(2)}, u32[]{:S(2)}) collective-permute-start(f32[16,16,128]{2,1,0:T(8,128)S(1)} %get-tuple-element.37), channel_id=1, source_target_pairs={{0,2},{2,4},{4,6},{6,8},{8,10},{10,12},{12,14},{14,16},{16,18},{18... | collective-permute-start | bytes 393224 | tf_op jit(solution)/shard_map/ppermute | solution.py:394
  94.2 4.3 %collective-permute-done.7 = f32[16,16,128]{2,1,0:T(8,128)S(1)} collective-permute-done((f32[16,16,128]{2,1,0:T(8,128)S(1)}, f32[16,16,128]{2,1,0:T(8,128)S(1)}, u32[]{:S(2)}, u32[]{:S(2)}) %collective-permute-start.7) | collective-permute-done | bytes 131104 | tf_op jit(solution)/shard_map/ppermute | solution.py:394
  98.6 3.4 %collective-permute-done.9 = f32[16,16,128]{2,1,0:T(8,128)S(1)} collective-permute-done((f32[16,16,128]{2,1,0:T(8,128)S(1)}, f32[16,16,128]{2,1,0:T(8,128)S(1)}, u32[]{:S(2)}, u32[]{:S(2)}) %collective-permute-start.9) | collective-permute-done | bytes 131104 | tf_op jit(solution)/shard_map/ppermute | solution.py:394
  101.9 0.0 collective-permute-done.6
  101.9 0.0 collective-permute-done.8
  101.9 0.1 fusion.5
  102.0 0.1 fusion.e_own
  102.1 1.9 %collective-permute-start.11 = (f32[16,48,128]{2,1,0:T(8,128)S(1)}, f32[16,48,128]{2,1,0:T(8,128)S(1)}, u32[]{:S(2)}, u32[]{:S(2)}) collective-permute-start(f32[16,48,128]{2,1,0:T(8,128)S(1)} %fusion.e_own), channel_id=1, source_target_pairs={{64,128},{192,256},{320,384},{128,64},{256,192},{384,320},{65,129}... | collective-permute-start | bytes 1179656 | tf_op jit(solution)/shard_map/ppermute | solution.py:399
  104.0 3.5 %collective-permute-start.10 = (f32[16,48,128]{2,1,0:T(8,128)S(1)}, f32[16,48,128]{2,1,0:T(8,128)S(1)}, u32[]{:S(2)}, u32[]{:S(2)}) collective-permute-start(f32[16,48,128]{2,1,0:T(8,128)S(1)} %fusion.e_own), channel_id=1, source_target_pairs={{0,64},{128,192},{256,320},{384,448},{64,0},{192,128},{320,256},{4... | collective-permute-start | bytes 1179656 | tf_op jit(solution)/shard_map/ppermute | solution.py:399
  107.5 3.7 %collective-permute-done.11.e_outside = f32[16,48,128]{2,1,0:T(8,128)S(1)} collective-permute-done((f32[16,48,128]{2,1,0:T(8,128)S(1)}, f32[16,48,128]{2,1,0:T(8,128)S(1)}, u32[]{:S(2)}, u32[]{:S(2)}) %collective-permute-start.11) | collective-permute-done | bytes 393248 | tf_op jit(solution)/shard_map/ppermute | solution.py:399
  111.2 0.0 collective-permute-done.10.e_inside
  111.2 0.0 copy-done.1
  111.2 3.5 %forward_and_back.1 = (f32[16,48,128]{2,1,0:T(8,128)S(1)}, f32[16,48,128]{2,1,0:T(8,128)S(1)}, f32[16,48,128]{2,1,0:T(8,128)S(1)}) custom-call(f32[6,128]{1,0:T(8,128)S(1)} %broadcast_in_dim.2.background, bf16[6,32,96]{2,1,0:T(8,128)(2,1)S(1)} %get-tuple-element.22.z_fwd, bf16[96,144]{1,0:T(8,128)(2,1)S(1)} %copy-done.8, bf16[6,384,128]{2,1,0:T(8,128)(2,1)S(1)} %copy-done.1, ...), custom_call_target="tpu_custom_call" | custom-call | tf_op jit(solution)/shard_map/forward_and_back/pallas_call | solution.py:370
  114.7 1.9 %collective-permute-start.12 = (f32[16,48,128]{2,1,0:T(8,128)S(1)}, f32[16,48,128]{2,1,0:T(8,128)S(1)}, u32[]{:S(2)}, u32[]{:S(2)}) collective-permute-start(f32[16,48,128]{2,1,0:T(8,128)S(1)} %get-tuple-element.29), channel_id=1, source_target_pairs={{64,128},{192,256},{320,384},{128,64},{256,192},{384,320},{65,129}... | collective-permute-start | bytes 1179656 | tf_op jit(solution)/shard_map/ppermute | solution.py:406
  116.7 3.5 %collective-permute-start.13 = (f32[16,48,128]{2,1,0:T(8,128)S(1)}, f32[16,48,128]{2,1,0:T(8,128)S(1)}, u32[]{:S(2)}, u32[]{:S(2)}) collective-permute-start(f32[16,48,128]{2,1,0:T(8,128)S(1)} %get-tuple-element.30), channel_id=1, source_target_pairs={{0,64},{128,192},{256,320},{384,448},{64,0},{192,128},{320,256},{4... | collective-permute-start | bytes 1179656 | tf_op jit(solution)/shard_map/ppermute | solution.py:407
  120.2 3.6 %collective-permute-done.12 = f32[16,48,128]{2,1,0:T(8,128)S(1)} collective-permute-done((f32[16,48,128]{2,1,0:T(8,128)S(1)}, f32[16,48,128]{2,1,0:T(8,128)S(1)}, u32[]{:S(2)}, u32[]{:S(2)}) %collective-permute-start.12) | collective-permute-done | bytes 393248 | tf_op jit(solution)/shard_map/ppermute | solution.py:406
  123.8 0.0 collective-permute-done.13
  123.8 0.1 add_add_fusion
  123.9 1.9 %collective-permute-start.14 = (f32[16,16,128]{2,1,0:T(8,128)S(1)}, f32[16,16,128]{2,1,0:T(8,128)S(1)}, u32[]{:S(2)}, u32[]{:S(2)}) collective-permute-start(f32[16,16,128]{2,1,0:T(8,128)S(1)} %get-tuple-element.34), channel_id=1, source_target_pairs={{0,1},{2,3},{4,5},{6,7},{8,9},{10,11},{12,13},{14,15},{16,17},{18,... | collective-permute-start | bytes 393224 | tf_op jit(solution)/shard_map/ppermute | solution.py:387
  125.9 6.2 %collective-permute-start.15 = (f32[16,16,128]{2,1,0:T(8,128)S(1)}, f32[16,16,128]{2,1,0:T(8,128)S(1)}, u32[]{:S(2)}, u32[]{:S(2)}) collective-permute-start(f32[16,16,128]{2,1,0:T(8,128)S(1)} %get-tuple-element.35), channel_id=1, source_target_pairs={{1,2},{3,4},{5,6},{7,8},{9,10},{11,12},{13,14},{15,16},{17,18},{19... | collective-permute-start | bytes 393224 | tf_op jit(solution)/shard_map/ppermute | solution.py:387
  132.0 0.0 collective-permute-done.14
  132.0 4.6 %collective-permute-done.15 = f32[16,16,128]{2,1,0:T(8,128)S(1)} collective-permute-done((f32[16,16,128]{2,1,0:T(8,128)S(1)}, f32[16,16,128]{2,1,0:T(8,128)S(1)}, u32[]{:S(2)}, u32[]{:S(2)}) %collective-permute-start.15) | collective-permute-done | bytes 131104 | tf_op jit(solution)/shard_map/ppermute | solution.py:387
  136.6 0.7 fusion.3
  (21 shorter events, 0.1 us)
Async XLA Ops:
  0.0 17.4 %collective-permute-start = (f32[16,16,128]{2,1,0:T(8,128)}, f32[16,16,128]{2,1,0:T(8,128)S(1)}, u32[]{:S(2)}, u32[]{:S(2)}) collective-permute-start(f32[16,16,128]{2,1,0:T(8,128)} %param.17), channel_id=1, source_target_pairs={{0,1},{2,3},{4,5},{6,7},{8,9},{10,11},{12,13},{14,15},{16,17},{18,... | collective-permute-start | bytes 393224 | tf_op jit(solution)/shard_map/ppermute | solution.py:387
  4.3 13.1 %collective-permute-start.1 = (f32[16,16,128]{2,1,0:T(8,128)}, f32[16,16,128]{2,1,0:T(8,128)S(1)}, u32[]{:S(2)}, u32[]{:S(2)}) collective-permute-start(f32[16,16,128]{2,1,0:T(8,128)} %param.17), channel_id=1, source_target_pairs={{1,2},{3,4},{5,6},{7,8},{9,10},{11,12},{13,14},{15,16},{17,18},{19... | collective-permute-start | bytes 393224 | tf_op jit(solution)/shard_map/ppermute | solution.py:387
  14.0 1.1 copy-start.2
  17.4 10.8 %copy-start.10 = (f32[16,16,128]{2,1,0:T(8,128)S(1)}, f32[16,16,128]{2,1,0:T(8,128)}, u32[]{:S(2)}) copy-start(f32[16,16,128]{2,1,0:T(8,128)} %param.17) | copy-start | bytes 393220
  17.4 16.3 %copy-start.11 = (f32[6,33]{1,0:T(8,128)S(1)}, f32[6,33]{1,0:T(8,128)}, u32[]{:S(2)}) copy-start(f32[6,33]{1,0:T(8,128)} %param.15) | copy-start | bytes 2380
  17.4 16.3 %copy-start.12 = (f32[6,33]{1,0:T(8,128)S(1)}, f32[6,33]{1,0:T(8,128)}, u32[]{:S(2)}) copy-start(f32[6,33]{1,0:T(8,128)} %param.14) | copy-start | bytes 2380
  17.4 16.3 %copy-start.13 = (f32[6,33]{1,0:T(8,128)S(1)}, f32[6,33]{1,0:T(8,128)}, u32[]{:S(2)}) copy-start(f32[6,33]{1,0:T(8,128)} %param.13) | copy-start | bytes 2380
  17.4 16.5 %copy-start.9 = (s32[6]{0:T(128)S(1)}, s32[6]{0:T(128)}, u32[]{:S(2)}) copy-start(s32[6]{0:T(128)} %shift.1) | copy-start | bytes 76
  17.4 21.4 %copy-start.14 = (f32[6]{0:T(128)S(1)}, f32[6]{0:T(128)}, u32[]{:S(2)}) copy-start(f32[6]{0:T(128)} %param.16) | copy-start | bytes 76
  17.4 48.6 %all-to-all-start = ((f32[64,1,6272]{2,1,0:T(1,128)}), f32[64,1,6272]{2,1,0:T(1,128)S(1)}, u32[]{:S(2)}, u32[]{:S(2)}) async-start(f32[64,1,6272]{2,1,0:T(1,128)} %bitcast.3), calls=%async_computation | async-start | bytes 3211264 | tf_op jit(solution)/shard_map/all_to_all | solution.py:445
  28.2 9.1 %collective-permute-start.3 = (f32[16,48,128]{2,1,0:T(8,128)S(1)}, f32[16,48,128]{2,1,0:T(8,128)S(1)}, u32[]{:S(2)}, u32[]{:S(2)}) collective-permute-start(f32[16,48,128]{2,1,0:T(8,128)S(1)} %constant_dynamic-update-slice_fusion.own), channel_id=1, source_target_pairs={{64,128},{192,256},{320,384},{128,64},{256,192},{384,320},{65,129}... | collective-permute-start | bytes 1179656 | tf_op jit(solution)/shard_map/ppermute | solution.py:399
  30.2 7.9 %collective-permute-start.2 = (f32[16,48,128]{2,1,0:T(8,128)S(1)}, f32[16,48,128]{2,1,0:T(8,128)S(1)}, u32[]{:S(2)}, u32[]{:S(2)}) collective-permute-start(f32[16,48,128]{2,1,0:T(8,128)S(1)} %constant_dynamic-update-slice_fusion.own), channel_id=1, source_target_pairs={{0,64},{128,192},{256,320},{384,448},{64,0},{192,128},{320,256},{4... | collective-permute-start | bytes 1179656 | tf_op jit(solution)/shard_map/ppermute | solution.py:399
  37.3 0.7 copy-start.3
  38.1 0.7 copy-start.5
  38.9 1.0 copy-start.4
  39.9 1.0 copy-start.6
  42.3 0.8 copy-start
  43.1 0.6 copy-start.7
  68.4 9.1 %collective-permute-start.4 = (f32[16,48,128]{2,1,0:T(8,128)S(1)}, f32[16,48,128]{2,1,0:T(8,128)S(1)}, u32[]{:S(2)}, u32[]{:S(2)}) collective-permute-start(f32[16,48,128]{2,1,0:T(8,128)S(1)} %get-tuple-element.26), channel_id=1, source_target_pairs={{64,128},{192,256},{320,384},{128,64},{256,192},{384,320},{65,129}... | collective-permute-start | bytes 1179656 | tf_op jit(solution)/shard_map/ppermute | solution.py:406
  70.3 7.2 %collective-permute-start.5 = (f32[16,48,128]{2,1,0:T(8,128)S(1)}, f32[16,48,128]{2,1,0:T(8,128)S(1)}, u32[]{:S(2)}, u32[]{:S(2)}) collective-permute-start(f32[16,48,128]{2,1,0:T(8,128)S(1)} %get-tuple-element.27), channel_id=1, source_target_pairs={{0,64},{128,192},{256,320},{384,448},{64,0},{192,128},{320,256},{4... | collective-permute-start | bytes 1179656 | tf_op jit(solution)/shard_map/ppermute | solution.py:407
  77.6 24.4 %collective-permute-start.6 = (f32[16,32,128]{2,1,0:T(8,128)S(1)}, f32[16,32,128]{2,1,0:T(8,128)S(1)}, u32[]{:S(2)}, u32[]{:S(2)}) collective-permute-start(f32[16,32,128]{2,1,0:T(8,128)S(1)} %get-tuple-element.38), channel_id=1, source_target_pairs={{0,1},{2,3},{4,5},{6,7},{8,9},{10,11},{12,13},{14,15},{16,17},{18,... | collective-permute-start | bytes 786440 | tf_op jit(solution)/shard_map/ppermute | solution.py:387
  79.8 31.4 %copy-start.1 = (bf16[6,384,128]{2,1,0:T(8,128)(2,1)S(1)}, bf16[6,384,128]{2,1,0:T(8,128)(2,1)}, u32[]{:S(2)}) copy-start(bf16[6,384,128]{2,1,0:T(8,128)(2,1)} %copy-done) | copy-start | bytes 1769476
  79.8 31.4 %copy-start.8 = (bf16[96,144]{1,0:T(8,128)(2,1)S(1)}, bf16[96,144]{1,0:T(8,128)(2,1)}, u32[]{:S(2)}) copy-start(bf16[96,144]{1,0:T(8,128)(2,1)} %copy-done.7) | copy-start | bytes 82948
  79.8 22.2 %collective-permute-start.8 = (f32[16,32,128]{2,1,0:T(8,128)S(1)}, f32[16,32,128]{2,1,0:T(8,128)S(1)}, u32[]{:S(2)}, u32[]{:S(2)}) collective-permute-start(f32[16,32,128]{2,1,0:T(8,128)S(1)} %get-tuple-element.39), channel_id=1, source_target_pairs={{1,2},{3,4},{5,6},{7,8},{9,10},{11,12},{13,14},{15,16},{17,18},{19... | collective-permute-start | bytes 786440 | tf_op jit(solution)/shard_map/ppermute | solution.py:387
  87.5 11.1 %collective-permute-start.7 = (f32[16,16,128]{2,1,0:T(8,128)S(1)}, f32[16,16,128]{2,1,0:T(8,128)S(1)}, u32[]{:S(2)}, u32[]{:S(2)}) collective-permute-start(f32[16,16,128]{2,1,0:T(8,128)S(1)} %get-tuple-element.36), channel_id=1, source_target_pairs={{2,0},{4,2},{6,4},{8,6},{10,8},{12,10},{14,12},{16,14},{18,16},{20... | collective-permute-start | bytes 393224 | tf_op jit(solution)/shard_map/ppermute | solution.py:394
  90.9 11.1 %collective-permute-start.9 = (f32[16,16,128]{2,1,0:T(8,128)S(1)}, f32[16,16,128]{2,1,0:T(8,128)S(1)}, u32[]{:S(2)}, u32[]{:S(2)}) collective-permute-start(f32[16,16,128]{2,1,0:T(8,128)S(1)} %get-tuple-element.37), channel_id=1, source_target_pairs={{0,2},{2,4},{4,6},{6,8},{8,10},{10,12},{12,14},{14,16},{16,18},{18... | collective-permute-start | bytes 393224 | tf_op jit(solution)/shard_map/ppermute | solution.py:394
  102.1 9.1 %collective-permute-start.11 = (f32[16,48,128]{2,1,0:T(8,128)S(1)}, f32[16,48,128]{2,1,0:T(8,128)S(1)}, u32[]{:S(2)}, u32[]{:S(2)}) collective-permute-start(f32[16,48,128]{2,1,0:T(8,128)S(1)} %fusion.e_own), channel_id=1, source_target_pairs={{64,128},{192,256},{320,384},{128,64},{256,192},{384,320},{65,129}... | collective-permute-start | bytes 1179656 | tf_op jit(solution)/shard_map/ppermute | solution.py:399
  104.0 7.2 %collective-permute-start.10 = (f32[16,48,128]{2,1,0:T(8,128)S(1)}, f32[16,48,128]{2,1,0:T(8,128)S(1)}, u32[]{:S(2)}, u32[]{:S(2)}) collective-permute-start(f32[16,48,128]{2,1,0:T(8,128)S(1)} %fusion.e_own), channel_id=1, source_target_pairs={{0,64},{128,192},{256,320},{384,448},{64,0},{192,128},{320,256},{4... | collective-permute-start | bytes 1179656 | tf_op jit(solution)/shard_map/ppermute | solution.py:399
  114.7 9.1 %collective-permute-start.12 = (f32[16,48,128]{2,1,0:T(8,128)S(1)}, f32[16,48,128]{2,1,0:T(8,128)S(1)}, u32[]{:S(2)}, u32[]{:S(2)}) collective-permute-start(f32[16,48,128]{2,1,0:T(8,128)S(1)} %get-tuple-element.29), channel_id=1, source_target_pairs={{64,128},{192,256},{320,384},{128,64},{256,192},{384,320},{65,129}... | collective-permute-start | bytes 1179656 | tf_op jit(solution)/shard_map/ppermute | solution.py:406
  116.7 7.2 %collective-permute-start.13 = (f32[16,48,128]{2,1,0:T(8,128)S(1)}, f32[16,48,128]{2,1,0:T(8,128)S(1)}, u32[]{:S(2)}, u32[]{:S(2)}) collective-permute-start(f32[16,48,128]{2,1,0:T(8,128)S(1)} %get-tuple-element.30), channel_id=1, source_target_pairs={{0,64},{128,192},{256,320},{384,448},{64,0},{192,128},{320,256},{4... | collective-permute-start | bytes 1179656 | tf_op jit(solution)/shard_map/ppermute | solution.py:407
  123.9 8.1 %collective-permute-start.14 = (f32[16,16,128]{2,1,0:T(8,128)S(1)}, f32[16,16,128]{2,1,0:T(8,128)S(1)}, u32[]{:S(2)}, u32[]{:S(2)}) collective-permute-start(f32[16,16,128]{2,1,0:T(8,128)S(1)} %get-tuple-element.34), channel_id=1, source_target_pairs={{0,1},{2,3},{4,5},{6,7},{8,9},{10,11},{12,13},{14,15},{16,17},{18,... | collective-permute-start | bytes 393224 | tf_op jit(solution)/shard_map/ppermute | solution.py:387
  125.9 10.8 %collective-permute-start.15 = (f32[16,16,128]{2,1,0:T(8,128)S(1)}, f32[16,16,128]{2,1,0:T(8,128)S(1)}, u32[]{:S(2)}, u32[]{:S(2)}) collective-permute-start(f32[16,16,128]{2,1,0:T(8,128)S(1)} %get-tuple-element.35), channel_id=1, source_target_pairs={{1,2},{3,4},{5,6},{7,8},{9,10},{11,12},{13,14},{15,16},{17,18},{19... | collective-permute-start | bytes 393224 | tf_op jit(solution)/shard_map/ppermute | solution.py:387
